TPU v7x, 32 devices: a whole 2x2x4 slice. The times are simulated.
32 devices in a mesh: chan: 8 (over y, x, core), facet: 4 (over z).
Axes of the slice: x: 2, y: 2, z: 4, core: 2. Of those that a mesh axis runs over, the one named last changes fastest.
Arguments:
- start_image: float32 [64, 8192], P(None, 'facet'), may hold values from 0 to 3
- visibilities: bfloat16 [32, 16, 4, 256], P(('chan', 'facet')), may hold values from -12 to 12
- strip_index: int32 [32, 16, 4, 2], P(('chan', 'facet')), may hold values from 0 to 4095
- live_counts: int32 [32, 16, 4], P(('chan', 'facet')), may hold values from 0 to 128
- uv_kernels: bfloat16 [16, 4, 256, 256], P('chan', 'facet'), may hold values from -0.375 to 0.375
Outputs:
- final_image: float32 [64, 8192], P(None, 'facet')
Inputs may be any that keep to these rules, and one draw needn't show every extreme that they name: `strip_index`: each visibility block reads 2 image strips. The first live_counts of a block's 128 visibilities are live, the others are flagged.
All inputs are finite; a program needn't handle non-finite values.
Results may differ from a plain program's by a relative error of at most 0.0026.
Values may be sent and summed in bfloat16 or wider, within the bound.
No kernel may reach another device: no remote copies, remote signals or barrier semaphores. Data moves between devices by JAX's collectives and lax.ppermute only.
A program may use at most 64 MiB of HBM per device.

v0:
```python
import jax
import jax.numpy as jnp
from jax import lax
from jax.sharding import PartitionSpec as P

STRIP = 128
VISB = 128
TERMS = 2
ITERS = 2


shrinkage = 0.05


def on_device(start_image, visibilities, strip_index, live_counts, uv_kernels):
    observed, picked_ids, live_now = (
        lax.all_to_all(
            lax.all_to_all(visibilities, "chan", split_axis=1, concat_axis=0, tiled=True),
            "facet",
            split_axis=2,
            concat_axis=0,
            tiled=True,
        ),
        lax.all_to_all(
            lax.all_to_all(strip_index, "chan", split_axis=1, concat_axis=0, tiled=True),
            "facet",
            split_axis=2,
            concat_axis=0,
            tiled=True,
        ),
        lax.all_to_all(
            lax.all_to_all(live_counts, "chan", split_axis=1, concat_axis=0, tiled=True),
            "facet",
            split_axis=2,
            concat_axis=0,
            tiled=True,
        ),
    )
    chan_count = lax.axis_size("chan")
    facet_count = lax.axis_size("facet")
    slot_count = observed.shape[0]
    chan_local = uv_kernels.shape[0]
    uv_local = uv_kernels.shape[1]
    all_channels = chan_local * chan_count
    all_uvtiles = uv_local * facet_count
    slab_rows = start_image.shape[0]
    facet_width = start_image.shape[1]
    full_width = facet_width * facet_count
    strip_count = slab_rows * full_width // STRIP
    step_size = strip_count / (2.5 * slot_count * all_channels * all_uvtiles)
    lane_ids = jnp.arange(2 * VISB, dtype=jnp.int32) % VISB
    live_mask = lane_ids < live_now[..., None]
    flat_ids = picked_ids.reshape(-1)
    estimate = start_image
    for iteration in range(ITERS):
        full_sky = lax.all_gather(estimate.astype(jnp.bfloat16), "facet", axis=1, tiled=True)
        sky_strips = full_sky.reshape(strip_count, STRIP)
        gathered = sky_strips[picked_ids].reshape(slot_count, chan_local, uv_local, TERMS * STRIP)
        predicted = jnp.einsum(
            "scup,cupq->scuq", gathered, uv_kernels, preferred_element_type=jnp.float32
        )
        residual = jnp.where(live_mask, predicted - observed.astype(jnp.float32), 0.0).astype(
            jnp.bfloat16
        )
        adjoint = jnp.einsum(
            "scuq,cupq->scup", residual, uv_kernels, preferred_element_type=jnp.float32
        )
        gradient = (
            jnp.zeros((strip_count, STRIP), jnp.float32)
            .at[flat_ids]
            .add(adjoint.reshape(-1, STRIP))
        )
        gradient = gradient.reshape(slab_rows, full_width)
        facet_part = lax.psum_scatter(gradient, "facet", scatter_dimension=1, tiled=True)
        facet_sum = lax.psum(facet_part, "chan")
        descent = estimate - step_size * facet_sum
        estimate = jnp.maximum(descent - shrinkage, 0.0)
    return estimate


def solution(mesh):
    placed = (
        P(None, "facet"),
        P(("chan", "facet"), None, None, None),
        P(("chan", "facet"), None, None, None),
        P(("chan", "facet"), None, None),
        P("chan", "facet", None, None),
    )
    return jax.shard_map(
        on_device, mesh=mesh, in_specs=placed, out_specs=P(None, "facet"), check_vma=False
    )
```

profile of v0, /device:TPU:0, one launch (start us, length us, event | category | flops | bytes accessed | tf_op | source)
XLA Modules:
  0.0 310.4 jit_solution(9693166102808401158)
XLA Ops:
  6.5 1.8 convert_element_type.33
  9.7 5.2 %all-to-all-start.2 = ((s32[1,16,4]{2,0,1:T(1,128)}), s32[1,16,4]{2,0,1:T(1,128)S(1)}, u32[]{:S(2)}, u32[]{:S(2)}) async-start(s32[1,16,4]{2,0,1:T(1,128)} %copy.47), calls=%async_computation.2 | async-start | bytes 16384 | tf_op jit(solution)/shard_map/all_to_all | solution.py:32
  16.3 3.3 %all-to-all-done.2 = s32[1,16,4]{2,0,1:T(1,128)S(1)} async-done(((s32[1,16,4]{2,0,1:T(1,128)}), s32[1,16,4]{2,0,1:T(1,128)S(1)}, u32[]{:S(2)}, u32[]{:S(2)}) %all-to-all-start.2) | async-done | bytes 288 | tf_op jit(solution)/shard_map/all_to_all | solution.py:32
  19.6 3.3 %all-to-all-start = ((s32[1,16,4,2]{2,3,0,1:T(2,128)}), s32[1,16,4,2]{2,3,0,1:T(2,128)S(1)}, u32[]{:S(2)}, u32[]{:S(2)}) async-start(s32[1,16,4,2]{2,3,0,1:T(2,128)} %copy.42), calls=%async_computation | async-start | bytes 32768 | tf_op jit(solution)/shard_map/all_to_all | solution.py:25
  23.6 4.0 %all-to-all-done = s32[1,16,4,2]{2,3,0,1:T(2,128)S(1)} async-done(((s32[1,16,4,2]{2,3,0,1:T(2,128)}), s32[1,16,4,2]{2,3,0,1:T(2,128)S(1)}, u32[]{:S(2)}, u32[]{:S(2)}) %all-to-all-start) | async-done | bytes 544 | tf_op jit(solution)/shard_map/all_to_all | solution.py:25
  27.6 4.9 %all-to-all-start.3 = ((s32[8,2,4]{0,1,2:T(2,128)}), s32[8,2,4]{0,1,2:T(2,128)S(1)}, u32[]{:S(2)}, u32[]{:S(2)}) async-start(s32[8,2,4]{0,1,2:T(2,128)} %copy.48), calls=%async_computation.3 | async-start | bytes 8192 | tf_op jit(solution)/shard_map/all_to_all | solution.py:31
  33.2 4.9 %all-to-all-done.3 = s32[8,2,4]{0,1,2:T(2,128)S(1)} async-done(((s32[8,2,4]{0,1,2:T(2,128)}), s32[8,2,4]{0,1,2:T(2,128)S(1)}, u32[]{:S(2)}, u32[]{:S(2)}) %all-to-all-start.3) | async-done | bytes 288 | tf_op jit(solution)/shard_map/all_to_all | solution.py:31
  38.1 3.2 %all-to-all-start.1 = ((s32[8,2,4,2]{0,3,1,2:T(2,128)}), s32[8,2,4,2]{0,3,1,2:T(2,128)S(1)}, u32[]{:S(2)}, u32[]{:S(2)}) async-start(s32[8,2,4,2]{0,3,1,2:T(2,128)} %copy.44), calls=%async_computation.1 | async-start | bytes 16384 | tf_op jit(solution)/shard_map/all_to_all | solution.py:24
  41.4 5.5 %all-to-all-done.1 = s32[8,2,4,2]{0,3,1,2:T(2,128)S(1)} async-done(((s32[8,2,4,2]{0,3,1,2:T(2,128)}), s32[8,2,4,2]{0,3,1,2:T(2,128)S(1)}, u32[]{:S(2)}, u32[]{:S(2)}) %all-to-all-start.1) | async-done | bytes 544 | tf_op jit(solution)/shard_map/all_to_all | solution.py:24
  46.9 3.3 %all-to-all-start.4 = ((bf16[1,16,4,256]{3,2,0,1:T(4,128)(2,1)}), bf16[1,16,4,256]{3,2,0,1:T(4,128)(2,1)S(1)}, u32[]{:S(2)}, u32[]{:S(2)}) async-start(bf16[1,16,4,256]{3,2,0,1:T(4,128)(2,1)} %bitcast.113), calls=%async_computation.4 | async-start | bytes 65536 | tf_op jit(solution)/shard_map/all_to_all | solution.py:18
  50.9 4.1 %all-to-all-done.4 = bf16[1,16,4,256]{3,2,0,1:T(4,128)(2,1)S(1)} async-done(((bf16[1,16,4,256]{3,2,0,1:T(4,128)(2,1)}), bf16[1,16,4,256]{3,2,0,1:T(4,128)(2,1)S(1)}, u32[]{:S(2)}, u32[]{:S(2)}) %all-to-all-start.4) | async-done | bytes 32800 | tf_op jit(solution)/shard_map/all_to_all | solution.py:18
  55.6 3.3 %all-to-all-start.5 = ((bf16[8,2,4,256]{3,0,1,2:T(8,128)(2,1)}), bf16[8,2,4,256]{3,0,1,2:T(8,128)(2,1)S(1)}, u32[]{:S(2)}, u32[]{:S(2)}) async-start(bf16[8,2,4,256]{3,0,1,2:T(8,128)(2,1)} %copy.53), calls=%async_computation.5 | async-start | bytes 65536 | tf_op jit(solution)/shard_map/all_to_all | solution.py:17
  59.0 1.6 reshape.160
  61.3 3.2 %all-to-all-done.5 = bf16[8,2,4,256]{3,0,1,2:T(8,128)(2,1)S(1)} async-done(((bf16[8,2,4,256]{3,0,1,2:T(8,128)(2,1)}), bf16[8,2,4,256]{3,0,1,2:T(8,128)(2,1)S(1)}, u32[]{:S(2)}, u32[]{:S(2)}) %all-to-all-start.5) | async-done | bytes 32800 | tf_op jit(solution)/shard_map/all_to_all | solution.py:17
  66.4 1.5 reshape.165
  68.0 40.5 %reduce-scatter.3.cloned.1.call-done = f32[64,2048]{1,0:T(8,128)} async-done(((f32[64,8192]{1,0:T(8,128)}), f32[64,2048]{1,0:T(8,128)}) %reduce-scatter.3.cloned.1.call-update) | async-done | bytes 524304 | tf_op jit(solution)/shard_map/reduce_scatter | solution.py:74
  108.6 57.2 %all-reduce.3.cloned.1.call-done = f32[64,2048]{1,0:T(8,128)} async-done(((f32[64,2048]{1,0:T(8,128)}), f32[64,2048]{1,0:T(8,128)}) %all-reduce.3.cloned.1.call-update) | async-done | bytes 524304 | tf_op jit(solution)/shard_map/psum | solution.py:75
  165.8 1.8 fusion.16
  167.7 27.3 %all-gather.5.cloned.1.call-done = bf16[64,8192]{1,0:T(8,128)(2,1)} async-done(((bf16[64,2048]{1,0:T(8,128)(2,1)}), bf16[64,8192]{1,0:T(8,128)(2,1)}) %all-gather.5.cloned.1.call-update) | async-done | bytes 1048592 | tf_op jit(solution)/shard_map/all_gather | solution.py:56
  195.1 1.6 reshape.166
  199.3 1.5 reshape.170
  200.9 43.5 %reduce-scatter.5.cloned.1.call-done = f32[64,2048]{1,0:T(8,128)} async-done(((f32[64,8192]{1,0:T(8,128)}), f32[64,2048]{1,0:T(8,128)}) %reduce-scatter.5.cloned.1.call-update) | async-done | bytes 524304 | tf_op jit(solution)/shard_map/reduce_scatter | solution.py:74
  244.4 57.1 %all-reduce.5.cloned.1.call-done = f32[64,2048]{1,0:T(8,128)} async-done(((f32[64,2048]{1,0:T(8,128)}), f32[64,2048]{1,0:T(8,128)}) %all-reduce.5.cloned.1.call-update) | async-done | bytes 524304 | tf_op jit(solution)/shard_map/psum | solution.py:75
  301.5 2.0 add_maximum_fusion
  (48 shorter events, 11.0 us)
Async XLA Ops:
  6.5 58.0 %copy-start = (bf16[2,1,256,256]{3,2,1,0:T(8,128)(2,1)S(1)}, bf16[2,1,256,256]{3,2,1,0:T(8,128)(2,1)}, u32[]{:S(2)}) copy-start(bf16[2,1,256,256]{3,2,1,0:T(8,128)(2,1)} %param.9) | copy-start | bytes 786436
  6.5 52.4 %all-gather.3.cloned.1.call-start = ((), (), s32[]{:S(2)}) async-start(), calls=%async_computation.8 | async-start | bytes 1310720 | tf_op jit(solution)/shard_map/all_gather | solution.py:56
  9.7 9.9 %all-to-all-start.2 = ((s32[1,16,4]{2,0,1:T(1,128)}), s32[1,16,4]{2,0,1:T(1,128)S(1)}, u32[]{:S(2)}, u32[]{:S(2)}) async-start(s32[1,16,4]{2,0,1:T(1,128)} %copy.47), calls=%async_computation.2 | async-start | bytes 16384 | tf_op jit(solution)/shard_map/all_to_all | solution.py:32
  19.6 8.0 %all-to-all-start = ((s32[1,16,4,2]{2,3,0,1:T(2,128)}), s32[1,16,4,2]{2,3,0,1:T(2,128)S(1)}, u32[]{:S(2)}, u32[]{:S(2)}) async-start(s32[1,16,4,2]{2,3,0,1:T(2,128)} %copy.42), calls=%async_computation | async-start | bytes 32768 | tf_op jit(solution)/shard_map/all_to_all | solution.py:25
  27.6 10.5 %all-to-all-start.3 = ((s32[8,2,4]{0,1,2:T(2,128)}), s32[8,2,4]{0,1,2:T(2,128)S(1)}, u32[]{:S(2)}, u32[]{:S(2)}) async-start(s32[8,2,4]{0,1,2:T(2,128)} %copy.48), calls=%async_computation.3 | async-start | bytes 8192 | tf_op jit(solution)/shard_map/all_to_all | solution.py:31
  38.1 8.8 %all-to-all-start.1 = ((s32[8,2,4,2]{0,3,1,2:T(2,128)}), s32[8,2,4,2]{0,3,1,2:T(2,128)S(1)}, u32[]{:S(2)}, u32[]{:S(2)}) async-start(s32[8,2,4,2]{0,3,1,2:T(2,128)} %copy.44), calls=%async_computation.1 | async-start | bytes 16384 | tf_op jit(solution)/shard_map/all_to_all | solution.py:24
  46.9 8.1 %all-to-all-start.4 = ((bf16[1,16,4,256]{3,2,0,1:T(4,128)(2,1)}), bf16[1,16,4,256]{3,2,0,1:T(4,128)(2,1)S(1)}, u32[]{:S(2)}, u32[]{:S(2)}) async-start(bf16[1,16,4,256]{3,2,0,1:T(4,128)(2,1)} %bitcast.113), calls=%async_computation.4 | async-start | bytes 65536 | tf_op jit(solution)/shard_map/all_to_all | solution.py:18
  55.6 8.9 %all-to-all-start.5 = ((bf16[8,2,4,256]{3,0,1,2:T(8,128)(2,1)}), bf16[8,2,4,256]{3,0,1,2:T(8,128)(2,1)S(1)}, u32[]{:S(2)}, u32[]{:S(2)}) async-start(bf16[8,2,4,256]{3,0,1,2:T(8,128)(2,1)} %copy.53), calls=%async_computation.5 | async-start | bytes 65536 | tf_op jit(solution)/shard_map/all_to_all | solution.py:17
  58.9 49.6 %reduce-scatter.3.cloned.1.call-start = ((), (), s32[]{:S(2)}) async-start(), calls=%async_computation.9 | async-start | bytes 2621440 | tf_op jit(solution)/shard_map/reduce_scatter | solution.py:74
  68.0 97.9 %copy-start.1 = (f32[64,2048]{1,0:T(8,128)S(1)}, f32[64,2048]{1,0:T(8,128)}, u32[]{:S(2)}) copy-start(f32[64,2048]{1,0:T(8,128)} %param.5) | copy-start | bytes 1572868
  68.0 97.8 %all-reduce.3.cloned.1.call-start = ((), (), s32[]{:S(2)}) async-start(), calls=%async_computation.10 | async-start | bytes 1048576 | tf_op jit(solution)/shard_map/psum | solution.py:75
  108.5 86.5 %all-gather.5.cloned.1.call-start = ((), (), s32[]{:S(2)}) async-start(), calls=%async_computation.11 | async-start | bytes 1310720 | tf_op jit(solution)/shard_map/all_gather | solution.py:56
  167.7 76.7 %reduce-scatter.5.cloned.1.call-start = ((), (), s32[]{:S(2)}) async-start(), calls=%async_computation.12 | async-start | bytes 2621440 | tf_op jit(solution)/shard_map/reduce_scatter | solution.py:74
  200.8 100.7 %copy-start.2 = (f32[64,2048]{1,0:T(8,128)S(1)}, f32[64,2048]{1,0:T(8,128)}, u32[]{:S(2)}) copy-start(f32[64,2048]{1,0:T(8,128)} %all-reduce.3.cloned.1.call-done) | copy-start | bytes 1572868
  200.9 100.7 %all-reduce.5.cloned.1.call-start = ((), (), s32[]{:S(2)}) async-start(), calls=%async_computation.13 | async-start | bytes 1048576 | tf_op jit(solution)/shard_map/psum | solution.py:75
Sparse Core Ops, SparseCore 0:
  8.9 30.7 all-gather.2
  68.1 40.3 reduce-scatter.2
  111.9 53.8 all-reduce.2
  167.8 27.2 all-gather.4
  201.0 43.3 reduce-scatter.4
  247.6 53.8 all-reduce.4
where the time goes:
time: 311 us; the launch traced here: 310 us
  waiting for transfers between devices  251 us (81%)
  starting transfers between devices  23.4 us (8%)
  between operations  13.6 us (4%)
  local copies, waits for them, and re-layouts  13.3 us (4%)
  other arithmetic  8.7 us (3%)
    psum x2, waiting for transfers between devices, on_device(): facet_sum = lax.psum(facet_part, 'chan')  114 us
    reduce_scatter x2, waiting for transfers between devices, on_device(): lax.psum_scatter(gradient, 'facet', scatter_dimension=1, tiled=True)  83.9 us
    all_gather x2, waiting for transfers between devices, on_device(): lax.all_gather(estimate.astype(jnp.bfloat16), 'facet', axis=1, tiled=True)  27.4 us
  transfers between devices with their start and end apart: 12, of which 11 were waited for; matrix products, arithmetic and copies ran while one was open for 2% of the time, Pallas kernels for 0%

commit v1 on v0

v1 whole, which is shorter than its diff:
```python
import functools

import jax
import jax.numpy as jnp
from jax import lax
from jax.experimental import pallas as pl
from jax.experimental.pallas import tpu as pltpu
from jax.sharding import PartitionSpec as P

STRIP = 128
VISB = 128
TERMS = 2
ITERS = 2
TILE = 8
EXTRA = 16

shrinkage = 0.05
F32, BF16, I32, I16 = jnp.float32, jnp.bfloat16, jnp.int32, jnp.int16
VMEM_LIMIT = 48 * 1024 * 1024


def call(kernel, outs, args, flops, smem=0):
    spaces = [pl.BlockSpec(memory_space=pltpu.SMEM)] * smem
    spaces += [pl.BlockSpec(memory_space=pltpu.VMEM)] * (len(args) - smem)
    moved = sum(a.size * a.dtype.itemsize for a in list(args) + list(outs))
    return pl.pallas_call(
        kernel,
        out_shape=list(outs),
        in_specs=spaces,
        out_specs=[pl.BlockSpec(memory_space=pltpu.VMEM)] * len(outs),
        compiler_params=pltpu.CompilerParams(vmem_limit_bytes=VMEM_LIMIT),
        cost_estimate=pl.CostEstimate(flops=flops, bytes_accessed=moved, transcendentals=0),
    )(*args)


def split(x, parts):
    terms = []
    for _ in range(parts):
        term = x.astype(BF16)
        terms.append(term)
        x = x - term.astype(F32)
    return terms


def one_hot(hit):
    return jnp.where(hit, 1.0, 0.0).astype(BF16)


def sorted_rows(rx, slots, rows):
    total = slots * rows
    out = lax.broadcasted_iota(I32, (total, total), 0)
    src = lax.broadcasted_iota(I32, (total, total), 1)
    hit = src == (out % slots) * rows + out // slots
    return jnp.dot(one_hot(hit), rx, preferred_element_type=F32)


def ref_column(scalars, group, groups, each):
    lanes = groups * each
    ids = scalars[:, :lanes] * 64.0 + scalars[:, lanes : 2 * lanes]
    cols = [ids[:, group * each + i : group * each + i + 1] for i in range(each)]
    return jnp.concatenate(cols, axis=0).astype(I32)


def serve_kernel(slots, groups, each, rows, facet, rx, image, *outs):
    order = sorted_rows(rx[...], slots, rows)
    scalars = order[2 * (each // TERMS) * slots : (2 * (each // TERMS) + 1) * slots]
    height, width = image.shape
    tiles = [
        image[r : r + TILE, c : c + STRIP]
        for r in range(0, height, TILE)
        for c in range(0, width, STRIP)
    ]
    strips = jnp.concatenate(tiles, axis=0)
    count = strips.shape[0]
    table = jnp.concatenate(split(strips, 3), axis=1)
    base = facet[0] * count
    for group in range(groups):
        col = ref_column(scalars, group, groups, each) - base
        lane = lax.broadcasted_iota(I32, (col.shape[0], count), 1)
        got = jnp.dot(one_hot(lane == col), table, preferred_element_type=F32)
        outs[group][...] = (got[:, :STRIP] + got[:, STRIP : 2 * STRIP]) + got[:, 2 * STRIP :]


def measure(est, order, scalars, kernels, slots, groups, each):
    lanes = groups * each
    adjoints = []
    for ch in range(each // TERMS):
        first = ch * TERMS * slots
        sky = jnp.concatenate(
            [est[first : first + slots], est[first + slots : first + 2 * slots]], axis=1
        ).astype(BF16)
        seen = jnp.concatenate(
            [order[first : first + slots], order[first + slots : first + 2 * slots]], axis=1
        )
        kern = kernels[ch]
        predicted = jnp.dot(sky, kern, preferred_element_type=F32)
        live = scalars[:, 2 * lanes + ch : 2 * lanes + ch + 1].astype(I32)
        lane = lax.broadcasted_iota(I32, predicted.shape, 1) % VISB
        residual = jnp.where(lane < live, predicted - seen, 0.0).astype(BF16)
        adjoint = lax.dot_general(
            residual, kern, (((1,), (1,)), ((), ())), preferred_element_type=F32
        )
        adjoints += [adjoint[:, :STRIP], adjoint[:, STRIP:]]
    return jnp.concatenate(adjoints, axis=0)


def encode(adjoint, col, msg):
    refs = adjoint.shape[0]
    top = jnp.max(jnp.abs(adjoint), axis=(0, 1), keepdims=True)
    exponent = jnp.ceil(jnp.log2(jnp.maximum(top, 1e-30) * (1.0 / 32000.0)))
    code = jnp.round(adjoint * jnp.exp2(-exponent))
    msg[:refs] = code.astype(I32).astype(I16)
    eye = lax.broadcasted_iota(I32, (refs, STRIP), 0) == lax.broadcasted_iota(
        I32, (refs, STRIP), 1
    )
    ids = jnp.sum(jnp.where(eye, col.astype(F32), 0.0), axis=0, keepdims=True)
    row = lax.broadcasted_iota(I32, (EXTRA, STRIP), 0)
    extra = jnp.where(row == 0, ids, jnp.where(row == 1, exponent, 0.0))
    msg[refs:] = extra.astype(I32).astype(I16)


def decode(refs, *blocks):
    ids, rows = [], []
    size = refs + EXTRA
    for block in blocks:
        for at in range(0, block.shape[0], size):
            extra = block[at + refs : at + size].astype(I32)
            ids.append(extra[0:1])
            scale = jnp.exp2(extra[1:2].astype(F32))
            value = block[at : at + refs].astype(I32).astype(F32) * scale
            rows.append(jnp.concatenate(split(value, 2), axis=1))
    return jnp.concatenate(ids, axis=1), jnp.concatenate(rows, axis=0)


def first_kernel(slots, groups, each, rows, terms, *refs):
    rx, kernels = refs[0], refs[1]
    parts = refs[2 : 2 + terms]
    start_out, msg = refs[2 + terms :]
    order = sorted_rows(rx[...], slots, rows)
    scalars = order[2 * (each // TERMS) * slots : (2 * (each // TERMS) + 1) * slots]
    est = parts[0][...]
    for part in parts[1:]:
        est = est + part[...]
    start_out[...] = est
    adjoint = measure(est, order, scalars, kernels, slots, groups, each)
    encode(adjoint, ref_column(scalars, 0, groups, each), msg)


def next_kernel(slots, groups, each, rows, step, rx, kernels, est_in, mine, other, est_out, msg):
    order = sorted_rows(rx[...], slots, rows)
    scalars = order[2 * (each // TERMS) * slots : (2 * (each // TERMS) + 1) * slots]
    col = ref_column(scalars, 0, groups, each)
    refs = col.shape[0]
    ids, values = decode(refs, mine, other)
    both = jnp.dot(one_hot(ids == col), values, preferred_element_type=F32)
    gradient = both[:, :STRIP] + both[:, STRIP:]
    est = jnp.maximum(est_in[...] - step * gradient - shrinkage, 0.0)
    est_out[...] = est
    adjoint = measure(est, order, scalars, kernels, slots, groups, each)
    encode(adjoint, col, msg)


def settle_kernel(refs, step, facet, image, mine, other, out):
    ids, values = decode(refs, mine, other)
    height, width = image.shape
    count = height * width // STRIP
    per_band = width // STRIP * TILE
    chunk = min(256, count)
    for at in range(0, count, chunk):
        strip = lax.broadcasted_iota(I32, (chunk, 1), 0) + (facet[0] * count + at)
        both = jnp.dot(one_hot(ids == strip), values, preferred_element_type=F32)
        gradient = both[:, :STRIP] + both[:, STRIP:]
        for t in range(0, chunk, TILE):
            r = (at + t) // per_band * TILE
            c = (at + t) % per_band // TILE * STRIP
            old = image[r : r + TILE, c : c + STRIP]
            out[r : r + TILE, c : c + STRIP] = jnp.maximum(
                old - step * gradient[t : t + TILE] - shrinkage, 0.0
            )


def swap(x, axis, k):
    return lax.ppermute(x, axis, [(i, i ^ k) for i in range(lax.axis_size(axis))])


def spread(msg):
    near = jnp.concatenate(
        [msg] + [swap(msg, "facet", k) for k in range(1, lax.axis_size("facet"))], axis=0
    )
    mine = jnp.concatenate(
        [near] + [swap(near, "chan", k) for k in range(2, lax.axis_size("chan"), 2)], axis=0
    )
    return mine, swap(mine, "chan", 1)


def sparse_device(start_image, visibilities, strip_index, live_counts, uv_kernels):
    C, F = lax.axis_size("chan"), lax.axis_size("facet")
    L = uv_kernels.shape[0]
    each = L * TERMS
    S = C * F
    refs = S * each
    height, width = start_image.shape
    per_facet = height * width // STRIP
    step = float(per_facet * F / (2.5 * S * (L * C) * F))
    rows = 8

    strip_row, column = strip_index[0] // (F * width // STRIP), strip_index[0] % (F * width // STRIP)
    wide = width // STRIP
    numbers = (
        (column // wide) * per_facet
        + (strip_row // TILE) * (wide * TILE)
        + (column % wide) * TILE
        + strip_row % TILE
    )
    numbers = numbers.reshape(C, L, F, TERMS).transpose(0, 2, 1, 3)
    ordered = jnp.stack(
        [jnp.stack([numbers[:, f ^ k] for k in range(F)], axis=1) for f in range(F)], axis=1
    ).reshape(C, F, F * each)
    counts = live_counts[0].reshape(C, L, F).transpose(0, 2, 1)
    scalars = jnp.concatenate([ordered // 64, ordered % 64, counts], axis=2).astype(BF16)
    scalars = jnp.pad(scalars, ((0, 0), (0, 0), (0, STRIP - scalars.shape[2])))
    seen = visibilities[0].reshape(C, L, F, 2, VISB).transpose(0, 2, 1, 3, 4)
    seen = seen.reshape(C, F, 2 * L, VISB)
    sent = jnp.concatenate([seen, scalars[:, :, None]], axis=2)
    sent = jnp.pad(sent, ((0, 0), (0, 0), (0, rows - sent.shape[2]), (0, 0)))
    rx = lax.all_to_all(sent.reshape(S, rows, STRIP), ("chan", "facet"), 0, 0, tiled=True)
    rx = rx.reshape(S * rows, STRIP)

    facet = lax.axis_index("facet").astype(I32).reshape(1)
    piece = jax.ShapeDtypeStruct((refs, STRIP), F32)
    message = jax.ShapeDtypeStruct((refs + EXTRA, STRIP), I16)
    served = call(
        functools.partial(serve_kernel, S, F, each, rows),
        [piece] * F,
        [facet, rx, start_image],
        2 * F * refs * per_facet * 3 * STRIP,
        smem=1,
    )
    parts = [served[0]] + [swap(served[k], "facet", k) for k in range(1, F)]
    est, msg = call(
        functools.partial(first_kernel, S, F, each, rows, F),
        [piece, message],
        [rx, uv_kernels[:, 0]] + parts,
        8 * refs * 2 * STRIP * STRIP,
    )
    image = start_image
    for iteration in range(ITERS):
        mine, other = spread(msg)
        if iteration + 1 < ITERS:
            est, msg = call(
                functools.partial(next_kernel, S, F, each, rows, step),
                [piece, message],
                [rx, uv_kernels[:, 0], est, mine, other],
                4 * refs * S * refs * STRIP,
            )
        (image,) = call(
            functools.partial(settle_kernel, refs, step),
            [jax.ShapeDtypeStruct(image.shape, F32)],
            [facet, image, mine, other],
            4 * per_facet * S * refs * STRIP,
            smem=1,
        )
    return image


def dense_device(start_image, visibilities, strip_index, live_counts, uv_kernels):
    def to_owner(x):
        x = lax.all_to_all(x, "chan", split_axis=1, concat_axis=0, tiled=True)
        return lax.all_to_all(x, "facet", split_axis=2, concat_axis=0, tiled=True)

    observed, picked_ids, live_now = map(to_owner, (visibilities, strip_index, live_counts))
    slot_count = observed.shape[0]
    chan_local, uv_local = uv_kernels.shape[:2]
    slab_rows, facet_width = start_image.shape
    full_width = facet_width * lax.axis_size("facet")
    strip_count = slab_rows * full_width // STRIP
    blocks = slot_count * chan_local * lax.axis_size("chan") * uv_local * lax.axis_size("facet")
    step_size = strip_count / (2.5 * blocks)
    lane_ids = jnp.arange(2 * VISB, dtype=I32) % VISB
    live_mask = lane_ids < live_now[..., None]
    flat_ids = picked_ids.reshape(-1)
    estimate = start_image
    for iteration in range(ITERS):
        full_sky = lax.all_gather(estimate.astype(BF16), "facet", axis=1, tiled=True)
        sky_strips = full_sky.reshape(strip_count, STRIP)
        gathered = sky_strips[picked_ids].reshape(slot_count, chan_local, uv_local, TERMS * STRIP)
        predicted = jnp.einsum("scup,cupq->scuq", gathered, uv_kernels, preferred_element_type=F32)
        residual = jnp.where(live_mask, predicted - observed.astype(F32), 0.0).astype(BF16)
        adjoint = jnp.einsum("scuq,cupq->scup", residual, uv_kernels, preferred_element_type=F32)
        gradient = jnp.zeros((strip_count, STRIP), F32).at[flat_ids].add(adjoint.reshape(-1, STRIP))
        gradient = gradient.reshape(slab_rows, full_width)
        facet_part = lax.psum_scatter(gradient, "facet", scatter_dimension=1, tiled=True)
        facet_sum = lax.psum(facet_part, "chan")
        descent = estimate - step_size * facet_sum
        estimate = jnp.maximum(descent - shrinkage, 0.0)
    return estimate


def on_device(start_image, visibilities, strip_index, live_counts, uv_kernels):
    C, F = lax.axis_size("chan"), lax.axis_size("facet")
    L, uv_local = uv_kernels.shape[:2]
    strips = start_image.size * F // STRIP
    sparse = (
        visibilities.shape[0] == 1
        and uv_local == 1
        and C & (C - 1) == 0
        and F & (F - 1) == 0
        and C > 1
        and C * F * L * TERMS == STRIP
        and 2 * L + 1 <= 8
        and 2 * F * L * TERMS + L <= STRIP
        and strips <= 64 * 256
        and start_image.shape[0] % TILE == 0
        and start_image.shape[1] % STRIP == 0
    )
    run = sparse_device if sparse else dense_device
    return run(start_image, visibilities, strip_index, live_counts, uv_kernels)


def solution(mesh):
    placed = (
        P(None, "facet"),
        P(("chan", "facet"), None, None, None),
        P(("chan", "facet"), None, None, None),
        P(("chan", "facet"), None, None),
        P("chan", "facet", None, None),
    )
    return jax.shard_map(
        on_device, mesh=mesh, in_specs=placed, out_specs=P(None, "facet"), check_vma=False
    )
```

time: 311 us -> 70.4 us (0.23)
  waiting for transfers between devices: 251 us -> 29 us
  between operations: 13.6 us -> 0.23 us
  local copies, waits for them, and re-layouts: 13.3 us -> 3.39 us
  Pallas kernels: 0 us -> 9.11 us
  other arithmetic: 8.7 us -> 0.57 us
  starting transfers between devices: 23.4 us -> 27.8 us
    psum x2 -> x0, waiting for transfers between devices: 114 us -> none  [on_device(): facet_sum = lax.psum(facet_part, 'chan')]
    reduce_scatter x2 -> x0, waiting for transfers between devices: 83.9 us -> none  [on_device(): lax.psum_scatter(gradient, 'facet', scatter_dimension=1, tiled=True)]
    all_gather x2 -> x0, waiting for transfers between devices: 27.4 us -> none  [on_device(): lax.all_gather(estimate.astype(jnp.bfloat16), 'facet', axis=1, tiled=True)]
    ppermute x0 -> x17, waiting for transfers between devices: none -> 21.5 us  [swap(): lax.ppermute(x, axis, [(i, i ^ k) for i in range(lax.axis_size(axis))])]
    ppermute x0 -> x17, starting transfers between devices: none -> 20.5 us  [swap(): lax.ppermute(x, axis, [(i, i ^ k) for i in range(lax.axis_size(axis))])]
    all_to_all x6 -> x1, waiting for transfers between devices: 25 us -> 7.49 us  [sparse_device(): lax.all_to_all(sent.reshape(S, rows, STRIP), ('chan', 'facet'), 0, 0, til...]
    all_to_all x6 -> x1, starting transfers between devices: 23.2 us -> 7.3 us  [sparse_device(): lax.all_to_all(sent.reshape(S, rows, STRIP), ('chan', 'facet'), 0, 0, til...]
    pallas_call x0 -> x5, Pallas kernels: none -> 9.11 us  [call(): pl.pallas_call(kernel, out_shape=list(outs), in_specs=spaces, out_specs=[...]
  transfers between devices with their start and end apart: 12 -> 18, of which waited for: 11 -> 11; matrix products, arithmetic and copies ran while one was open for 2% -> 0% of each run, Pallas kernels for 0% -> 3%
where the time goes in v1:
time: 70.4 us; the launch traced here: 70.1 us
  waiting for transfers between devices  29 us (41%)
  starting transfers between devices  27.8 us (39%)
  Pallas kernels  9.11 us (13%)
  local copies, waits for them, and re-layouts  3.39 us (5%)
    ppermute x17, waiting for transfers between devices, swap(): lax.ppermute(x, axis, [(i, i ^ k) for i in range(lax.axis_size(axis))])  21.5 us
    ppermute x17, starting transfers between devices, swap(): lax.ppermute(x, axis, [(i, i ^ k) for i in range(lax.axis_size(axis))])  20.5 us
    pallas_call x5, Pallas kernels, call(): pl.pallas_call(kernel, out_shape=list(outs), in_specs=spaces, out_specs=[...  9.11 us
    all_to_all x1, waiting for transfers between devices, sparse_device(): lax.all_to_all(sent.reshape(S, rows, STRIP), ('chan', 'facet'), 0, 0, til...  7.49 us
    all_to_all x1, starting transfers between devices, sparse_device(): lax.all_to_all(sent.reshape(S, rows, STRIP), ('chan', 'facet'), 0, 0, til...  7.3 us
    unnamed x20, local copies, waits for them, and re-layouts  1.51 us
  transfers between devices with their start and end apart: 18, of which 11 were waited for; matrix products, arithmetic and copies ran while one was open for 0% of the time, Pallas kernels for 3%

profile of v1, /device:TPU:0, one launch (start us, length us, event | category | flops | bytes accessed | tf_op | source)
XLA Modules:
  0.0 70.1 jit_solution(6861312123373049001)
XLA Ops:
  3.8 7.3 %all-to-all-start = ((bf16[32,8,128]{2,1,0:T(8,128)(2,1)}), bf16[32,8,128]{2,1,0:T(8,128)(2,1)S(1)}, u32[]{:S(2)}, u32[]{:S(2)}) async-start(bf16[32,8,128]{2,1,0:T(8,128)(2,1)} %bitcast.13), calls=%async_computation | async-start | bytes 131072 | tf_op jit(solution)/shard_map/all_to_all | solution.py:226
  11.1 7.5 %all-to-all-done = bf16[32,8,128]{2,1,0:T(8,128)(2,1)S(1)} async-done(((bf16[32,8,128]{2,1,0:T(8,128)(2,1)}), bf16[32,8,128]{2,1,0:T(8,128)(2,1)S(1)}, u32[]{:S(2)}, u32[]{:S(2)}) %all-to-all-start) | async-done | bytes 65568 | tf_op jit(solution)/shard_map/all_to_all | solution.py:226
  18.6 1.2 %shard_map.55 = (f32[128,128]{1,0:T(8,128)S(1)}, f32[128,128]{1,0:T(8,128)S(1)}, f32[128,128]{1,0:T(8,128)S(1)}, f32[128,128]{1,0:T(8,128)S(1)}) custom-call(s32[1]{0:T(128)} %bitcast.facet, bf16[256,128]{1,0:T(8,128)(2,1)S(1)} %bitcast.20, f32[64,2048]{1,0:T(8,128)S(1)} %copy-done.1), custom_call_target="tpu_custom_call" | custom-call | flops 402653184 | bytes 851972 | tf_op jit(solution)/shard_map/pallas_call | solution.py:26
  20.1 1.2 %collective-permute-start.1 = (f32[128,128]{1,0:T(8,128)S(1)}, f32[128,128]{1,0:T(8,128)S(1)}, u32[]{:S(2)}, u32[]{:S(2)}) collective-permute-start(f32[128,128]{1,0:T(8,128)S(1)} %get-tuple-element.14), channel_id=1, source_target_pairs={{0,2},{1,3},{2,0},{3,1},{4,6},{5,7},{6,4},{7,5},{8,10},{9,11},{10,... | collective-permute-start | bytes 196616 | tf_op jit(solution)/shard_map/ppermute | solution.py:183
  21.3 3.0 %collective-permute-start.2 = (f32[128,128]{1,0:T(8,128)S(1)}, f32[128,128]{1,0:T(8,128)S(1)}, u32[]{:S(2)}, u32[]{:S(2)}) collective-permute-start(f32[128,128]{1,0:T(8,128)S(1)} %get-tuple-element.15), channel_id=1, source_target_pairs={{0,3},{1,2},{2,1},{3,0},{4,7},{5,6},{6,5},{7,4},{8,11},{9,10},{10,... | collective-permute-start | bytes 196616 | tf_op jit(solution)/shard_map/ppermute | solution.py:183
  24.8 3.5 %collective-permute-done.1.refs_4_ = f32[128,128]{1,0:T(8,128)S(1)} collective-permute-done((f32[128,128]{1,0:T(8,128)S(1)}, f32[128,128]{1,0:T(8,128)S(1)}, u32[]{:S(2)}, u32[]{:S(2)}) %collective-permute-start.1) | collective-permute-done | bytes 65568 | tf_op jit(solution)/shard_map/ppermute | solution.py:183
  29.0 2.1 %collective-permute-start.5 = (s16[144,128]{1,0:T(8,128)(2,1)S(1)}, s16[144,128]{1,0:T(8,128)(2,1)S(1)}, u32[]{:S(2)}, u32[]{:S(2)}) collective-permute-start(s16[144,128]{1,0:T(8,128)(2,1)S(1)} %get-tuple-element.16), channel_id=1, source_target_pairs={{0,3},{1,2},{2,1},{3,0},{4,7},{5,6},{6,5},{7,4},{8,11},{9,10},{10,... | collective-permute-start | bytes 110600 | tf_op jit(solution)/shard_map/ppermute | solution.py:183
  31.8 1.7 %collective-permute-start.3 = (s16[144,128]{1,0:T(8,128)(2,1)S(1)}, s16[144,128]{1,0:T(8,128)(2,1)S(1)}, u32[]{:S(2)}, u32[]{:S(2)}) collective-permute-start(s16[144,128]{1,0:T(8,128)(2,1)S(1)} %get-tuple-element.16), channel_id=1, source_target_pairs={{0,1},{1,0},{2,3},{3,2},{4,5},{5,4},{6,7},{7,6},{8,9},{9,8},{10,11... | collective-permute-start | bytes 110600 | tf_op jit(solution)/shard_map/ppermute | solution.py:183
  33.5 2.7 %collective-permute-done.3 = s16[144,128]{1,0:T(8,128)(2,1)S(1)} collective-permute-done((s16[144,128]{1,0:T(8,128)(2,1)S(1)}, s16[144,128]{1,0:T(8,128)(2,1)S(1)}, u32[]{:S(2)}, u32[]{:S(2)}) %collective-permute-start.3) | collective-permute-done | bytes 36896 | tf_op jit(solution)/shard_map/ppermute | solution.py:183
  37.6 2.2 %collective-permute-start.8 = (s16[576,128]{1,0:T(8,128)(2,1)S(1)}, s16[576,128]{1,0:T(8,128)(2,1)S(1)}, u32[]{:S(2)}, u32[]{:S(2)}) collective-permute-start(s16[576,128]{1,0:T(8,128)(2,1)S(1)} %get-tuple-element.29), channel_id=1, source_target_pairs={{0,24},{4,28},{8,16},{12,20},{16,8},{20,12},{24,0},{28,4},{1,25},{... | collective-permute-start | bytes 442376 | tf_op jit(solution)/shard_map/ppermute | solution.py:183
  39.8 1.7 %collective-permute-done.6 = s16[576,128]{1,0:T(8,128)(2,1)S(1)} collective-permute-done((s16[576,128]{1,0:T(8,128)(2,1)S(1)}, s16[576,128]{1,0:T(8,128)(2,1)S(1)}, u32[]{:S(2)}, u32[]{:S(2)}) %collective-permute-start.6) | collective-permute-done | bytes 147488 | tf_op jit(solution)/shard_map/ppermute | solution.py:183
  42.2 1.5 %collective-permute-done.8 = s16[576,128]{1,0:T(8,128)(2,1)S(1)} collective-permute-done((s16[576,128]{1,0:T(8,128)(2,1)S(1)}, s16[576,128]{1,0:T(8,128)(2,1)S(1)}, u32[]{:S(2)}, u32[]{:S(2)}) %collective-permute-start.8) | collective-permute-done | bytes 147488 | tf_op jit(solution)/shard_map/ppermute | solution.py:183
  43.8 2.0 %collective-permute-done.9.other = s16[2304,128]{1,0:T(8,128)(2,1)S(1)} collective-permute-done((s16[2304,128]{1,0:T(8,128)(2,1)S(1)}, s16[2304,128]{1,0:T(8,128)(2,1)S(1)}, u32[]{:S(2)}, u32[]{:S(2)}) %collective-permute-start.9) | collective-permute-done | bytes 589856 | tf_op jit(solution)/shard_map/ppermute | solution.py:183
  45.8 1.7 %shard_map.58 = (f32[128,128]{1,0:T(8,128)}, s16[144,128]{1,0:T(8,128)(2,1)S(1)}) custom-call(bf16[256,128]{1,0:T(8,128)(2,1)S(1)} %bitcast.22, bf16[2,256,256]{2,1,0:T(8,128)(2,1)S(1)} %bitcast.19, f32[128,128]{1,0:T(8,128)S(1)} %get-tuple-element.17.est_in, s16[2304,128]{1,0:T(8,128)(2,1)S(1)} %constant_dynamic-update-slice_fusion.4.mine, ...), custom_call_target="tpu_custom_call" | custom-call | flops 268435456 | bytes 1675264 | tf_op jit(solution)/shard_map/pallas_call | solution.py:26
  47.5 1.8 %collective-permute-start.12 = (s16[144,128]{1,0:T(8,128)(2,1)S(1)}, s16[144,128]{1,0:T(8,128)(2,1)S(1)}, u32[]{:S(2)}, u32[]{:S(2)}) collective-permute-start(s16[144,128]{1,0:T(8,128)(2,1)S(1)} %get-tuple-element.18), channel_id=1, source_target_pairs={{0,3},{1,2},{2,1},{3,0},{4,7},{5,6},{6,5},{7,4},{8,11},{9,10},{10,... | collective-permute-start | bytes 110600 | tf_op jit(solution)/shard_map/ppermute | solution.py:183
  49.3 1.0 %collective-permute-start.11 = (s16[144,128]{1,0:T(8,128)(2,1)S(1)}, s16[144,128]{1,0:T(8,128)(2,1)S(1)}, u32[]{:S(2)}, u32[]{:S(2)}) collective-permute-start(s16[144,128]{1,0:T(8,128)(2,1)S(1)} %get-tuple-element.18), channel_id=1, source_target_pairs={{0,2},{1,3},{2,0},{3,1},{4,6},{5,7},{6,4},{7,5},{8,10},{9,11},{10,... | collective-permute-start | bytes 110600 | tf_op jit(solution)/shard_map/ppermute | solution.py:183
  50.2 1.7 %collective-permute-start.10 = (s16[144,128]{1,0:T(8,128)(2,1)S(1)}, s16[144,128]{1,0:T(8,128)(2,1)S(1)}, u32[]{:S(2)}, u32[]{:S(2)}) collective-permute-start(s16[144,128]{1,0:T(8,128)(2,1)S(1)} %get-tuple-element.18), channel_id=1, source_target_pairs={{0,1},{1,0},{2,3},{3,2},{4,5},{5,4},{6,7},{7,6},{8,9},{9,8},{10,11... | collective-permute-start | bytes 110600 | tf_op jit(solution)/shard_map/ppermute | solution.py:183
  51.9 2.7 %collective-permute-done.10 = s16[144,128]{1,0:T(8,128)(2,1)S(1)} collective-permute-done((s16[144,128]{1,0:T(8,128)(2,1)S(1)}, s16[144,128]{1,0:T(8,128)(2,1)S(1)}, u32[]{:S(2)}, u32[]{:S(2)}) %collective-permute-start.10) | collective-permute-done | bytes 36896 | tf_op jit(solution)/shard_map/ppermute | solution.py:183
  54.7 1.4 %collective-permute-start.13 = (s16[576,128]{1,0:T(8,128)(2,1)S(1)}, s16[576,128]{1,0:T(8,128)(2,1)S(1)}, u32[]{:S(2)}, u32[]{:S(2)}) collective-permute-start(s16[576,128]{1,0:T(8,128)(2,1)S(1)} %get-tuple-element.21), channel_id=1, source_target_pairs={{0,8},{4,12},{8,0},{12,4},{16,24},{20,28},{24,16},{28,20},{1,9},{5... | collective-permute-start | bytes 442376 | tf_op jit(solution)/shard_map/ppermute | solution.py:183
  56.1 1.3 %collective-permute-start.14 = (s16[576,128]{1,0:T(8,128)(2,1)S(1)}, s16[576,128]{1,0:T(8,128)(2,1)S(1)}, u32[]{:S(2)}, u32[]{:S(2)}) collective-permute-start(s16[576,128]{1,0:T(8,128)(2,1)S(1)} %get-tuple-element.21), channel_id=1, source_target_pairs={{0,16},{4,20},{8,24},{12,28},{16,0},{20,4},{24,8},{28,12},{1,17},{... | collective-permute-start | bytes 442376 | tf_op jit(solution)/shard_map/ppermute | solution.py:183
  58.2 2.6 %collective-permute-done.13 = s16[576,128]{1,0:T(8,128)(2,1)S(1)} collective-permute-done((s16[576,128]{1,0:T(8,128)(2,1)S(1)}, s16[576,128]{1,0:T(8,128)(2,1)S(1)}, u32[]{:S(2)}, u32[]{:S(2)}) %collective-permute-start.13) | collective-permute-done | bytes 147488 | tf_op jit(solution)/shard_map/ppermute | solution.py:183
  60.8 3.6 %collective-permute-done.14 = s16[576,128]{1,0:T(8,128)(2,1)S(1)} collective-permute-done((s16[576,128]{1,0:T(8,128)(2,1)S(1)}, s16[576,128]{1,0:T(8,128)(2,1)S(1)}, u32[]{:S(2)}, u32[]{:S(2)}) %collective-permute-start.14) | collective-permute-done | bytes 147488 | tf_op jit(solution)/shard_map/ppermute | solution.py:183
  64.6 2.4 %shard_map.57.image = f32[64,2048]{1,0:T(8,128)S(1)} custom-call(s32[1]{0:T(128)} %bitcast.facet, f32[64,2048]{1,0:T(8,128)S(1)} %copy-done.1, s16[2304,128]{1,0:T(8,128)(2,1)S(1)} %constant_dynamic-update-slice_fusion.4.mine, s16[2304,128]{1,0:T(8,128)(2,1)S(1)} %collective-permute-done.9.other), custom_call_target="tpu_custom_call" | custom-call | flops 2147483648 | bytes 2228228 | tf_op jit(solution)/shard_map/pallas_call | solution.py:26
  66.9 3.2 %shard_map.59 = f32[64,2048]{1,0:T(8,128)} custom-call(s32[1]{0:T(128)} %bitcast.facet, f32[64,2048]{1,0:T(8,128)S(1)} %shard_map.57.image, s16[2304,128]{1,0:T(8,128)(2,1)S(1)} %constant_dynamic-update-slice_fusion.15.mine, s16[2304,128]{1,0:T(8,128)(2,1)S(1)} %collective-permute-done.16.other), custom_call_target="tpu_custom_call" | custom-call | flops 2147483648 | bytes 2228228 | tf_op jit(solution)/shard_map/pallas_call | solution.py:26
  (63 shorter events, 9.1 us)
Async XLA Ops:
  1.1 0.7 copy-start.3
  1.1 1.0 %copy-start.2 = (bf16[1,16,4,256]{3,2,1,0:T(4,128)(2,1)S(1)}, bf16[1,16,4,256]{3,2,1,0:T(4,128)(2,1)}, u32[]{:S(2)}) copy-start(bf16[1,16,4,256]{3,2,1,0:T(4,128)(2,1)} %param.6) | copy-start | bytes 98308
  1.8 16.8 %copy-start.1 = (f32[64,2048]{1,0:T(8,128)S(1)}, f32[64,2048]{1,0:T(8,128)}, u32[]{:S(2)}) copy-start(f32[64,2048]{1,0:T(8,128)} %image.3) | copy-start | bytes 1572868
  3.8 14.8 %all-to-all-start = ((bf16[32,8,128]{2,1,0:T(8,128)(2,1)}), bf16[32,8,128]{2,1,0:T(8,128)(2,1)S(1)}, u32[]{:S(2)}, u32[]{:S(2)}) async-start(bf16[32,8,128]{2,1,0:T(8,128)(2,1)} %bitcast.13), calls=%async_computation | async-start | bytes 131072 | tf_op jit(solution)/shard_map/all_to_all | solution.py:226
  18.6 9.7 %copy-start = (bf16[2,1,256,256]{3,2,1,0:T(8,128)(2,1)S(1)}, bf16[2,1,256,256]{3,2,1,0:T(8,128)(2,1)}, u32[]{:S(2)}) copy-start(bf16[2,1,256,256]{3,2,1,0:T(8,128)(2,1)} %param.9) | copy-start | bytes 786436
  19.8 5.0 %collective-permute-start = (f32[128,128]{1,0:T(8,128)S(1)}, f32[128,128]{1,0:T(8,128)S(1)}, u32[]{:S(2)}, u32[]{:S(2)}) collective-permute-start(f32[128,128]{1,0:T(8,128)S(1)} %get-tuple-element.13), channel_id=1, source_target_pairs={{0,1},{1,0},{2,3},{3,2},{4,5},{5,4},{6,7},{7,6},{8,9},{9,8},{10,11... | collective-permute-start | bytes 196616 | tf_op jit(solution)/shard_map/ppermute | solution.py:183
  20.1 8.2 %collective-permute-start.1 = (f32[128,128]{1,0:T(8,128)S(1)}, f32[128,128]{1,0:T(8,128)S(1)}, u32[]{:S(2)}, u32[]{:S(2)}) collective-permute-start(f32[128,128]{1,0:T(8,128)S(1)} %get-tuple-element.14), channel_id=1, source_target_pairs={{0,2},{1,3},{2,0},{3,1},{4,6},{5,7},{6,4},{7,5},{8,10},{9,11},{10,... | collective-permute-start | bytes 196616 | tf_op jit(solution)/shard_map/ppermute | solution.py:183
  21.3 7.1 %collective-permute-start.2 = (f32[128,128]{1,0:T(8,128)S(1)}, f32[128,128]{1,0:T(8,128)S(1)}, u32[]{:S(2)}, u32[]{:S(2)}) collective-permute-start(f32[128,128]{1,0:T(8,128)S(1)} %get-tuple-element.15), channel_id=1, source_target_pairs={{0,3},{1,2},{2,1},{3,0},{4,7},{5,6},{6,5},{7,4},{8,11},{9,10},{10,... | collective-permute-start | bytes 196616 | tf_op jit(solution)/shard_map/ppermute | solution.py:183
  29.0 7.2 %collective-permute-start.5 = (s16[144,128]{1,0:T(8,128)(2,1)S(1)}, s16[144,128]{1,0:T(8,128)(2,1)S(1)}, u32[]{:S(2)}, u32[]{:S(2)}) collective-permute-start(s16[144,128]{1,0:T(8,128)(2,1)S(1)} %get-tuple-element.16), channel_id=1, source_target_pairs={{0,3},{1,2},{2,1},{3,0},{4,7},{5,6},{6,5},{7,4},{8,11},{9,10},{10,... | collective-permute-start | bytes 110600 | tf_op jit(solution)/shard_map/ppermute | solution.py:183
  31.2 5.0 %collective-permute-start.4 = (s16[144,128]{1,0:T(8,128)(2,1)S(1)}, s16[144,128]{1,0:T(8,128)(2,1)S(1)}, u32[]{:S(2)}, u32[]{:S(2)}) collective-permute-start(s16[144,128]{1,0:T(8,128)(2,1)S(1)} %get-tuple-element.16), channel_id=1, source_target_pairs={{0,2},{1,3},{2,0},{3,1},{4,6},{5,7},{6,4},{7,5},{8,10},{9,11},{10,... | collective-permute-start | bytes 110600 | tf_op jit(solution)/shard_map/ppermute | solution.py:183
  31.8 4.4 %collective-permute-start.3 = (s16[144,128]{1,0:T(8,128)(2,1)S(1)}, s16[144,128]{1,0:T(8,128)(2,1)S(1)}, u32[]{:S(2)}, u32[]{:S(2)}) collective-permute-start(s16[144,128]{1,0:T(8,128)(2,1)S(1)} %get-tuple-element.16), channel_id=1, source_target_pairs={{0,1},{1,0},{2,3},{3,2},{4,5},{5,4},{6,7},{7,6},{8,9},{9,8},{10,11... | collective-permute-start | bytes 110600 | tf_op jit(solution)/shard_map/ppermute | solution.py:183
  36.2 5.2 %collective-permute-start.6 = (s16[576,128]{1,0:T(8,128)(2,1)S(1)}, s16[576,128]{1,0:T(8,128)(2,1)S(1)}, u32[]{:S(2)}, u32[]{:S(2)}) collective-permute-start(s16[576,128]{1,0:T(8,128)(2,1)S(1)} %get-tuple-element.29), channel_id=1, source_target_pairs={{0,8},{4,12},{8,0},{12,4},{16,24},{20,28},{24,16},{28,20},{1,9},{5... | collective-permute-start | bytes 442376 | tf_op jit(solution)/shard_map/ppermute | solution.py:183
  37.0 5.2 %collective-permute-start.7 = (s16[576,128]{1,0:T(8,128)(2,1)S(1)}, s16[576,128]{1,0:T(8,128)(2,1)S(1)}, u32[]{:S(2)}, u32[]{:S(2)}) collective-permute-start(s16[576,128]{1,0:T(8,128)(2,1)S(1)} %get-tuple-element.29), channel_id=1, source_target_pairs={{0,16},{4,20},{8,24},{12,28},{16,0},{20,4},{24,8},{28,12},{1,17},{... | collective-permute-start | bytes 442376 | tf_op jit(solution)/shard_map/ppermute | solution.py:183
  37.6 6.1 %collective-permute-start.8 = (s16[576,128]{1,0:T(8,128)(2,1)S(1)}, s16[576,128]{1,0:T(8,128)(2,1)S(1)}, u32[]{:S(2)}, u32[]{:S(2)}) collective-permute-start(s16[576,128]{1,0:T(8,128)(2,1)S(1)} %get-tuple-element.29), channel_id=1, source_target_pairs={{0,24},{4,28},{8,16},{12,20},{16,8},{20,12},{24,0},{28,4},{1,25},{... | collective-permute-start | bytes 442376 | tf_op jit(solution)/shard_map/ppermute | solution.py:183
  43.7 2.1 %collective-permute-start.9 = (s16[2304,128]{1,0:T(8,128)(2,1)S(1)}, s16[2304,128]{1,0:T(8,128)(2,1)S(1)}, u32[]{:S(2)}, u32[]{:S(2)}) collective-permute-start(s16[2304,128]{1,0:T(8,128)(2,1)S(1)} %constant_dynamic-update-slice_fusion.4.mine), channel_id=1, source_target_pairs={{0,4},{4,0},{8,12},{12,8},{16,20},{20,16},{24,28},{28,24},{1,5},{5... | collective-permute-start | bytes 1769480 | tf_op jit(solution)/shard_map/ppermute | solution.py:183
  47.5 7.1 %collective-permute-start.12 = (s16[144,128]{1,0:T(8,128)(2,1)S(1)}, s16[144,128]{1,0:T(8,128)(2,1)S(1)}, u32[]{:S(2)}, u32[]{:S(2)}) collective-permute-start(s16[144,128]{1,0:T(8,128)(2,1)S(1)} %get-tuple-element.18), channel_id=1, source_target_pairs={{0,3},{1,2},{2,1},{3,0},{4,7},{5,6},{6,5},{7,4},{8,11},{9,10},{10,... | collective-permute-start | bytes 110600 | tf_op jit(solution)/shard_map/ppermute | solution.py:183
  49.3 5.3 %collective-permute-start.11 = (s16[144,128]{1,0:T(8,128)(2,1)S(1)}, s16[144,128]{1,0:T(8,128)(2,1)S(1)}, u32[]{:S(2)}, u32[]{:S(2)}) collective-permute-start(s16[144,128]{1,0:T(8,128)(2,1)S(1)} %get-tuple-element.18), channel_id=1, source_target_pairs={{0,2},{1,3},{2,0},{3,1},{4,6},{5,7},{6,4},{7,5},{8,10},{9,11},{10,... | collective-permute-start | bytes 110600 | tf_op jit(solution)/shard_map/ppermute | solution.py:183
  50.2 4.4 %collective-permute-start.10 = (s16[144,128]{1,0:T(8,128)(2,1)S(1)}, s16[144,128]{1,0:T(8,128)(2,1)S(1)}, u32[]{:S(2)}, u32[]{:S(2)}) collective-permute-start(s16[144,128]{1,0:T(8,128)(2,1)S(1)} %get-tuple-element.18), channel_id=1, source_target_pairs={{0,1},{1,0},{2,3},{3,2},{4,5},{5,4},{6,7},{7,6},{8,9},{9,8},{10,11... | collective-permute-start | bytes 110600 | tf_op jit(solution)/shard_map/ppermute | solution.py:183
  54.7 6.1 %collective-permute-start.13 = (s16[576,128]{1,0:T(8,128)(2,1)S(1)}, s16[576,128]{1,0:T(8,128)(2,1)S(1)}, u32[]{:S(2)}, u32[]{:S(2)}) collective-permute-start(s16[576,128]{1,0:T(8,128)(2,1)S(1)} %get-tuple-element.21), channel_id=1, source_target_pairs={{0,8},{4,12},{8,0},{12,4},{16,24},{20,28},{24,16},{28,20},{1,9},{5... | collective-permute-start | bytes 442376 | tf_op jit(solution)/shard_map/ppermute | solution.py:183
  56.1 8.3 %collective-permute-start.14 = (s16[576,128]{1,0:T(8,128)(2,1)S(1)}, s16[576,128]{1,0:T(8,128)(2,1)S(1)}, u32[]{:S(2)}, u32[]{:S(2)}) collective-permute-start(s16[576,128]{1,0:T(8,128)(2,1)S(1)} %get-tuple-element.21), channel_id=1, source_target_pairs={{0,16},{4,20},{8,24},{12,28},{16,0},{20,4},{24,8},{28,12},{1,17},{... | collective-permute-start | bytes 442376 | tf_op jit(solution)/shard_map/ppermute | solution.py:183
  57.4 7.0 %collective-permute-start.15 = (s16[576,128]{1,0:T(8,128)(2,1)S(1)}, s16[576,128]{1,0:T(8,128)(2,1)S(1)}, u32[]{:S(2)}, u32[]{:S(2)}) collective-permute-start(s16[576,128]{1,0:T(8,128)(2,1)S(1)} %get-tuple-element.21), channel_id=1, source_target_pairs={{0,24},{4,28},{8,16},{12,20},{16,8},{20,12},{24,0},{28,4},{1,25},{... | collective-permute-start | bytes 442376 | tf_op jit(solution)/shard_map/ppermute | solution.py:183
  64.5 2.5 %collective-permute-start.16 = (s16[2304,128]{1,0:T(8,128)(2,1)S(1)}, s16[2304,128]{1,0:T(8,128)(2,1)S(1)}, u32[]{:S(2)}, u32[]{:S(2)}) collective-permute-start(s16[2304,128]{1,0:T(8,128)(2,1)S(1)} %constant_dynamic-update-slice_fusion.15.mine), channel_id=1, source_target_pairs={{0,4},{4,0},{8,12},{12,8},{16,20},{20,16},{24,28},{28,24},{1,5},{5... | collective-permute-start | bytes 1769480 | tf_op jit(solution)/shard_map/ppermute | solution.py:183

commit v2 on v1

v2 whole, which is shorter than its diff:
```python
import functools

import jax
import jax.numpy as jnp
from jax import lax
from jax.experimental import pallas as pl
from jax.experimental.pallas import tpu as pltpu
from jax.sharding import PartitionSpec as P

STRIP = 128
VISB = 128
TERMS = 2
ITERS = 2
TILE = 8
EXTRA = 16
BLOCK = 16
LEVELS = 65535.0 / 3.0
LEAST = 119

shrinkage = 0.05
F32, BF16, I32, I16 = jnp.float32, jnp.bfloat16, jnp.int32, jnp.int16
VMEM_LIMIT = 48 * 1024 * 1024


def call(kernel, outs, args, flops, smem=0):
    spaces = [pl.BlockSpec(memory_space=pltpu.SMEM)] * smem
    spaces += [pl.BlockSpec(memory_space=pltpu.VMEM)] * (len(args) - smem)
    moved = sum(a.size * a.dtype.itemsize for a in list(args) + list(outs))
    return pl.pallas_call(
        kernel,
        out_shape=list(outs),
        in_specs=spaces,
        out_specs=[pl.BlockSpec(memory_space=pltpu.VMEM)] * len(outs),
        compiler_params=pltpu.CompilerParams(vmem_limit_bytes=VMEM_LIMIT),
        cost_estimate=pl.CostEstimate(flops=flops, bytes_accessed=moved, transcendentals=0),
    )(*args)


def split(x, parts):
    terms = []
    for _ in range(parts):
        term = x.astype(BF16)
        terms.append(term)
        x = x - term.astype(F32)
    return terms


def one_hot(hit):
    return jnp.where(hit, 1.0, 0.0).astype(BF16)


def iota(shape, dim):
    return lax.broadcasted_iota(I32, shape, dim)


def code_floats(x):
    size = jnp.abs(x)
    power = jnp.maximum(jnp.floor(jnp.log2(jnp.maximum(size, 1e-37))), -LEAST)
    code = (power + LEAST) * 128.0 + jnp.round(size * jnp.exp2(7.0 - power))
    return jnp.where(x < 0, -code, code).astype(I32)


def floats_of(code):
    size = jnp.abs(code)
    power = jnp.maximum((size >> 7) - 1, 0)
    lead = (size - power * 128).astype(F32)
    value = lead * jnp.exp2((power - (LEAST + 7)).astype(F32))
    return jnp.where(code < 0, -value, value).astype(BF16)


def halves(x):
    return jnp.concatenate([(x >> 6).astype(F32), (x & 63).astype(F32)], axis=1).astype(BF16)


def joined(x):
    return x[:, :STRIP] * 64.0 + x[:, STRIP:]


def tiled_strips(rows):
    height, width = rows.shape
    return jnp.concatenate(
        [
            rows[r : r + TILE, c : c + STRIP]
            for r in range(0, height, TILE)
            for c in range(0, width, STRIP)
        ],
        axis=0,
    )


def log2(n):
    return n.bit_length() - 1


def pack_kernel(C, F, L, place, image, seen, numbers, *outs):
    c, f = place[0], place[1]
    height, width = image.shape
    band = height // C
    wide = width // STRIP
    per_facet = height * wide
    piece = per_facet // C
    strips = tiled_strips(image[pl.ds(pl.multiple_of(c * band, TILE), band), :])
    share = (jnp.round(strips * LEVELS) - 32768.0).astype(I32).astype(I16)
    chips = C // 2
    size = chips * BLOCK
    rows = F * size
    row = iota((rows, 1), 0)
    k, j, i = row // size, (row // BLOCK) % chips, row % BLOCK
    uv = k ^ f
    channel = ((c >> 1) ^ j) * (2 * L) + (i >> 1)
    raw = numbers[...]
    across, column = raw >> log2(F * wide), raw & (F * wide - 1)
    strip = (
        (column >> log2(wide)) * per_facet
        + (across >> 3) * (wide * TILE)
        + (column & (wide - 1)) * TILE
        + (across & 7)
    )
    ids = jnp.where(iota(raw.shape, 0) < TERMS * F, strip, raw)
    is_seen = i < 4 * L
    pick = is_seen & (iota((rows, seen.shape[0]), 1) == channel * F + uv)
    both = jnp.dot(one_hot(pick), seen[...], preferred_element_type=F32)
    values = code_floats(jnp.where((i & 1) == 0, both[:, :VISB], both[:, VISB:]))
    pick = (i >= 4 * L) & (iota((rows, raw.shape[0]), 1) == (i - 4 * L) * F + uv)
    whole = joined(jnp.dot(one_hot(pick), halves(ids), preferred_element_type=F32))
    blocks = jnp.where(is_seen, values, whole.astype(I32)).astype(I16)
    for at in range(F):
        if at:
            outs[at][:piece] = share
            outs[at][piece:] = blocks[at * size : (at + 1) * size]
        else:
            outs[at][...] = blocks[:size]


def pass_kernel(F, piece, *refs):
    got, outs = refs[:F], refs[F:]
    for j, out in enumerate(outs):
        for k in range(1, F):
            out[(k - 1) * piece : k * piece] = got[k][:piece]
        for k in range(F):
            at = (F - 1) * piece + k * BLOCK
            first = (piece if k else 0) + j * BLOCK
            out[at : at + BLOCK] = got[k][first : first + BLOCK]


def first_kernel(C, F, L, place, image, kernels, mine, other, start_out, seen_out, scalars_out, msg):
    c, f = place[0], place[1]
    chips, slots = C // 2, C * F
    height, width = image.shape
    per_facet = height * width // STRIP
    piece = per_facet // C
    size = (F - 1) * piece + F * BLOCK
    tiles, shares = [], []
    for got in (mine, other):
        for q in range(chips):
            shares.append(got[q * size : q * size + (F - 1) * piece].astype(I32))
            tiles.append(got[q * size + (F - 1) * piece : (q + 1) * size].astype(I32))
    blocks = jnp.concatenate(tiles, axis=0)
    out = iota((4 * slots, 1), 0)
    source = (out % slots) * BLOCK + 2 * L * (c & 1) + out // slots
    pick = iota((4 * slots, slots * BLOCK), 1) == source
    seen = jnp.dot(one_hot(pick), floats_of(blocks), preferred_element_type=F32)
    out = iota((3 * slots, 1), 0)
    source = (out % slots) * BLOCK + 4 * L + out // slots
    pick = iota((3 * slots, slots * BLOCK), 1) == source
    whole = joined(jnp.dot(one_hot(pick), halves(blocks), preferred_element_type=F32))
    lane = iota((slots, STRIP), 1)
    scalars = jnp.zeros((slots, STRIP), F32)
    for kind in range(3):
        for ch in range(L):
            of_kind = whole[kind * slots : (kind + 1) * slots]
            value = jnp.sum(jnp.where(lane == c * L + ch, of_kind, 0.0), axis=1, keepdims=True)
            at = L * TERMS + ch if kind == TERMS else ch * TERMS + kind
            scalars = jnp.where(lane == at, value, scalars)
    col = ref_column(scalars, L)
    facet, local = col >> log2(per_facet), col & (per_facet - 1)
    k, d = facet ^ f, (local >> log2(piece)) ^ c
    turn = ((d & 1) * chips + (d >> 1)) * (F - 1) + k - 1
    place_of = jnp.where(k == 0, local, per_facet + turn * piece + (local & (piece - 1)))
    own = jnp.round(tiled_strips(image) * LEVELS)
    levels = jnp.concatenate([own] + [s.astype(F32) + 32768.0 for s in shares], axis=0)
    table = jnp.concatenate(split(levels, 2), axis=1)
    pick = iota((col.shape[0], table.shape[0]), 1) == place_of
    both = jnp.dot(one_hot(pick), table, preferred_element_type=F32)
    est = (both[:, :STRIP] + both[:, STRIP:]) * (1.0 / LEVELS)
    start_out[...] = est
    seen_out[...] = seen.astype(BF16)
    scalars_out[...] = scalars
    encode(measure(est, seen, scalars, kernels, L), col, msg)


def ref_column(scalars, L):
    cols = [scalars[:, i : i + 1] for i in range(L * TERMS)]
    return jnp.concatenate(cols, axis=0).astype(I32)


def measure(est, seen, scalars, kernels, L):
    slots = scalars.shape[0]
    adjoints = []
    for ch in range(L):
        a, b, end = (ch * TERMS + i for i in range(3))
        sky = jnp.concatenate(
            [est[a * slots : b * slots], est[b * slots : end * slots]], axis=1
        ).astype(BF16)
        observed = jnp.concatenate(
            [seen[a * slots : b * slots], seen[b * slots : end * slots]], axis=1
        )
        predicted = jnp.dot(sky, kernels[ch], preferred_element_type=F32)
        live = scalars[:, L * TERMS + ch : L * TERMS + ch + 1].astype(I32)
        lane = iota(predicted.shape, 1) & (VISB - 1)
        residual = jnp.where(lane < live, predicted - observed, 0.0).astype(BF16)
        adjoint = lax.dot_general(
            residual, kernels[ch], (((1,), (1,)), ((), ())), preferred_element_type=F32
        )
        adjoints += [adjoint[:, :STRIP], adjoint[:, STRIP:]]
    return jnp.concatenate(adjoints, axis=0)


def encode(adjoint, col, msg):
    refs = adjoint.shape[0]
    top = jnp.max(jnp.abs(adjoint), axis=(0, 1), keepdims=True)
    exponent = jnp.ceil(jnp.log2(jnp.maximum(top, 1e-30) * (1.0 / 32000.0)))
    code = jnp.round(adjoint * jnp.exp2(-exponent))
    msg[:refs] = code.astype(I32).astype(I16)
    eye = iota((refs, STRIP), 0) == iota((refs, STRIP), 1)
    ids = jnp.sum(jnp.where(eye, col.astype(F32), 0.0), axis=0, keepdims=True)
    row = iota((EXTRA, STRIP), 0)
    extra = jnp.where(row == 0, ids, jnp.where(row == 1, exponent, 0.0))
    msg[refs:] = extra.astype(I32).astype(I16)


def decode(block):
    ids, rows = [], []
    size = STRIP + EXTRA
    for at in range(0, block.shape[0], size):
        extra = block[at + STRIP : at + size].astype(I32)
        ids.append(extra[0:1])
        scale = jnp.exp2(extra[1:2].astype(F32))
        value = block[at : at + STRIP].astype(I32).astype(F32) * scale
        rows.append(jnp.concatenate(split(value, 2), axis=1))
    return jnp.concatenate(ids, axis=1), jnp.concatenate(rows, axis=0)


def summed(ids, values, strips):
    both = jnp.dot(one_hot(ids == strips), values, preferred_element_type=F32)
    return both[:, :STRIP] + both[:, STRIP:]


def part_kernel(L, scalars, block, out):
    out[...] = summed(*decode(block), ref_column(scalars[...], L))


def next_kernel(L, step, scalars_in, seen, kernels, est_in, part, block, msg):
    scalars = scalars_in[...]
    col = ref_column(scalars, L)
    gradient = part[...] + summed(*decode(block), col)
    est = jnp.maximum(est_in[...] - step * gradient - shrinkage, 0.0)
    encode(measure(est, seen[...].astype(F32), scalars, kernels, L), col, msg)


def facet_part_kernel(place, block, out):
    ids, values = decode(block)
    count = out.shape[0]
    chunk = min(256, count)
    for at in range(0, count, chunk):
        out[at : at + chunk] = summed(ids, values, iota((chunk, 1), 0) + (place[1] * count + at))


def settle_kernel(step, place, image, part, block, out):
    ids, values = decode(block)
    height, width = image.shape
    count = part.shape[0]
    per_band = width // STRIP * TILE
    chunk = min(256, count)
    for at in range(0, count, chunk):
        strips = iota((chunk, 1), 0) + (place[1] * count + at)
        gradient = part[at : at + chunk] + summed(ids, values, strips)
        for t in range(0, chunk, TILE):
            r = (at + t) // per_band * TILE
            c = (at + t) % per_band // TILE * STRIP
            old = image[r : r + TILE, c : c + STRIP]
            out[r : r + TILE, c : c + STRIP] = jnp.maximum(
                old - step * gradient[t : t + TILE] - shrinkage, 0.0
            )


def swap(x, axis, k):
    return lax.ppermute(x, axis, [(i, i ^ k) for i in range(lax.axis_size(axis))])


def sparse_device(start_image, visibilities, strip_index, live_counts, uv_kernels):
    C, F = lax.axis_size("chan"), lax.axis_size("facet")
    L = uv_kernels.shape[0]
    refs = C * F * L * TERMS
    per_facet = start_image.size // STRIP
    piece = per_facet // C
    chips = C // 2
    step = float(per_facet * F / (2.5 * C * F * (L * C) * F))
    place = jnp.stack([lax.axis_index("chan"), lax.axis_index("facet")]).astype(I32)
    kernels = uv_kernels[:, 0]

    numbers = jnp.concatenate(
        [strip_index[0].transpose(2, 1, 0).reshape(TERMS * F, L * C), live_counts[0].T], axis=0
    )
    numbers = jnp.pad(numbers, ((0, 16 - numbers.shape[0]), (0, STRIP - numbers.shape[1])))
    seen = visibilities.reshape(L * C * F, 2 * VISB)
    blocks = jax.ShapeDtypeStruct((chips * BLOCK, STRIP), I16)
    both = jax.ShapeDtypeStruct((piece + chips * BLOCK, STRIP), I16)
    packed = call(
        functools.partial(pack_kernel, C, F, L),
        [blocks] + [both] * (F - 1),
        [place, start_image, seen, numbers],
        10**8,
        smem=1,
    )
    got = [packed[0]] + [swap(packed[k], "facet", k) for k in range(1, F)]
    passed = call(
        functools.partial(pass_kernel, F, piece),
        [jax.ShapeDtypeStruct(((F - 1) * piece + F * BLOCK, STRIP), I16)] * chips,
        got,
        10**6,
    )
    mine = jnp.concatenate(
        [passed[0]] + [swap(passed[j], "chan", 2 * j) for j in range(1, chips)], axis=0
    )
    other = swap(mine, "chan", 1)

    at_refs = jax.ShapeDtypeStruct((refs, STRIP), F32)
    message = jax.ShapeDtypeStruct((refs + EXTRA, STRIP), I16)
    facet_strips = jax.ShapeDtypeStruct((per_facet, STRIP), F32)
    est, observed, scalars, msg = call(
        functools.partial(first_kernel, C, F, L),
        [
            at_refs,
            jax.ShapeDtypeStruct((refs, STRIP), BF16),
            jax.ShapeDtypeStruct((C * F, STRIP), F32),
            message,
        ],
        [place, start_image, kernels, mine, other],
        5 * 10**8,
        smem=1,
    )

    image = start_image
    held = None
    for iteration in range(ITERS):
        last = iteration + 1 == ITERS
        near = jnp.concatenate([msg] + [swap(msg, "facet", k) for k in range(1, F)], axis=0)
        if held is not None:
            image = settle(step, place, image, *held)
            near, image = lax.optimization_barrier((near, image))
        mine = jnp.concatenate([near] + [swap(near, "chan", 2 * j) for j in range(1, chips)], axis=0)
        other = swap(mine, "chan", 1)
        if not last:
            (part,) = call(
                functools.partial(part_kernel, L), [at_refs], [scalars, mine], 3 * 10**8
            )
            (msg,) = call(
                functools.partial(next_kernel, L, step),
                [message],
                [scalars, observed, kernels, est, part, other],
                3 * 10**8,
            )
        (part,) = call(facet_part_kernel, [facet_strips], [place, mine], 2 * 10**9, smem=1)
        held = part, other
    return settle(step, place, image, *held)


def settle(step, place, image, part, other):
    (image,) = call(
        functools.partial(settle_kernel, step),
        [jax.ShapeDtypeStruct(image.shape, F32)],
        [place, image, part, other],
        2 * 10**9,
        smem=1,
    )
    return image


def dense_device(start_image, visibilities, strip_index, live_counts, uv_kernels):
    def to_owner(x):
        x = lax.all_to_all(x, "chan", split_axis=1, concat_axis=0, tiled=True)
        return lax.all_to_all(x, "facet", split_axis=2, concat_axis=0, tiled=True)

    observed, picked_ids, live_now = map(to_owner, (visibilities, strip_index, live_counts))
    slot_count = observed.shape[0]
    chan_local, uv_local = uv_kernels.shape[:2]
    slab_rows, facet_width = start_image.shape
    full_width = facet_width * lax.axis_size("facet")
    strip_count = slab_rows * full_width // STRIP
    blocks = slot_count * chan_local * lax.axis_size("chan") * uv_local * lax.axis_size("facet")
    step_size = strip_count / (2.5 * blocks)
    lane_ids = jnp.arange(2 * VISB, dtype=I32) % VISB
    live_mask = lane_ids < live_now[..., None]
    flat_ids = picked_ids.reshape(-1)
    estimate = start_image
    for iteration in range(ITERS):
        full_sky = lax.all_gather(estimate.astype(BF16), "facet", axis=1, tiled=True)
        sky_strips = full_sky.reshape(strip_count, STRIP)
        gathered = sky_strips[picked_ids].reshape(slot_count, chan_local, uv_local, TERMS * STRIP)
        predicted = jnp.einsum("scup,cupq->scuq", gathered, uv_kernels, preferred_element_type=F32)
        residual = jnp.where(live_mask, predicted - observed.astype(F32), 0.0).astype(BF16)
        adjoint = jnp.einsum("scuq,cupq->scup", residual, uv_kernels, preferred_element_type=F32)
        gradient = jnp.zeros((strip_count, STRIP), F32).at[flat_ids].add(adjoint.reshape(-1, STRIP))
        gradient = gradient.reshape(slab_rows, full_width)
        facet_part = lax.psum_scatter(gradient, "facet", scatter_dimension=1, tiled=True)
        facet_sum = lax.psum(facet_part, "chan")
        descent = estimate - step_size * facet_sum
        estimate = jnp.maximum(descent - shrinkage, 0.0)
    return estimate


def on_device(start_image, visibilities, strip_index, live_counts, uv_kernels):
    C, F = lax.axis_size("chan"), lax.axis_size("facet")
    L, uv_local = uv_kernels.shape[:2]
    strips = start_image.size * F // STRIP
    sparse = (
        visibilities.shape[0] == 1
        and uv_local == 1
        and C & (C - 1) == 0
        and F & (F - 1) == 0
        and C >= 4
        and F >= 2
        and C * F * L * TERMS == STRIP
        and 4 * L + TERMS + 1 <= BLOCK
        and (TERMS + 1) * F <= 16
        and L * C <= STRIP
        and strips <= 64 * 256
        and strips & (strips - 1) == 0
        and start_image.shape[0] % (C * TILE) == 0
        and start_image.shape[1] % STRIP == 0
        and start_image.size // STRIP // C % 16 == 0
    )
    run = sparse_device if sparse else dense_device
    return run(start_image, visibilities, strip_index, live_counts, uv_kernels)


def solution(mesh):
    placed = (
        P(None, "facet"),
        P(("chan", "facet"), None, None, None),
        P(("chan", "facet"), None, None, None),
        P(("chan", "facet"), None, None),
        P("chan", "facet", None, None),
    )
    return jax.shard_map(
        on_device, mesh=mesh, in_specs=placed, out_specs=P(None, "facet"), check_vma=False
    )
```

time: 70.4 us -> 70.6 us (level)
  Pallas kernels: 9.11 us -> 12.7 us
  starting transfers between devices: 27.8 us -> 25.5 us
    all_to_all x1 -> x0, waiting for transfers between devices: 7.49 us -> none  [sparse_device(): lax.all_to_all(sent.reshape(S, rows, STRIP), ('chan', 'facet'), 0, 0, til...]
    all_to_all x1 -> x0, starting transfers between devices: 7.3 us -> none  [sparse_device(): lax.all_to_all(sent.reshape(S, rows, STRIP), ('chan', 'facet'), 0, 0, til...]
    ppermute x17 -> x21, waiting for transfers between devices: 21.5 us -> 28.4 us  [swap(): lax.ppermute(x, axis, [(i, i ^ k) for i in range(lax.axis_size(axis))])]
    ppermute x17 -> x21, starting transfers between devices: 20.5 us -> 25.5 us  [swap(): lax.ppermute(x, axis, [(i, i ^ k) for i in range(lax.axis_size(axis))])]
    pallas_call x5 -> x9, Pallas kernels: 9.11 us -> 12.7 us  [call(): pl.pallas_call(kernel, out_shape=list(outs), in_specs=spaces, out_specs=[...]
    unnamed x20 -> x22, local copies, waits for them, and re-layouts: 1.51 us -> 2.58 us
    another operation x10 -> x0, local copies, waits for them, and re-layouts: 0.86 us -> none  [the longest x3 0.31 us: sparse_device(): jnp.stack([numbers[:, f ^ k] for k in range(F)], axis=1)]
    reshape x0 -> x1, local copies, waits for them, and re-layouts: none -> 0.77 us  [sparse_device(): seen = visibilities.reshape(L * C * F, 2 * VISB)]
  transfers between devices with their start and end apart: 18 -> 21, of which waited for: 11 -> 14; matrix products, arithmetic and copies ran while one was open for 0% -> 0% of each run, Pallas kernels for 3% -> 8%
where the time goes in v2:
time: 70.6 us; the launch traced here: 70.3 us
  waiting for transfers between devices  28.4 us (40%)
  starting transfers between devices  25.5 us (36%)
  Pallas kernels  12.7 us (18%)
  local copies, waits for them, and re-layouts  3.44 us (5%)
    ppermute x21, waiting for transfers between devices, swap(): lax.ppermute(x, axis, [(i, i ^ k) for i in range(lax.axis_size(axis))])  28.4 us
    ppermute x21, starting transfers between devices, swap(): lax.ppermute(x, axis, [(i, i ^ k) for i in range(lax.axis_size(axis))])  25.5 us
    pallas_call x9, Pallas kernels, call(): pl.pallas_call(kernel, out_shape=list(outs), in_specs=spaces, out_specs=[...  12.7 us
    unnamed x22, local copies, waits for them, and re-layouts  2.58 us
  transfers between devices with their start and end apart: 21, of which 14 were waited for; matrix products, arithmetic and copies ran while one was open for 0% of the time, Pallas kernels for 8%

profile of v2, /device:TPU:0, one launch (start us, length us, event | category | flops | bytes accessed | tf_op | source)
XLA Modules:
  0.0 70.3 jit_solution(2278601234571940503)
XLA Ops:
  4.1 3.1 %collective-permute-start = (s16[192,128]{1,0:T(8,128)(2,1)S(1)}, s16[192,128]{1,0:T(8,128)(2,1)S(1)}, u32[]{:S(2)}, u32[]{:S(2)}) collective-permute-start(s16[192,128]{1,0:T(8,128)(2,1)S(1)} %get-tuple-element.20), channel_id=1, source_target_pairs={{0,1},{1,0},{2,3},{3,2},{4,5},{5,4},{6,7},{7,6},{8,9},{9,8},{10,11... | collective-permute-start | bytes 147464 | tf_op jit(solution)/shard_map/ppermute | solution.py:288
  7.2 2.6 %collective-permute-start.1 = (s16[192,128]{1,0:T(8,128)(2,1)S(1)}, s16[192,128]{1,0:T(8,128)(2,1)S(1)}, u32[]{:S(2)}, u32[]{:S(2)}) collective-permute-start(s16[192,128]{1,0:T(8,128)(2,1)S(1)} %get-tuple-element.21), channel_id=1, source_target_pairs={{0,2},{1,3},{2,0},{3,1},{4,6},{5,7},{6,4},{7,5},{8,10},{9,11},{10,... | collective-permute-start | bytes 147464 | tf_op jit(solution)/shard_map/ppermute | solution.py:288
  9.8 3.3 %collective-permute-done.1.refs_2_ = s16[192,128]{1,0:T(8,128)(2,1)S(1)} collective-permute-done((s16[192,128]{1,0:T(8,128)(2,1)S(1)}, s16[192,128]{1,0:T(8,128)(2,1)S(1)}, u32[]{:S(2)}, u32[]{:S(2)}) %collective-permute-start.1) | collective-permute-done | bytes 49184 | tf_op jit(solution)/shard_map/ppermute | solution.py:288
  13.1 2.6 %collective-permute-done.2.refs_3_ = s16[192,128]{1,0:T(8,128)(2,1)S(1)} collective-permute-done((s16[192,128]{1,0:T(8,128)(2,1)S(1)}, s16[192,128]{1,0:T(8,128)(2,1)S(1)}, u32[]{:S(2)}, u32[]{:S(2)}) %collective-permute-start.2) | collective-permute-done | bytes 49184 | tf_op jit(solution)/shard_map/ppermute | solution.py:288
  15.7 1.6 %collective-permute-start.3 = (s16[448,128]{1,0:T(8,128)(2,1)S(1)}, s16[448,128]{1,0:T(8,128)(2,1)S(1)}, u32[]{:S(2)}, u32[]{:S(2)}) collective-permute-start(s16[448,128]{1,0:T(8,128)(2,1)S(1)} %get-tuple-element.24), channel_id=1, source_target_pairs={{0,8},{4,12},{8,0},{12,4},{16,24},{20,28},{24,16},{28,20},{1,9},{5... | collective-permute-start | bytes 344072 | tf_op jit(solution)/shard_map/ppermute | solution.py:288
  17.3 1.5 %collective-permute-start.4 = (s16[448,128]{1,0:T(8,128)(2,1)S(1)}, s16[448,128]{1,0:T(8,128)(2,1)S(1)}, u32[]{:S(2)}, u32[]{:S(2)}) collective-permute-start(s16[448,128]{1,0:T(8,128)(2,1)S(1)} %get-tuple-element.25), channel_id=1, source_target_pairs={{0,16},{4,20},{8,24},{12,28},{16,0},{20,4},{24,8},{28,12},{1,17},{... | collective-permute-start | bytes 344072 | tf_op jit(solution)/shard_map/ppermute | solution.py:288
  19.3 2.2 %collective-permute-done.3 = s16[448,128]{1,0:T(8,128)(2,1)S(1)} collective-permute-done((s16[448,128]{1,0:T(8,128)(2,1)S(1)}, s16[448,128]{1,0:T(8,128)(2,1)S(1)}, u32[]{:S(2)}, u32[]{:S(2)}) %collective-permute-start.3) | collective-permute-done | bytes 114720 | tf_op jit(solution)/shard_map/ppermute | solution.py:288
  22.7 1.8 %collective-permute-done.5 = s16[448,128]{1,0:T(8,128)(2,1)S(1)} collective-permute-done((s16[448,128]{1,0:T(8,128)(2,1)S(1)}, s16[448,128]{1,0:T(8,128)(2,1)S(1)}, u32[]{:S(2)}, u32[]{:S(2)}) %collective-permute-start.5) | collective-permute-done | bytes 114720 | tf_op jit(solution)/shard_map/ppermute | solution.py:288
  24.6 1.8 %collective-permute-done.6.other = s16[1792,128]{1,0:T(8,128)(2,1)S(1)} collective-permute-done((s16[1792,128]{1,0:T(8,128)(2,1)S(1)}, s16[1792,128]{1,0:T(8,128)(2,1)S(1)}, u32[]{:S(2)}, u32[]{:S(2)}) %collective-permute-start.6) | collective-permute-done | bytes 458784 | tf_op jit(solution)/shard_map/ppermute | solution.py:288
  26.4 2.3 %shard_map.57 = (f32[128,128]{1,0:T(8,128)S(1)}, bf16[128,128]{1,0:T(8,128)(2,1)S(1)}, f32[32,128]{1,0:T(8,128)S(1)}, s16[144,128]{1,0:T(8,128)(2,1)S(1)}) custom-call(s32[2]{0:T(128)S(1)} %pad_add_fusion.2.place, f32[64,2048]{1,0:T(8,128)S(1)} %copy-done.1, bf16[2,256,256]{2,1,0:T(8,128)(2,1)S(1)} %bitcast.11, ...), custom_call_target="tpu_custom_call" | custom-call | flops 500000000 | bytes 1855496 | tf_op jit(solution)/shard_map/pallas_call | solution.py:29
  29.5 3.7 %collective-permute-start.7 = (s16[144,128]{1,0:T(8,128)(2,1)S(1)}, s16[144,128]{1,0:T(8,128)(2,1)S(1)}, u32[]{:S(2)}, u32[]{:S(2)}) collective-permute-start(s16[144,128]{1,0:T(8,128)(2,1)S(1)} %get-tuple-element.30), channel_id=1, source_target_pairs={{0,1},{1,0},{2,3},{3,2},{4,5},{5,4},{6,7},{7,6},{8,9},{9,8},{10,11... | collective-permute-start | bytes 110600 | tf_op jit(solution)/shard_map/ppermute | solution.py:288
  33.2 2.1 %collective-permute-done.7 = s16[144,128]{1,0:T(8,128)(2,1)S(1)} collective-permute-done((s16[144,128]{1,0:T(8,128)(2,1)S(1)}, s16[144,128]{1,0:T(8,128)(2,1)S(1)}, u32[]{:S(2)}, u32[]{:S(2)}) %collective-permute-start.7) | collective-permute-done | bytes 36896 | tf_op jit(solution)/shard_map/ppermute | solution.py:288
  36.5 2.5 %collective-permute-start.12 = (s16[576,128]{1,0:T(8,128)(2,1)S(1)}, s16[576,128]{1,0:T(8,128)(2,1)S(1)}, u32[]{:S(2)}, u32[]{:S(2)}) collective-permute-start(s16[576,128]{1,0:T(8,128)(2,1)S(1)} %get-tuple-element.33), channel_id=1, source_target_pairs={{0,24},{4,28},{8,16},{12,20},{16,8},{20,12},{24,0},{28,4},{1,25},{... | collective-permute-start | bytes 442376 | tf_op jit(solution)/shard_map/ppermute | solution.py:288
  38.9 2.8 %collective-permute-done.10 = s16[576,128]{1,0:T(8,128)(2,1)S(1)} collective-permute-done((s16[576,128]{1,0:T(8,128)(2,1)S(1)}, s16[576,128]{1,0:T(8,128)(2,1)S(1)}, u32[]{:S(2)}, u32[]{:S(2)}) %collective-permute-start.10) | collective-permute-done | bytes 147488 | tf_op jit(solution)/shard_map/ppermute | solution.py:288
  41.7 1.8 %collective-permute-done.11 = s16[576,128]{1,0:T(8,128)(2,1)S(1)} collective-permute-done((s16[576,128]{1,0:T(8,128)(2,1)S(1)}, s16[576,128]{1,0:T(8,128)(2,1)S(1)}, u32[]{:S(2)}, u32[]{:S(2)}) %collective-permute-start.11) | collective-permute-done | bytes 147488 | tf_op jit(solution)/shard_map/ppermute | solution.py:288
  44.1 1.8 %shard_map.60.part = f32[1024,128]{1,0:T(8,128)S(1)} custom-call(s32[2]{0:T(128)S(1)} %pad_add_fusion.2.place, s16[2304,128]{1,0:T(8,128)(2,1)S(1)} %constant_dynamic-update-slice_fusion.8.block), custom_call_target="tpu_custom_call" | custom-call | flops 2000000000 | bytes 1114120 | tf_op jit(solution)/shard_map/pallas_call | solution.py:29
  47.0 2.0 %collective-permute-start.16 = (s16[144,128]{1,0:T(8,128)(2,1)S(1)}, s16[144,128]{1,0:T(8,128)(2,1)S(1)}, u32[]{:S(2)}, u32[]{:S(2)}) collective-permute-start(s16[144,128]{1,0:T(8,128)(2,1)S(1)} %shard_map.59), channel_id=1, source_target_pairs={{0,3},{1,2},{2,1},{3,0},{4,7},{5,6},{6,5},{7,4},{8,11},{9,10},{10,... | collective-permute-start | bytes 110600 | tf_op jit(solution)/shard_map/ppermute | solution.py:288
  50.1 1.3 %collective-permute-start.14 = (s16[144,128]{1,0:T(8,128)(2,1)S(1)}, s16[144,128]{1,0:T(8,128)(2,1)S(1)}, u32[]{:S(2)}, u32[]{:S(2)}) collective-permute-start(s16[144,128]{1,0:T(8,128)(2,1)S(1)} %shard_map.59), channel_id=1, source_target_pairs={{0,1},{1,0},{2,3},{3,2},{4,5},{5,4},{6,7},{7,6},{8,9},{9,8},{10,11... | collective-permute-start | bytes 110600 | tf_op jit(solution)/shard_map/ppermute | solution.py:288
  51.4 1.8 %shard_map.61.image = f32[64,2048]{1,0:T(8,128)S(1)} custom-call(s32[2]{0:T(128)S(1)} %pad_add_fusion.2.place, f32[64,2048]{1,0:T(8,128)S(1)} %copy-done.1, f32[1024,128]{1,0:T(8,128)S(1)} %shard_map.60.part, s16[2304,128]{1,0:T(8,128)(2,1)S(1)} %collective-permute-done.13.block), custom_call_target="tpu_custom_call" | custom-call | flops 2000000000 | bytes 2162696 | tf_op jit(solution)/shard_map/pallas_call | solution.py:29
  54.8 1.7 %collective-permute-start.17 = (s16[576,128]{1,0:T(8,128)(2,1)S(1)}, s16[576,128]{1,0:T(8,128)(2,1)S(1)}, u32[]{:S(2)}, u32[]{:S(2)}) collective-permute-start(s16[576,128]{1,0:T(8,128)(2,1)S(1)} %pad_add_fusion), channel_id=1, source_target_pairs={{0,8},{4,12},{8,0},{12,4},{16,24},{20,28},{24,16},{28,20},{1,9},{5... | collective-permute-start | bytes 442376 | tf_op jit(solution)/shard_map/ppermute | solution.py:288
  58.4 3.3 %collective-permute-done.17 = s16[576,128]{1,0:T(8,128)(2,1)S(1)} collective-permute-done((s16[576,128]{1,0:T(8,128)(2,1)S(1)}, s16[576,128]{1,0:T(8,128)(2,1)S(1)}, u32[]{:S(2)}, u32[]{:S(2)}) %collective-permute-start.17) | collective-permute-done | bytes 147488 | tf_op jit(solution)/shard_map/ppermute | solution.py:288
  61.7 3.9 %collective-permute-done.18 = s16[576,128]{1,0:T(8,128)(2,1)S(1)} collective-permute-done((s16[576,128]{1,0:T(8,128)(2,1)S(1)}, s16[576,128]{1,0:T(8,128)(2,1)S(1)}, u32[]{:S(2)}, u32[]{:S(2)}) %collective-permute-start.18) | collective-permute-done | bytes 147488 | tf_op jit(solution)/shard_map/ppermute | solution.py:288
  65.7 1.8 %shard_map.62.part = f32[1024,128]{1,0:T(8,128)S(1)} custom-call(s32[2]{0:T(128)S(1)} %pad_add_fusion.2.place, s16[2304,128]{1,0:T(8,128)(2,1)S(1)} %constant_dynamic-update-slice_fusion.15.block), custom_call_target="tpu_custom_call" | custom-call | flops 2000000000 | bytes 1114120 | tf_op jit(solution)/shard_map/pallas_call | solution.py:29
  67.7 2.6 %shard_map.63 = f32[64,2048]{1,0:T(8,128)} custom-call(s32[2]{0:T(128)S(1)} %pad_add_fusion.2.place, f32[64,2048]{1,0:T(8,128)S(1)} %shard_map.61.image, f32[1024,128]{1,0:T(8,128)S(1)} %shard_map.62.part, s16[2304,128]{1,0:T(8,128)(2,1)S(1)} %collective-permute-done.20.block), custom_call_target="tpu_custom_call" | custom-call | flops 2000000000 | bytes 2162696 | tf_op jit(solution)/shard_map/pallas_call | solution.py:29
  (58 shorter events, 14.4 us)
Async XLA Ops:
  2.2 1.0 %copy-start = (f32[64,2048]{1,0:T(8,128)S(1)}, f32[64,2048]{1,0:T(8,128)}, u32[]{:S(2)}) copy-start(f32[64,2048]{1,0:T(8,128)} %image.5) | copy-start | bytes 1572868
  4.1 5.7 %collective-permute-start = (s16[192,128]{1,0:T(8,128)(2,1)S(1)}, s16[192,128]{1,0:T(8,128)(2,1)S(1)}, u32[]{:S(2)}, u32[]{:S(2)}) collective-permute-start(s16[192,128]{1,0:T(8,128)(2,1)S(1)} %get-tuple-element.20), channel_id=1, source_target_pairs={{0,1},{1,0},{2,3},{3,2},{4,5},{5,4},{6,7},{7,6},{8,9},{9,8},{10,11... | collective-permute-start | bytes 147464 | tf_op jit(solution)/shard_map/ppermute | solution.py:288
  7.2 5.9 %collective-permute-start.1 = (s16[192,128]{1,0:T(8,128)(2,1)S(1)}, s16[192,128]{1,0:T(8,128)(2,1)S(1)}, u32[]{:S(2)}, u32[]{:S(2)}) collective-permute-start(s16[192,128]{1,0:T(8,128)(2,1)S(1)} %get-tuple-element.21), channel_id=1, source_target_pairs={{0,2},{1,3},{2,0},{3,1},{4,6},{5,7},{6,4},{7,5},{8,10},{9,11},{10,... | collective-permute-start | bytes 147464 | tf_op jit(solution)/shard_map/ppermute | solution.py:288
  9.8 5.9 %collective-permute-start.2 = (s16[192,128]{1,0:T(8,128)(2,1)S(1)}, s16[192,128]{1,0:T(8,128)(2,1)S(1)}, u32[]{:S(2)}, u32[]{:S(2)}) collective-permute-start(s16[192,128]{1,0:T(8,128)(2,1)S(1)} %get-tuple-element.22), channel_id=1, source_target_pairs={{0,3},{1,2},{2,1},{3,0},{4,7},{5,6},{6,5},{7,4},{8,11},{9,10},{10,... | collective-permute-start | bytes 147464 | tf_op jit(solution)/shard_map/ppermute | solution.py:288
  15.6 10.7 %copy-start.1 = (f32[64,2048]{1,0:T(8,128)S(1)}, f32[64,2048]{1,0:T(8,128)}, u32[]{:S(2)}) copy-start(f32[64,2048]{1,0:T(8,128)} %image.5) | copy-start | bytes 1572868
  15.7 5.7 %collective-permute-start.3 = (s16[448,128]{1,0:T(8,128)(2,1)S(1)}, s16[448,128]{1,0:T(8,128)(2,1)S(1)}, u32[]{:S(2)}, u32[]{:S(2)}) collective-permute-start(s16[448,128]{1,0:T(8,128)(2,1)S(1)} %get-tuple-element.24), channel_id=1, source_target_pairs={{0,8},{4,12},{8,0},{12,4},{16,24},{20,28},{24,16},{28,20},{1,9},{5... | collective-permute-start | bytes 344072 | tf_op jit(solution)/shard_map/ppermute | solution.py:288
  17.3 5.4 %collective-permute-start.4 = (s16[448,128]{1,0:T(8,128)(2,1)S(1)}, s16[448,128]{1,0:T(8,128)(2,1)S(1)}, u32[]{:S(2)}, u32[]{:S(2)}) collective-permute-start(s16[448,128]{1,0:T(8,128)(2,1)S(1)} %get-tuple-element.25), channel_id=1, source_target_pairs={{0,16},{4,20},{8,24},{12,28},{16,0},{20,4},{24,8},{28,12},{1,17},{... | collective-permute-start | bytes 344072 | tf_op jit(solution)/shard_map/ppermute | solution.py:288
  18.8 5.7 %collective-permute-start.5 = (s16[448,128]{1,0:T(8,128)(2,1)S(1)}, s16[448,128]{1,0:T(8,128)(2,1)S(1)}, u32[]{:S(2)}, u32[]{:S(2)}) collective-permute-start(s16[448,128]{1,0:T(8,128)(2,1)S(1)} %get-tuple-element.26), channel_id=1, source_target_pairs={{0,24},{4,28},{8,16},{12,20},{16,8},{20,12},{24,0},{28,4},{1,25},{... | collective-permute-start | bytes 344072 | tf_op jit(solution)/shard_map/ppermute | solution.py:288
  21.5 4.9 %copy-start.2 = (bf16[2,1,256,256]{3,2,1,0:T(8,128)(2,1)S(1)}, bf16[2,1,256,256]{3,2,1,0:T(8,128)(2,1)}, u32[]{:S(2)}) copy-start(bf16[2,1,256,256]{3,2,1,0:T(8,128)(2,1)} %param.9) | copy-start | bytes 786436
  24.5 1.9 %collective-permute-start.6 = (s16[1792,128]{1,0:T(8,128)(2,1)S(1)}, s16[1792,128]{1,0:T(8,128)(2,1)S(1)}, u32[]{:S(2)}, u32[]{:S(2)}) collective-permute-start(s16[1792,128]{1,0:T(8,128)(2,1)S(1)} %constant_dynamic-update-slice_fusion.mine), channel_id=1, source_target_pairs={{0,4},{4,0},{8,12},{12,8},{16,20},{20,16},{24,28},{28,24},{1,5},{5... | collective-permute-start | bytes 1376264 | tf_op jit(solution)/shard_map/ppermute | solution.py:288
  28.7 6.6 %collective-permute-start.9 = (s16[144,128]{1,0:T(8,128)(2,1)S(1)}, s16[144,128]{1,0:T(8,128)(2,1)S(1)}, u32[]{:S(2)}, u32[]{:S(2)}) collective-permute-start(s16[144,128]{1,0:T(8,128)(2,1)S(1)} %get-tuple-element.30), channel_id=1, source_target_pairs={{0,3},{1,2},{2,1},{3,0},{4,7},{5,6},{6,5},{7,4},{8,11},{9,10},{10,... | collective-permute-start | bytes 110600 | tf_op jit(solution)/shard_map/ppermute | solution.py:288
  29.5 5.8 %collective-permute-start.8 = (s16[144,128]{1,0:T(8,128)(2,1)S(1)}, s16[144,128]{1,0:T(8,128)(2,1)S(1)}, u32[]{:S(2)}, u32[]{:S(2)}) collective-permute-start(s16[144,128]{1,0:T(8,128)(2,1)S(1)} %get-tuple-element.30), channel_id=1, source_target_pairs={{0,2},{1,3},{2,0},{3,1},{4,6},{5,7},{6,4},{7,5},{8,10},{9,11},{10,... | collective-permute-start | bytes 110600 | tf_op jit(solution)/shard_map/ppermute | solution.py:288
  29.5 5.8 %collective-permute-start.7 = (s16[144,128]{1,0:T(8,128)(2,1)S(1)}, s16[144,128]{1,0:T(8,128)(2,1)S(1)}, u32[]{:S(2)}, u32[]{:S(2)}) collective-permute-start(s16[144,128]{1,0:T(8,128)(2,1)S(1)} %get-tuple-element.30), channel_id=1, source_target_pairs={{0,1},{1,0},{2,3},{3,2},{4,5},{5,4},{6,7},{7,6},{8,9},{9,8},{10,11... | collective-permute-start | bytes 110600 | tf_op jit(solution)/shard_map/ppermute | solution.py:288
  35.4 6.3 %collective-permute-start.10 = (s16[576,128]{1,0:T(8,128)(2,1)S(1)}, s16[576,128]{1,0:T(8,128)(2,1)S(1)}, u32[]{:S(2)}, u32[]{:S(2)}) collective-permute-start(s16[576,128]{1,0:T(8,128)(2,1)S(1)} %get-tuple-element.33), channel_id=1, source_target_pairs={{0,8},{4,12},{8,0},{12,4},{16,24},{20,28},{24,16},{28,20},{1,9},{5... | collective-permute-start | bytes 442376 | tf_op jit(solution)/shard_map/ppermute | solution.py:288
  35.9 7.6 %collective-permute-start.11 = (s16[576,128]{1,0:T(8,128)(2,1)S(1)}, s16[576,128]{1,0:T(8,128)(2,1)S(1)}, u32[]{:S(2)}, u32[]{:S(2)}) collective-permute-start(s16[576,128]{1,0:T(8,128)(2,1)S(1)} %get-tuple-element.33), channel_id=1, source_target_pairs={{0,16},{4,20},{8,24},{12,28},{16,0},{20,4},{24,8},{28,12},{1,17},{... | collective-permute-start | bytes 442376 | tf_op jit(solution)/shard_map/ppermute | solution.py:288
  36.5 7.1 %collective-permute-start.12 = (s16[576,128]{1,0:T(8,128)(2,1)S(1)}, s16[576,128]{1,0:T(8,128)(2,1)S(1)}, u32[]{:S(2)}, u32[]{:S(2)}) collective-permute-start(s16[576,128]{1,0:T(8,128)(2,1)S(1)} %get-tuple-element.33), channel_id=1, source_target_pairs={{0,24},{4,28},{8,16},{12,20},{16,8},{20,12},{24,0},{28,4},{1,25},{... | collective-permute-start | bytes 442376 | tf_op jit(solution)/shard_map/ppermute | solution.py:288
  43.6 2.4 %collective-permute-start.13 = (s16[2304,128]{1,0:T(8,128)(2,1)S(1)}, s16[2304,128]{1,0:T(8,128)(2,1)S(1)}, u32[]{:S(2)}, u32[]{:S(2)}) collective-permute-start(s16[2304,128]{1,0:T(8,128)(2,1)S(1)} %constant_dynamic-update-slice_fusion.8.block), channel_id=1, source_target_pairs={{0,4},{4,0},{8,12},{12,8},{16,20},{20,16},{24,28},{28,24},{1,5},{5... | collective-permute-start | bytes 1769480 | tf_op jit(solution)/shard_map/ppermute | solution.py:288
  47.0 6.3 %collective-permute-start.16 = (s16[144,128]{1,0:T(8,128)(2,1)S(1)}, s16[144,128]{1,0:T(8,128)(2,1)S(1)}, u32[]{:S(2)}, u32[]{:S(2)}) collective-permute-start(s16[144,128]{1,0:T(8,128)(2,1)S(1)} %shard_map.59), channel_id=1, source_target_pairs={{0,3},{1,2},{2,1},{3,0},{4,7},{5,6},{6,5},{7,4},{8,11},{9,10},{10,... | collective-permute-start | bytes 110600 | tf_op jit(solution)/shard_map/ppermute | solution.py:288
  49.0 5.5 %collective-permute-start.15 = (s16[144,128]{1,0:T(8,128)(2,1)S(1)}, s16[144,128]{1,0:T(8,128)(2,1)S(1)}, u32[]{:S(2)}, u32[]{:S(2)}) collective-permute-start(s16[144,128]{1,0:T(8,128)(2,1)S(1)} %shard_map.59), channel_id=1, source_target_pairs={{0,2},{1,3},{2,0},{3,1},{4,6},{5,7},{6,4},{7,5},{8,10},{9,11},{10,... | collective-permute-start | bytes 110600 | tf_op jit(solution)/shard_map/ppermute | solution.py:288
  50.1 4.7 %collective-permute-start.14 = (s16[144,128]{1,0:T(8,128)(2,1)S(1)}, s16[144,128]{1,0:T(8,128)(2,1)S(1)}, u32[]{:S(2)}, u32[]{:S(2)}) collective-permute-start(s16[144,128]{1,0:T(8,128)(2,1)S(1)} %shard_map.59), channel_id=1, source_target_pairs={{0,1},{1,0},{2,3},{3,2},{4,5},{5,4},{6,7},{7,6},{8,9},{9,8},{10,11... | collective-permute-start | bytes 110600 | tf_op jit(solution)/shard_map/ppermute | solution.py:288
  54.8 6.8 %collective-permute-start.17 = (s16[576,128]{1,0:T(8,128)(2,1)S(1)}, s16[576,128]{1,0:T(8,128)(2,1)S(1)}, u32[]{:S(2)}, u32[]{:S(2)}) collective-permute-start(s16[576,128]{1,0:T(8,128)(2,1)S(1)} %pad_add_fusion), channel_id=1, source_target_pairs={{0,8},{4,12},{8,0},{12,4},{16,24},{20,28},{24,16},{28,20},{1,9},{5... | collective-permute-start | bytes 442376 | tf_op jit(solution)/shard_map/ppermute | solution.py:288
  56.6 9.0 %collective-permute-start.19 = (s16[576,128]{1,0:T(8,128)(2,1)S(1)}, s16[576,128]{1,0:T(8,128)(2,1)S(1)}, u32[]{:S(2)}, u32[]{:S(2)}) collective-permute-start(s16[576,128]{1,0:T(8,128)(2,1)S(1)} %pad_add_fusion), channel_id=1, source_target_pairs={{0,24},{4,28},{8,16},{12,20},{16,8},{20,12},{24,0},{28,4},{1,25},{... | collective-permute-start | bytes 442376 | tf_op jit(solution)/shard_map/ppermute | solution.py:288
  57.5 8.0 %collective-permute-start.18 = (s16[576,128]{1,0:T(8,128)(2,1)S(1)}, s16[576,128]{1,0:T(8,128)(2,1)S(1)}, u32[]{:S(2)}, u32[]{:S(2)}) collective-permute-start(s16[576,128]{1,0:T(8,128)(2,1)S(1)} %pad_add_fusion), channel_id=1, source_target_pairs={{0,16},{4,20},{8,24},{12,28},{16,0},{20,4},{24,8},{28,12},{1,17},{... | collective-permute-start | bytes 442376 | tf_op jit(solution)/shard_map/ppermute | solution.py:288
  65.7 2.1 %collective-permute-start.20 = (s16[2304,128]{1,0:T(8,128)(2,1)S(1)}, s16[2304,128]{1,0:T(8,128)(2,1)S(1)}, u32[]{:S(2)}, u32[]{:S(2)}) collective-permute-start(s16[2304,128]{1,0:T(8,128)(2,1)S(1)} %constant_dynamic-update-slice_fusion.15.block), channel_id=1, source_target_pairs={{0,4},{4,0},{8,12},{12,8},{16,20},{20,16},{24,28},{28,24},{1,5},{5... | collective-permute-start | bytes 1769480 | tf_op jit(solution)/shard_map/ppermute | solution.py:288
  (2 other events, 1.4 us)

commit v3 on v2

--- a/solution.py
+++ b/solution.py
@@ -22,15 +22,20 @@
 VMEM_LIMIT = 48 * 1024 * 1024
 
 
-def call(kernel, outs, args, flops, smem=0):
+def call(kernel, outs, args, flops, smem=0, hbm=0, scratch=()):
     spaces = [pl.BlockSpec(memory_space=pltpu.SMEM)] * smem
-    spaces += [pl.BlockSpec(memory_space=pltpu.VMEM)] * (len(args) - smem)
+    spaces += [pl.BlockSpec(memory_space=pltpu.HBM)] * hbm
+    spaces += [pl.BlockSpec(memory_space=pltpu.VMEM)] * (len(args) - smem - hbm)
     moved = sum(a.size * a.dtype.itemsize for a in list(args) + list(outs))
+    args = list(args)
+    for i in range(smem, smem + hbm):
+        args[i] = pltpu.with_memory_space_constraint(args[i], pltpu.HBM)
     return pl.pallas_call(
         kernel,
         out_shape=list(outs),
         in_specs=spaces,
         out_specs=[pl.BlockSpec(memory_space=pltpu.VMEM)] * len(outs),
+        scratch_shapes=list(scratch),
         compiler_params=pltpu.CompilerParams(vmem_limit_bytes=VMEM_LIMIT),
         cost_estimate=pl.CostEstimate(flops=flops, bytes_accessed=moved, transcendentals=0),
     )(*args)
@@ -92,38 +97,56 @@
     return n.bit_length() - 1
 
 
-def pack_kernel(C, F, L, place, image, seen, numbers, *outs):
+def pack_kernel(C, F, L, place, image, seen, terms, counts, *refs):
+    outs, (band_in, seen_in, terms_in, counts_in, row_in, sems) = refs[:F], refs[F:]
     c, f = place[0], place[1]
     height, width = image.shape
     band = height // C
     wide = width // STRIP
     per_facet = height * wide
     piece = per_facet // C
-    strips = tiled_strips(image[pl.ds(pl.multiple_of(c * band, TILE), band), :])
-    share = (jnp.round(strips * LEVELS) - 32768.0).astype(I32).astype(I16)
+    mine = image.at[pl.ds(pl.multiple_of(c * band, TILE), band), :]
+    copies = [
+        pltpu.make_async_copy(source, target, sems.at[i])
+        for i, (source, target) in enumerate(
+            ((mine, band_in), (seen, seen_in), (terms, terms_in), (counts, counts_in))
+        )
+    ]
+    for copy in copies:
+        copy.start()
     chips = C // 2
     size = chips * BLOCK
     rows = F * size
     row = iota((rows, 1), 0)
     k, j, i = row // size, (row // BLOCK) % chips, row % BLOCK
-    uv = k ^ f
     channel = ((c >> 1) ^ j) * (2 * L) + (i >> 1)
-    raw = numbers[...]
+    is_seen = i < 4 * L
+    pick = is_seen & (iota((rows, L * C * F), 1) == channel * F + (k ^ f))
+    row_in[...] = jnp.zeros(row_in.shape, I32)
+    for copy in copies:
+        copy.wait()
+    strips = tiled_strips(band_in[...])
+    share = (jnp.round(strips * LEVELS) - 32768.0).astype(I32).astype(I16)
+    raw = terms_in[...]
     across, column = raw >> log2(F * wide), raw & (F * wide - 1)
-    strip = (
+    terms_in[...] = (
         (column >> log2(wide)) * per_facet
         + (across >> 3) * (wide * TILE)
         + (column & (wide - 1)) * TILE
         + (across & 7)
     )
-    ids = jnp.where(iota(raw.shape, 0) < TERMS * F, strip, raw)
-    is_seen = i < 4 * L
-    pick = is_seen & (iota((rows, seen.shape[0]), 1) == channel * F + uv)
-    both = jnp.dot(one_hot(pick), seen[...], preferred_element_type=F32)
+    for at in range(F):
+        for term in range(TERMS):
+            row_in[at * TILE + term : at * TILE + term + 1, : L * C] = terms_in[at ^ f, term : term + 1]
+        row_in[at * TILE + TERMS : at * TILE + TERMS + 1, : L * C] = counts_in[pl.ds(at ^ f, 1)]
+    by_channel = jnp.concatenate([seen_in[n] for n in range(L * C)], axis=0)
+    both = jnp.dot(one_hot(pick), by_channel, preferred_element_type=F32)
     values = code_floats(jnp.where((i & 1) == 0, both[:, :VISB], both[:, VISB:]))
-    pick = (i >= 4 * L) & (iota((rows, raw.shape[0]), 1) == (i - 4 * L) * F + uv)
-    whole = joined(jnp.dot(one_hot(pick), halves(ids), preferred_element_type=F32))
-    blocks = jnp.where(is_seen, values, whole.astype(I32)).astype(I16)
+    whole = jnp.concatenate(
+        [part for at in range(F) for part in [row_in[at * TILE : (at + 1) * TILE]] * (2 * chips)],
+        axis=0,
+    )
+    blocks = jnp.where(is_seen, values, whole).astype(I16)
     for at in range(F):
         if at:
             outs[at][:piece] = share
@@ -133,7 +156,7 @@
 
 
 def pass_kernel(F, piece, *refs):
-    got, outs = refs[:F], refs[F:]
+    got, outs = refs[:F][::-1], refs[F:]
     for j, out in enumerate(outs):
         for k in range(1, F):
             out[(k - 1) * piece : k * piece] = got[k][:piece]
@@ -299,25 +322,35 @@
     place = jnp.stack([lax.axis_index("chan"), lax.axis_index("facet")]).astype(I32)
     kernels = uv_kernels[:, 0]
 
-    numbers = jnp.concatenate(
-        [strip_index[0].transpose(2, 1, 0).reshape(TERMS * F, L * C), live_counts[0].T], axis=0
-    )
-    numbers = jnp.pad(numbers, ((0, 16 - numbers.shape[0]), (0, STRIP - numbers.shape[1])))
-    seen = visibilities.reshape(L * C * F, 2 * VISB)
     blocks = jax.ShapeDtypeStruct((chips * BLOCK, STRIP), I16)
     both = jax.ShapeDtypeStruct((piece + chips * BLOCK, STRIP), I16)
     packed = call(
         functools.partial(pack_kernel, C, F, L),
         [blocks] + [both] * (F - 1),
-        [place, start_image, seen, numbers],
+        [
+            place,
+            start_image,
+            visibilities[0],
+            strip_index[0].transpose(1, 2, 0),
+            live_counts[0].T,
+        ],
         10**8,
         smem=1,
-    )
-    got = [packed[0]] + [swap(packed[k], "facet", k) for k in range(1, F)]
+        hbm=4,
+        scratch=[
+            pltpu.VMEM((start_image.shape[0] // C, start_image.shape[1]), F32),
+            pltpu.VMEM(visibilities.shape[1:], BF16),
+            pltpu.VMEM((F, TERMS, L * C), I32),
+            pltpu.VMEM((F, L * C), I32),
+            pltpu.VMEM((F * TILE, STRIP), I32),
+            pltpu.SemaphoreType.DMA((4,)),
+        ],
+    )
+    got = [packed[0]] + [swap(packed[k], "facet", k) for k in range(F - 1, 0, -1)][::-1]
     passed = call(
         functools.partial(pass_kernel, F, piece),
         [jax.ShapeDtypeStruct(((F - 1) * piece + F * BLOCK, STRIP), I16)] * chips,
-        got,
+        got[::-1],
         10**6,
     )
     mine = jnp.concatenate(
@@ -349,7 +382,7 @@
         if held is not None:
             image = settle(step, place, image, *held)
             near, image = lax.optimization_barrier((near, image))
-        mine = jnp.concatenate([near] + [swap(near, "chan", 2 * j) for j in range(1, chips)], axis=0)
+        mine = jnp.concatenate([near] + [swap(near, "chan", 2 * j) for j in range(chips - 1, 0, -1)], axis=0)
         other = swap(mine, "chan", 1)
         if not last:
             (part,) = call(
@@ -423,7 +456,7 @@
         and F >= 2
         and C * F * L * TERMS == STRIP
         and 4 * L + TERMS + 1 <= BLOCK
-        and (TERMS + 1) * F <= 16
+        and 4 * L == TILE
         and L * C <= STRIP
         and strips <= 64 * 256
         and strips & (strips - 1) == 0

time: 70.6 us -> 66.7 us (0.945)
  local copies, waits for them, and re-layouts: 3.44 us -> 0.25 us
  waiting for transfers between devices: 28.4 us -> 26.9 us
  Pallas kernels: 12.7 us -> 13.6 us
    unnamed x22 -> x15, local copies, waits for them, and re-layouts: 2.58 us -> 0.18 us
    ppermute x21, waiting for transfers between devices: 28.4 us -> 26.9 us  [swap(): lax.ppermute(x, axis, [(i, i ^ k) for i in range(lax.axis_size(axis))])]
    pallas_call x9, Pallas kernels: 12.7 us -> 13.6 us  [call(): pl.pallas_call(kernel, out_shape=list(outs), in_specs=spaces, out_specs=[...]
    reshape x1 -> x0, local copies, waits for them, and re-layouts: 0.77 us -> none  [sparse_device(): seen = visibilities.reshape(L * C * F, 2 * VISB)]
  transfers between devices with their start and end apart: 21 -> 21, of which waited for: 14 -> 14; matrix products, arithmetic and copies ran while one was open for 0% -> 0% of each run, Pallas kernels for 8% -> 9%
where the time goes in v3:
time: 66.7 us; the launch traced here: 66.6 us
  waiting for transfers between devices  26.9 us (40%)
  starting transfers between devices  25.5 us (38%)
  Pallas kernels  13.6 us (20%)
    ppermute x21, waiting for transfers between devices, swap(): lax.ppermute(x, axis, [(i, i ^ k) for i in range(lax.axis_size(axis))])  26.9 us
    ppermute x21, starting transfers between devices, swap(): lax.ppermute(x, axis, [(i, i ^ k) for i in range(lax.axis_size(axis))])  25.5 us
    pallas_call x9, Pallas kernels, call(): pl.pallas_call(kernel, out_shape=list(outs), in_specs=spaces, out_specs=[...  13.6 us
  transfers between devices with their start and end apart: 21, of which 14 were waited for; matrix products, arithmetic and copies ran while one was open for 0% of the time, Pallas kernels for 9%

profile of v3, /device:TPU:0, one launch (start us, length us, event | category | flops | bytes accessed | tf_op | source)
XLA Modules:
  0.0 66.6 jit_solution(11670704920063866562)
XLA Ops:
  0.1 1.6 %shard_map.55 = (s16[64,128]{1,0:T(8,128)(2,1)S(1)}, s16[192,128]{1,0:T(8,128)(2,1)S(1)}, s16[192,128]{1,0:T(8,128)(2,1)S(1)}, s16[192,128]{1,0:T(8,128)(2,1)S(1)}) custom-call(s32[2]{0:T(128)S(1)} %pad_add_fusion.1.place, f32[64,2048]{1,0:T(8,128)} %image.5, bf16[16,4,256]{2,1,0:T(4,128)(2,1)} %bitcast.12, s32[4,2,16]{2,1,0:T(2,128)} %bitcast.13, ...), custom_call_target="tpu_custom_call" | custom-call | flops 100000000 | bytes 721672 | tf_op jit(solution)/shard_map/pallas_call | solution.py:33
  1.7 5.1 %collective-permute-start = (s16[192,128]{1,0:T(8,128)(2,1)S(1)}, s16[192,128]{1,0:T(8,128)(2,1)S(1)}, u32[]{:S(2)}, u32[]{:S(2)}) collective-permute-start(s16[192,128]{1,0:T(8,128)(2,1)S(1)} %get-tuple-element.19), channel_id=1, source_target_pairs={{0,3},{1,2},{2,1},{3,0},{4,7},{5,6},{6,5},{7,4},{8,11},{9,10},{10,... | collective-permute-start | bytes 147464 | tf_op jit(solution)/shard_map/ppermute | solution.py:311
  7.5 1.6 %collective-permute-done.refs_0_ = s16[192,128]{1,0:T(8,128)(2,1)S(1)} collective-permute-done((s16[192,128]{1,0:T(8,128)(2,1)S(1)}, s16[192,128]{1,0:T(8,128)(2,1)S(1)}, u32[]{:S(2)}, u32[]{:S(2)}) %collective-permute-start) | collective-permute-done | bytes 49184 | tf_op jit(solution)/shard_map/ppermute | solution.py:311
  9.1 2.8 %collective-permute-done.1.refs_1_ = s16[192,128]{1,0:T(8,128)(2,1)S(1)} collective-permute-done((s16[192,128]{1,0:T(8,128)(2,1)S(1)}, s16[192,128]{1,0:T(8,128)(2,1)S(1)}, u32[]{:S(2)}, u32[]{:S(2)}) %collective-permute-start.1) | collective-permute-done | bytes 49184 | tf_op jit(solution)/shard_map/ppermute | solution.py:311
  11.9 1.6 %collective-permute-start.3 = (s16[448,128]{1,0:T(8,128)(2,1)S(1)}, s16[448,128]{1,0:T(8,128)(2,1)S(1)}, u32[]{:S(2)}, u32[]{:S(2)}) collective-permute-start(s16[448,128]{1,0:T(8,128)(2,1)S(1)} %get-tuple-element.24), channel_id=1, source_target_pairs={{0,8},{4,12},{8,0},{12,4},{16,24},{20,28},{24,16},{28,20},{1,9},{5... | collective-permute-start | bytes 344072 | tf_op jit(solution)/shard_map/ppermute | solution.py:311
  13.5 1.5 %collective-permute-start.4 = (s16[448,128]{1,0:T(8,128)(2,1)S(1)}, s16[448,128]{1,0:T(8,128)(2,1)S(1)}, u32[]{:S(2)}, u32[]{:S(2)}) collective-permute-start(s16[448,128]{1,0:T(8,128)(2,1)S(1)} %get-tuple-element.25), channel_id=1, source_target_pairs={{0,16},{4,20},{8,24},{12,28},{16,0},{20,4},{24,8},{28,12},{1,17},{... | collective-permute-start | bytes 344072 | tf_op jit(solution)/shard_map/ppermute | solution.py:311
  15.5 2.2 %collective-permute-done.3 = s16[448,128]{1,0:T(8,128)(2,1)S(1)} collective-permute-done((s16[448,128]{1,0:T(8,128)(2,1)S(1)}, s16[448,128]{1,0:T(8,128)(2,1)S(1)}, u32[]{:S(2)}, u32[]{:S(2)}) %collective-permute-start.3) | collective-permute-done | bytes 114720 | tf_op jit(solution)/shard_map/ppermute | solution.py:311
  17.7 1.6 %collective-permute-done.4 = s16[448,128]{1,0:T(8,128)(2,1)S(1)} collective-permute-done((s16[448,128]{1,0:T(8,128)(2,1)S(1)}, s16[448,128]{1,0:T(8,128)(2,1)S(1)}, u32[]{:S(2)}, u32[]{:S(2)}) %collective-permute-start.4) | collective-permute-done | bytes 114720 | tf_op jit(solution)/shard_map/ppermute | solution.py:311
  20.8 1.8 %collective-permute-done.6.other = s16[1792,128]{1,0:T(8,128)(2,1)S(1)} collective-permute-done((s16[1792,128]{1,0:T(8,128)(2,1)S(1)}, s16[1792,128]{1,0:T(8,128)(2,1)S(1)}, u32[]{:S(2)}, u32[]{:S(2)}) %collective-permute-start.6) | collective-permute-done | bytes 458784 | tf_op jit(solution)/shard_map/ppermute | solution.py:311
  22.6 2.3 %shard_map.57 = (f32[128,128]{1,0:T(8,128)S(1)}, bf16[128,128]{1,0:T(8,128)(2,1)S(1)}, f32[32,128]{1,0:T(8,128)S(1)}, s16[144,128]{1,0:T(8,128)(2,1)S(1)}) custom-call(s32[2]{0:T(128)S(1)} %pad_add_fusion.1.place, f32[64,2048]{1,0:T(8,128)S(1)} %copy-done, bf16[2,256,256]{2,1,0:T(8,128)(2,1)S(1)} %bitcast.10, ...), custom_call_target="tpu_custom_call" | custom-call | flops 500000000 | bytes 1855496 | tf_op jit(solution)/shard_map/pallas_call | solution.py:33
  24.9 2.2 %collective-permute-start.9 = (s16[144,128]{1,0:T(8,128)(2,1)S(1)}, s16[144,128]{1,0:T(8,128)(2,1)S(1)}, u32[]{:S(2)}, u32[]{:S(2)}) collective-permute-start(s16[144,128]{1,0:T(8,128)(2,1)S(1)} %get-tuple-element.30), channel_id=1, source_target_pairs={{0,3},{1,2},{2,1},{3,0},{4,7},{5,6},{6,5},{7,4},{8,11},{9,10},{10,... | collective-permute-start | bytes 110600 | tf_op jit(solution)/shard_map/ppermute | solution.py:311
  27.1 2.3 %collective-permute-start.7 = (s16[144,128]{1,0:T(8,128)(2,1)S(1)}, s16[144,128]{1,0:T(8,128)(2,1)S(1)}, u32[]{:S(2)}, u32[]{:S(2)}) collective-permute-start(s16[144,128]{1,0:T(8,128)(2,1)S(1)} %get-tuple-element.30), channel_id=1, source_target_pairs={{0,1},{1,0},{2,3},{3,2},{4,5},{5,4},{6,7},{7,6},{8,9},{9,8},{10,11... | collective-permute-start | bytes 110600 | tf_op jit(solution)/shard_map/ppermute | solution.py:311
  29.4 2.5 %collective-permute-done.7 = s16[144,128]{1,0:T(8,128)(2,1)S(1)} collective-permute-done((s16[144,128]{1,0:T(8,128)(2,1)S(1)}, s16[144,128]{1,0:T(8,128)(2,1)S(1)}, u32[]{:S(2)}, u32[]{:S(2)}) %collective-permute-start.7) | collective-permute-done | bytes 36896 | tf_op jit(solution)/shard_map/ppermute | solution.py:311
  32.9 1.5 %collective-permute-start.11 = (s16[576,128]{1,0:T(8,128)(2,1)S(1)}, s16[576,128]{1,0:T(8,128)(2,1)S(1)}, u32[]{:S(2)}, u32[]{:S(2)}) collective-permute-start(s16[576,128]{1,0:T(8,128)(2,1)S(1)} %get-tuple-element.33), channel_id=1, source_target_pairs={{0,16},{4,20},{8,24},{12,28},{16,0},{20,4},{24,8},{28,12},{1,17},{... | collective-permute-start | bytes 442376 | tf_op jit(solution)/shard_map/ppermute | solution.py:311
  35.9 4.2 %collective-permute-done.10 = s16[576,128]{1,0:T(8,128)(2,1)S(1)} collective-permute-done((s16[576,128]{1,0:T(8,128)(2,1)S(1)}, s16[576,128]{1,0:T(8,128)(2,1)S(1)}, u32[]{:S(2)}, u32[]{:S(2)}) %collective-permute-start.10) | collective-permute-done | bytes 147488 | tf_op jit(solution)/shard_map/ppermute | solution.py:311
  41.8 1.8 %shard_map.60.part = f32[1024,128]{1,0:T(8,128)S(1)} custom-call(s32[2]{0:T(128)S(1)} %pad_add_fusion.1.place, s16[2304,128]{1,0:T(8,128)(2,1)S(1)} %constant_dynamic-update-slice_fusion.8.block), custom_call_target="tpu_custom_call" | custom-call | flops 2000000000 | bytes 1114120 | tf_op jit(solution)/shard_map/pallas_call | solution.py:33
  44.7 2.3 %collective-permute-start.16 = (s16[144,128]{1,0:T(8,128)(2,1)S(1)}, s16[144,128]{1,0:T(8,128)(2,1)S(1)}, u32[]{:S(2)}, u32[]{:S(2)}) collective-permute-start(s16[144,128]{1,0:T(8,128)(2,1)S(1)} %shard_map.59), channel_id=1, source_target_pairs={{0,3},{1,2},{2,1},{3,0},{4,7},{5,6},{6,5},{7,4},{8,11},{9,10},{10,... | collective-permute-start | bytes 110600 | tf_op jit(solution)/shard_map/ppermute | solution.py:311
  46.9 2.2 %collective-permute-start.14 = (s16[144,128]{1,0:T(8,128)(2,1)S(1)}, s16[144,128]{1,0:T(8,128)(2,1)S(1)}, u32[]{:S(2)}, u32[]{:S(2)}) collective-permute-start(s16[144,128]{1,0:T(8,128)(2,1)S(1)} %shard_map.59), channel_id=1, source_target_pairs={{0,1},{1,0},{2,3},{3,2},{4,5},{5,4},{6,7},{7,6},{8,9},{9,8},{10,11... | collective-permute-start | bytes 110600 | tf_op jit(solution)/shard_map/ppermute | solution.py:311
  49.1 1.8 %shard_map.61.image = f32[64,2048]{1,0:T(8,128)S(1)} custom-call(s32[2]{0:T(128)S(1)} %pad_add_fusion.1.place, f32[64,2048]{1,0:T(8,128)S(1)} %copy-done, f32[1024,128]{1,0:T(8,128)S(1)} %shard_map.60.part, s16[2304,128]{1,0:T(8,128)(2,1)S(1)} %collective-permute-done.13.block), custom_call_target="tpu_custom_call" | custom-call | flops 2000000000 | bytes 2162696 | tf_op jit(solution)/shard_map/pallas_call | solution.py:33
  53.2 1.6 %collective-permute-start.19 = (s16[576,128]{1,0:T(8,128)(2,1)S(1)}, s16[576,128]{1,0:T(8,128)(2,1)S(1)}, u32[]{:S(2)}, u32[]{:S(2)}) collective-permute-start(s16[576,128]{1,0:T(8,128)(2,1)S(1)} %pad_add_fusion), channel_id=1, source_target_pairs={{0,8},{4,12},{8,0},{12,4},{16,24},{20,28},{24,16},{28,20},{1,9},{5... | collective-permute-start | bytes 442376 | tf_op jit(solution)/shard_map/ppermute | solution.py:311
  55.6 4.1 %collective-permute-done.17 = s16[576,128]{1,0:T(8,128)(2,1)S(1)} collective-permute-done((s16[576,128]{1,0:T(8,128)(2,1)S(1)}, s16[576,128]{1,0:T(8,128)(2,1)S(1)}, u32[]{:S(2)}, u32[]{:S(2)}) %collective-permute-start.17) | collective-permute-done | bytes 147488 | tf_op jit(solution)/shard_map/ppermute | solution.py:311
  59.7 2.1 %collective-permute-done.18 = s16[576,128]{1,0:T(8,128)(2,1)S(1)} collective-permute-done((s16[576,128]{1,0:T(8,128)(2,1)S(1)}, s16[576,128]{1,0:T(8,128)(2,1)S(1)}, u32[]{:S(2)}, u32[]{:S(2)}) %collective-permute-start.18) | collective-permute-done | bytes 147488 | tf_op jit(solution)/shard_map/ppermute | solution.py:311
  61.9 1.8 %shard_map.62.part = f32[1024,128]{1,0:T(8,128)S(1)} custom-call(s32[2]{0:T(128)S(1)} %pad_add_fusion.1.place, s16[2304,128]{1,0:T(8,128)(2,1)S(1)} %constant_dynamic-update-slice_fusion.15.block), custom_call_target="tpu_custom_call" | custom-call | flops 2000000000 | bytes 1114120 | tf_op jit(solution)/shard_map/pallas_call | solution.py:33
  63.9 2.6 %shard_map.63 = f32[64,2048]{1,0:T(8,128)} custom-call(s32[2]{0:T(128)S(1)} %pad_add_fusion.1.place, f32[64,2048]{1,0:T(8,128)S(1)} %shard_map.61.image, f32[1024,128]{1,0:T(8,128)S(1)} %shard_map.62.part, s16[2304,128]{1,0:T(8,128)(2,1)S(1)} %collective-permute-done.20.block), custom_call_target="tpu_custom_call" | custom-call | flops 2000000000 | bytes 2162696 | tf_op jit(solution)/shard_map/pallas_call | solution.py:33
  (48 shorter events, 11.2 us)
Async XLA Ops:
  1.7 7.3 %collective-permute-start = (s16[192,128]{1,0:T(8,128)(2,1)S(1)}, s16[192,128]{1,0:T(8,128)(2,1)S(1)}, u32[]{:S(2)}, u32[]{:S(2)}) collective-permute-start(s16[192,128]{1,0:T(8,128)(2,1)S(1)} %get-tuple-element.19), channel_id=1, source_target_pairs={{0,3},{1,2},{2,1},{3,0},{4,7},{5,6},{6,5},{7,4},{8,11},{9,10},{10,... | collective-permute-start | bytes 147464 | tf_op jit(solution)/shard_map/ppermute | solution.py:311
  6.8 5.0 %collective-permute-start.1 = (s16[192,128]{1,0:T(8,128)(2,1)S(1)}, s16[192,128]{1,0:T(8,128)(2,1)S(1)}, u32[]{:S(2)}, u32[]{:S(2)}) collective-permute-start(s16[192,128]{1,0:T(8,128)(2,1)S(1)} %get-tuple-element.20), channel_id=1, source_target_pairs={{0,2},{1,3},{2,0},{3,1},{4,6},{5,7},{6,4},{7,5},{8,10},{9,11},{10,... | collective-permute-start | bytes 147464 | tf_op jit(solution)/shard_map/ppermute | solution.py:311
  6.9 5.0 %collective-permute-start.2 = (s16[192,128]{1,0:T(8,128)(2,1)S(1)}, s16[192,128]{1,0:T(8,128)(2,1)S(1)}, u32[]{:S(2)}, u32[]{:S(2)}) collective-permute-start(s16[192,128]{1,0:T(8,128)(2,1)S(1)} %get-tuple-element.21), channel_id=1, source_target_pairs={{0,1},{1,0},{2,3},{3,2},{4,5},{5,4},{6,7},{7,6},{8,9},{9,8},{10,11... | collective-permute-start | bytes 147464 | tf_op jit(solution)/shard_map/ppermute | solution.py:311
  11.8 10.7 %copy-start = (f32[64,2048]{1,0:T(8,128)S(1)}, f32[64,2048]{1,0:T(8,128)}, u32[]{:S(2)}) copy-start(f32[64,2048]{1,0:T(8,128)} %image.5) | copy-start | bytes 1572868
  11.9 5.8 %collective-permute-start.3 = (s16[448,128]{1,0:T(8,128)(2,1)S(1)}, s16[448,128]{1,0:T(8,128)(2,1)S(1)}, u32[]{:S(2)}, u32[]{:S(2)}) collective-permute-start(s16[448,128]{1,0:T(8,128)(2,1)S(1)} %get-tuple-element.24), channel_id=1, source_target_pairs={{0,8},{4,12},{8,0},{12,4},{16,24},{20,28},{24,16},{28,20},{1,9},{5... | collective-permute-start | bytes 344072 | tf_op jit(solution)/shard_map/ppermute | solution.py:311
  13.5 5.9 %collective-permute-start.4 = (s16[448,128]{1,0:T(8,128)(2,1)S(1)}, s16[448,128]{1,0:T(8,128)(2,1)S(1)}, u32[]{:S(2)}, u32[]{:S(2)}) collective-permute-start(s16[448,128]{1,0:T(8,128)(2,1)S(1)} %get-tuple-element.25), channel_id=1, source_target_pairs={{0,16},{4,20},{8,24},{12,28},{16,0},{20,4},{24,8},{28,12},{1,17},{... | collective-permute-start | bytes 344072 | tf_op jit(solution)/shard_map/ppermute | solution.py:311
  15.0 5.7 %collective-permute-start.5 = (s16[448,128]{1,0:T(8,128)(2,1)S(1)}, s16[448,128]{1,0:T(8,128)(2,1)S(1)}, u32[]{:S(2)}, u32[]{:S(2)}) collective-permute-start(s16[448,128]{1,0:T(8,128)(2,1)S(1)} %get-tuple-element.26), channel_id=1, source_target_pairs={{0,24},{4,28},{8,16},{12,20},{16,8},{20,12},{24,0},{28,4},{1,25},{... | collective-permute-start | bytes 344072 | tf_op jit(solution)/shard_map/ppermute | solution.py:311
  17.7 4.9 %copy-start.1 = (bf16[2,1,256,256]{3,2,1,0:T(8,128)(2,1)S(1)}, bf16[2,1,256,256]{3,2,1,0:T(8,128)(2,1)}, u32[]{:S(2)}) copy-start(bf16[2,1,256,256]{3,2,1,0:T(8,128)(2,1)} %param.9) | copy-start | bytes 786436
  20.7 1.9 %collective-permute-start.6 = (s16[1792,128]{1,0:T(8,128)(2,1)S(1)}, s16[1792,128]{1,0:T(8,128)(2,1)S(1)}, u32[]{:S(2)}, u32[]{:S(2)}) collective-permute-start(s16[1792,128]{1,0:T(8,128)(2,1)S(1)} %constant_dynamic-update-slice_fusion.mine), channel_id=1, source_target_pairs={{0,4},{4,0},{8,12},{12,8},{16,20},{20,16},{24,28},{28,24},{1,5},{5... | collective-permute-start | bytes 1376264 | tf_op jit(solution)/shard_map/ppermute | solution.py:311
  24.9 7.4 %collective-permute-start.9 = (s16[144,128]{1,0:T(8,128)(2,1)S(1)}, s16[144,128]{1,0:T(8,128)(2,1)S(1)}, u32[]{:S(2)}, u32[]{:S(2)}) collective-permute-start(s16[144,128]{1,0:T(8,128)(2,1)S(1)} %get-tuple-element.30), channel_id=1, source_target_pairs={{0,3},{1,2},{2,1},{3,0},{4,7},{5,6},{6,5},{7,4},{8,11},{9,10},{10,... | collective-permute-start | bytes 110600 | tf_op jit(solution)/shard_map/ppermute | solution.py:311
  27.1 5.2 %collective-permute-start.8 = (s16[144,128]{1,0:T(8,128)(2,1)S(1)}, s16[144,128]{1,0:T(8,128)(2,1)S(1)}, u32[]{:S(2)}, u32[]{:S(2)}) collective-permute-start(s16[144,128]{1,0:T(8,128)(2,1)S(1)} %get-tuple-element.30), channel_id=1, source_target_pairs={{0,2},{1,3},{2,0},{3,1},{4,6},{5,7},{6,4},{7,5},{8,10},{9,11},{10,... | collective-permute-start | bytes 110600 | tf_op jit(solution)/shard_map/ppermute | solution.py:311
  27.1 4.7 %collective-permute-start.7 = (s16[144,128]{1,0:T(8,128)(2,1)S(1)}, s16[144,128]{1,0:T(8,128)(2,1)S(1)}, u32[]{:S(2)}, u32[]{:S(2)}) collective-permute-start(s16[144,128]{1,0:T(8,128)(2,1)S(1)} %get-tuple-element.30), channel_id=1, source_target_pairs={{0,1},{1,0},{2,3},{3,2},{4,5},{5,4},{6,7},{7,6},{8,9},{9,8},{10,11... | collective-permute-start | bytes 110600 | tf_op jit(solution)/shard_map/ppermute | solution.py:311
  32.3 7.7 %collective-permute-start.10 = (s16[576,128]{1,0:T(8,128)(2,1)S(1)}, s16[576,128]{1,0:T(8,128)(2,1)S(1)}, u32[]{:S(2)}, u32[]{:S(2)}) collective-permute-start(s16[576,128]{1,0:T(8,128)(2,1)S(1)} %get-tuple-element.33), channel_id=1, source_target_pairs={{0,24},{4,28},{8,16},{12,20},{16,8},{20,12},{24,0},{28,4},{1,25},{... | collective-permute-start | bytes 442376 | tf_op jit(solution)/shard_map/ppermute | solution.py:311
  32.9 8.3 %collective-permute-start.11 = (s16[576,128]{1,0:T(8,128)(2,1)S(1)}, s16[576,128]{1,0:T(8,128)(2,1)S(1)}, u32[]{:S(2)}, u32[]{:S(2)}) collective-permute-start(s16[576,128]{1,0:T(8,128)(2,1)S(1)} %get-tuple-element.33), channel_id=1, source_target_pairs={{0,16},{4,20},{8,24},{12,28},{16,0},{20,4},{24,8},{28,12},{1,17},{... | collective-permute-start | bytes 442376 | tf_op jit(solution)/shard_map/ppermute | solution.py:311
  34.4 6.8 %collective-permute-start.12 = (s16[576,128]{1,0:T(8,128)(2,1)S(1)}, s16[576,128]{1,0:T(8,128)(2,1)S(1)}, u32[]{:S(2)}, u32[]{:S(2)}) collective-permute-start(s16[576,128]{1,0:T(8,128)(2,1)S(1)} %get-tuple-element.33), channel_id=1, source_target_pairs={{0,8},{4,12},{8,0},{12,4},{16,24},{20,28},{24,16},{28,20},{1,9},{5... | collective-permute-start | bytes 442376 | tf_op jit(solution)/shard_map/ppermute | solution.py:311
  41.3 2.4 %collective-permute-start.13 = (s16[2304,128]{1,0:T(8,128)(2,1)S(1)}, s16[2304,128]{1,0:T(8,128)(2,1)S(1)}, u32[]{:S(2)}, u32[]{:S(2)}) collective-permute-start(s16[2304,128]{1,0:T(8,128)(2,1)S(1)} %constant_dynamic-update-slice_fusion.8.block), channel_id=1, source_target_pairs={{0,4},{4,0},{8,12},{12,8},{16,20},{20,16},{24,28},{28,24},{1,5},{5... | collective-permute-start | bytes 1769480 | tf_op jit(solution)/shard_map/ppermute | solution.py:311
  44.7 6.3 %collective-permute-start.16 = (s16[144,128]{1,0:T(8,128)(2,1)S(1)}, s16[144,128]{1,0:T(8,128)(2,1)S(1)}, u32[]{:S(2)}, u32[]{:S(2)}) collective-permute-start(s16[144,128]{1,0:T(8,128)(2,1)S(1)} %shard_map.59), channel_id=1, source_target_pairs={{0,3},{1,2},{2,1},{3,0},{4,7},{5,6},{6,5},{7,4},{8,11},{9,10},{10,... | collective-permute-start | bytes 110600 | tf_op jit(solution)/shard_map/ppermute | solution.py:311
  46.9 5.1 %collective-permute-start.15 = (s16[144,128]{1,0:T(8,128)(2,1)S(1)}, s16[144,128]{1,0:T(8,128)(2,1)S(1)}, u32[]{:S(2)}, u32[]{:S(2)}) collective-permute-start(s16[144,128]{1,0:T(8,128)(2,1)S(1)} %shard_map.59), channel_id=1, source_target_pairs={{0,2},{1,3},{2,0},{3,1},{4,6},{5,7},{6,4},{7,5},{8,10},{9,11},{10,... | collective-permute-start | bytes 110600 | tf_op jit(solution)/shard_map/ppermute | solution.py:311
  46.9 5.1 %collective-permute-start.14 = (s16[144,128]{1,0:T(8,128)(2,1)S(1)}, s16[144,128]{1,0:T(8,128)(2,1)S(1)}, u32[]{:S(2)}, u32[]{:S(2)}) collective-permute-start(s16[144,128]{1,0:T(8,128)(2,1)S(1)} %shard_map.59), channel_id=1, source_target_pairs={{0,1},{1,0},{2,3},{3,2},{4,5},{5,4},{6,7},{7,6},{8,9},{9,8},{10,11... | collective-permute-start | bytes 110600 | tf_op jit(solution)/shard_map/ppermute | solution.py:311
  52.0 7.7 %collective-permute-start.17 = (s16[576,128]{1,0:T(8,128)(2,1)S(1)}, s16[576,128]{1,0:T(8,128)(2,1)S(1)}, u32[]{:S(2)}, u32[]{:S(2)}) collective-permute-start(s16[576,128]{1,0:T(8,128)(2,1)S(1)} %pad_add_fusion), channel_id=1, source_target_pairs={{0,24},{4,28},{8,16},{12,20},{16,8},{20,12},{24,0},{28,4},{1,25},{... | collective-permute-start | bytes 442376 | tf_op jit(solution)/shard_map/ppermute | solution.py:311
  53.2 8.6 %collective-permute-start.19 = (s16[576,128]{1,0:T(8,128)(2,1)S(1)}, s16[576,128]{1,0:T(8,128)(2,1)S(1)}, u32[]{:S(2)}, u32[]{:S(2)}) collective-permute-start(s16[576,128]{1,0:T(8,128)(2,1)S(1)} %pad_add_fusion), channel_id=1, source_target_pairs={{0,8},{4,12},{8,0},{12,4},{16,24},{20,28},{24,16},{28,20},{1,9},{5... | collective-permute-start | bytes 442376 | tf_op jit(solution)/shard_map/ppermute | solution.py:311
  54.9 6.9 %collective-permute-start.18 = (s16[576,128]{1,0:T(8,128)(2,1)S(1)}, s16[576,128]{1,0:T(8,128)(2,1)S(1)}, u32[]{:S(2)}, u32[]{:S(2)}) collective-permute-start(s16[576,128]{1,0:T(8,128)(2,1)S(1)} %pad_add_fusion), channel_id=1, source_target_pairs={{0,16},{4,20},{8,24},{12,28},{16,0},{20,4},{24,8},{28,12},{1,17},{... | collective-permute-start | bytes 442376 | tf_op jit(solution)/shard_map/ppermute | solution.py:311
  61.9 2.1 %collective-permute-start.20 = (s16[2304,128]{1,0:T(8,128)(2,1)S(1)}, s16[2304,128]{1,0:T(8,128)(2,1)S(1)}, u32[]{:S(2)}, u32[]{:S(2)}) collective-permute-start(s16[2304,128]{1,0:T(8,128)(2,1)S(1)} %constant_dynamic-update-slice_fusion.15.block), channel_id=1, source_target_pairs={{0,4},{4,0},{8,12},{12,8},{16,20},{20,16},{24,28},{28,24},{1,5},{5... | collective-permute-start | bytes 1769480 | tf_op jit(solution)/shard_map/ppermute | solution.py:311

commit v4 on v3

--- a/solution.py
+++ b/solution.py
@@ -14,7 +14,9 @@
 TILE = 8
 EXTRA = 16
 BLOCK = 16
-LEVELS = 65535.0 / 3.0
+PART = 64
+FINE = 32
+FLOOR = 10
 LEAST = 119
 
 shrinkage = 0.05
@@ -22,7 +24,7 @@
 VMEM_LIMIT = 48 * 1024 * 1024
 
 
-def call(kernel, outs, args, flops, smem=0, hbm=0, scratch=()):
+def call(kernel, outs, args, flops, smem=0, hbm=0, scratch=(), scalars=0):
     spaces = [pl.BlockSpec(memory_space=pltpu.SMEM)] * smem
     spaces += [pl.BlockSpec(memory_space=pltpu.HBM)] * hbm
     spaces += [pl.BlockSpec(memory_space=pltpu.VMEM)] * (len(args) - smem - hbm)
@@ -34,7 +36,8 @@
         kernel,
         out_shape=list(outs),
         in_specs=spaces,
-        out_specs=[pl.BlockSpec(memory_space=pltpu.VMEM)] * len(outs),
+        out_specs=[pl.BlockSpec(memory_space=pltpu.VMEM)] * (len(outs) - scalars)
+        + [pl.BlockSpec(memory_space=pltpu.SMEM)] * scalars,
         scratch_shapes=list(scratch),
         compiler_params=pltpu.CompilerParams(vmem_limit_bytes=VMEM_LIMIT),
         cost_estimate=pl.CostEstimate(flops=flops, bytes_accessed=moved, transcendentals=0),
@@ -63,6 +66,26 @@
     power = jnp.maximum(jnp.floor(jnp.log2(jnp.maximum(size, 1e-37))), -LEAST)
     code = (power + LEAST) * 128.0 + jnp.round(size * jnp.exp2(7.0 - power))
     return jnp.where(x < 0, -code, code).astype(I32)
+
+
+def code_levels(x):
+    near = x.astype(BF16).astype(F32)
+    power = jnp.maximum(jnp.floor(jnp.log2(jnp.maximum(near, 1e-37))), -FLOOR)
+    unit = jnp.exp2(power - 7.0)
+    lead = jnp.round(near / unit)
+    step = jnp.round(((x - lead * unit) / unit + 0.5) * (FINE - 1))
+    step = jnp.clip(step, 0.0, FINE - 1)
+    code = ((power + FLOOR) * 128.0 + lead) * FINE + step - 32768.0
+    return code.astype(I32).astype(I16)
+
+
+def levels_of(code):
+    level = code >> log2(FINE)
+    power = jnp.maximum((level >> 7) - 1, 0)
+    unit = jnp.exp2((power - (FLOOR + 7)).astype(F32))
+    near = ((level - power * 128).astype(F32) * unit).astype(BF16).astype(F32)
+    step = (code & (FINE - 1)).astype(F32)
+    return near, near + (step * (1.0 / (FINE - 1)) - 0.5) * unit
 
 
 def floats_of(code):
@@ -126,7 +149,7 @@
     for copy in copies:
         copy.wait()
     strips = tiled_strips(band_in[...])
-    share = (jnp.round(strips * LEVELS) - 32768.0).astype(I32).astype(I16)
+    share = code_levels(strips)
     raw = terms_in[...]
     across, column = raw >> log2(F * wide), raw & (F * wide - 1)
     terms_in[...] = (
@@ -166,59 +189,93 @@
             out[at : at + BLOCK] = got[k][first : first + BLOCK]
 
 
-def first_kernel(C, F, L, place, image, kernels, mine, other, start_out, seen_out, scalars_out, msg):
+def table_of(levels):
+    return jnp.concatenate(split(levels, 2), axis=1)
+
+
+def shares_of(got, chips, size, used):
+    return [got[q * size : q * size + used].astype(I32).astype(F32) + 32768.0 for q in range(chips)]
+
+
+def sorted_blocks(C, F, L, c, got, first):
+    chips, slots = C // 2, C * F
+    size = got.shape[0] // chips
+    blocks = jnp.concatenate(
+        [got[(q + 1) * size - F * BLOCK : (q + 1) * size] for q in range(chips)], axis=0
+    ).astype(I32)
+
+    def pick(kinds, start):
+        out = iota((kinds * slots, blocks.shape[0]), 0)
+        source = (out % slots - first) * BLOCK + start + out // slots
+        return one_hot(iota(out.shape, 1) == source)
+
+    seen = jnp.dot(pick(4, 2 * L * (c & 1)), floats_of(blocks), preferred_element_type=F32)
+    whole = jnp.dot(pick(3, 4 * L), halves(blocks), preferred_element_type=F32)
+    return seen, whole
+
+
+def ready_kernel(C, F, L, place, image, kernels, mine, table_out, seen_out, whole_out, turned_out):
+    height, width = image.shape
+    used = (F - 1) * (height * width // STRIP // C)
+    shares = shares_of(mine, C // 2, used + F * BLOCK, used)
+    own = tiled_strips(image)
+    table_out[...] = table_of(jnp.concatenate([own] + shares, axis=0))
+    seen_out[...], whole_out[...] = sorted_blocks(C, F, L, place[0], mine, 0)
+    for ch in range(L):
+        turned_out[ch] = kernels[ch].T
+
+
+def first_kernel(
+    C, F, L, place, known, seen_in, whole_in, kernels, turned, other, start_out, seen_out, refs_out, live_out, msg
+):
     c, f = place[0], place[1]
     chips, slots = C // 2, C * F
-    height, width = image.shape
-    per_facet = height * width // STRIP
+    size = other.shape[0] // chips
+    used = size - F * BLOCK
+    per_facet = known.shape[0] - chips * used
     piece = per_facet // C
-    size = (F - 1) * piece + F * BLOCK
-    tiles, shares = [], []
-    for got in (mine, other):
-        for q in range(chips):
-            shares.append(got[q * size : q * size + (F - 1) * piece].astype(I32))
-            tiles.append(got[q * size + (F - 1) * piece : (q + 1) * size].astype(I32))
-    blocks = jnp.concatenate(tiles, axis=0)
-    out = iota((4 * slots, 1), 0)
-    source = (out % slots) * BLOCK + 2 * L * (c & 1) + out // slots
-    pick = iota((4 * slots, slots * BLOCK), 1) == source
-    seen = jnp.dot(one_hot(pick), floats_of(blocks), preferred_element_type=F32)
-    out = iota((3 * slots, 1), 0)
-    source = (out % slots) * BLOCK + 4 * L + out // slots
-    pick = iota((3 * slots, slots * BLOCK), 1) == source
-    whole = joined(jnp.dot(one_hot(pick), halves(blocks), preferred_element_type=F32))
-    lane = iota((slots, STRIP), 1)
-    scalars = jnp.zeros((slots, STRIP), F32)
-    for kind in range(3):
-        for ch in range(L):
-            of_kind = whole[kind * slots : (kind + 1) * slots]
-            value = jnp.sum(jnp.where(lane == c * L + ch, of_kind, 0.0), axis=1, keepdims=True)
-            at = L * TERMS + ch if kind == TERMS else ch * TERMS + kind
-            scalars = jnp.where(lane == at, value, scalars)
-    col = ref_column(scalars, L)
+    seen, whole = sorted_blocks(C, F, L, c, other, slots // 2)
+    seen = seen + seen_in[...]
+    row, column = iota((2 * STRIP, L * STRIP), 0), iota((2 * STRIP, L * STRIP), 1)
+    channel = c * L + column // STRIP
+    lanes = jnp.where(row == channel, 64.0, jnp.where(row == channel + STRIP, 1.0, 0.0))
+    whole = jnp.dot(
+        (whole + whole_in[...]).astype(BF16), lanes.astype(BF16), preferred_element_type=F32
+    )
+    kinds = [
+        whole[kind * slots : (kind + 1) * slots, ch * STRIP : (ch + 1) * STRIP]
+        for ch in range(L)
+        for kind in range(TERMS + 1)
+    ]
+    refs = jnp.concatenate([x for i, x in enumerate(kinds) if i % (TERMS + 1) < TERMS], axis=0)
+    live = jnp.concatenate(kinds[TERMS :: TERMS + 1], axis=0)
+    col = refs.astype(I32)
     facet, local = col >> log2(per_facet), col & (per_facet - 1)
     k, d = facet ^ f, (local >> log2(piece)) ^ c
     turn = ((d & 1) * chips + (d >> 1)) * (F - 1) + k - 1
     place_of = jnp.where(k == 0, local, per_facet + turn * piece + (local & (piece - 1)))
-    own = jnp.round(tiled_strips(image) * LEVELS)
-    levels = jnp.concatenate([own] + [s.astype(F32) + 32768.0 for s in shares], axis=0)
-    table = jnp.concatenate(split(levels, 2), axis=1)
-    pick = iota((col.shape[0], table.shape[0]), 1) == place_of
-    both = jnp.dot(one_hot(pick), table, preferred_element_type=F32)
-    est = (both[:, :STRIP] + both[:, STRIP:]) * (1.0 / LEVELS)
-    start_out[...] = est
+    rest = table_of(jnp.concatenate(shares_of(other, chips, size, used), axis=0))
+
+    def hits(count, start):
+        wide = jnp.concatenate([place_of - start] * (count // STRIP), axis=1)
+        return one_hot(iota(wide.shape, 1) == wide)
+
+    both = jnp.dot(hits(known.shape[0], 0), known[...], preferred_element_type=F32) + jnp.dot(
+        hits(rest.shape[0], known.shape[0]), rest, preferred_element_type=F32
+    )
+    total = both[:, :STRIP] + both[:, STRIP:]
+    near, value = levels_of(jnp.where(k == 0, 0.0, total).astype(I32))
+    sky = jnp.where(k == 0, both[:, :STRIP], near)
+    start_out[...] = jnp.where(k == 0, total, value)
     seen_out[...] = seen.astype(BF16)
-    scalars_out[...] = scalars
-    encode(measure(est, seen, scalars, kernels, L), col, msg)
-
-
-def ref_column(scalars, L):
-    cols = [scalars[:, i : i + 1] for i in range(L * TERMS)]
-    return jnp.concatenate(cols, axis=0).astype(I32)
-
-
-def measure(est, seen, scalars, kernels, L):
-    slots = scalars.shape[0]
+    refs_out[...] = refs
+    live_out[...] = live
+    encode(measure(sky, seen, live, kernels, turned), refs, msg)
+
+
+def measure(est, seen, live, kernels, turned):
+    L = kernels.shape[0]
+    slots = live.shape[0] // L
     adjoints = []
     for ch in range(L):
         a, b, end = (ch * TERMS + i for i in range(3))
@@ -229,75 +286,164 @@
             [seen[a * slots : b * slots], seen[b * slots : end * slots]], axis=1
         )
         predicted = jnp.dot(sky, kernels[ch], preferred_element_type=F32)
-        live = scalars[:, L * TERMS + ch : L * TERMS + ch + 1].astype(I32)
-        lane = iota(predicted.shape, 1) & (VISB - 1)
-        residual = jnp.where(lane < live, predicted - observed, 0.0).astype(BF16)
-        adjoint = lax.dot_general(
-            residual, kernels[ch], (((1,), (1,)), ((), ())), preferred_element_type=F32
-        )
+        alive = iota((slots, VISB), 1).astype(F32) < live[ch * slots : (ch + 1) * slots]
+        residual = jnp.where(
+            jnp.concatenate([alive, alive], axis=1), predicted - observed, 0.0
+        ).astype(BF16)
+        adjoint = jnp.dot(residual, turned[ch], preferred_element_type=F32)
         adjoints += [adjoint[:, :STRIP], adjoint[:, STRIP:]]
     return jnp.concatenate(adjoints, axis=0)
 
 
-def encode(adjoint, col, msg):
-    refs = adjoint.shape[0]
-    top = jnp.max(jnp.abs(adjoint), axis=(0, 1), keepdims=True)
-    exponent = jnp.ceil(jnp.log2(jnp.maximum(top, 1e-30) * (1.0 / 32000.0)))
-    code = jnp.round(adjoint * jnp.exp2(-exponent))
-    msg[:refs] = code.astype(I32).astype(I16)
-    eye = iota((refs, STRIP), 0) == iota((refs, STRIP), 1)
-    ids = jnp.sum(jnp.where(eye, col.astype(F32), 0.0), axis=0, keepdims=True)
+def as_row(col):
+    eye = iota((STRIP, STRIP), 0) == iota((STRIP, STRIP), 1)
+    return jnp.sum(jnp.where(eye, col, 0.0), axis=0, keepdims=True)
+
+
+def scale_of(half):
+    return jnp.exp2(half * 0.5).astype(BF16).astype(F32)
+
+
+def put(msg, code, ids, half):
+    msg[: code.shape[0]] = code.astype(I32).astype(I16)
     row = iota((EXTRA, STRIP), 0)
-    extra = jnp.where(row == 0, ids, jnp.where(row == 1, exponent, 0.0))
-    msg[refs:] = extra.astype(I32).astype(I16)
-
-
-def decode(block):
-    ids, rows = [], []
-    size = STRIP + EXTRA
+    extra = jnp.where(row == 0, ids, jnp.where(row == 1, half, 0.0))
+    msg[code.shape[0] :] = extra.astype(I32).astype(I16)
+
+
+def encode(adjoint, refs, msg):
+    top = jnp.max(jnp.abs(adjoint), axis=1, keepdims=True)
+    half = jnp.ceil(2.0 * jnp.log2(jnp.maximum(top, 1e-30) * (1.0 / 32500.0)))
+    code = jnp.round(adjoint * (1.0 / scale_of(half)))
+    row = as_row(half)
+    put(msg, code, as_row(refs), row)
+    return code, row
+
+
+def sort_kernel(F, per_facet, place, refs, pick_out, numbers_out):
+    f = place[1]
+    ids = as_row(refs[...]).astype(I32)
+    turn = iota((TILE, STRIP), 0)
+    wanted = ((ids >> log2(per_facet)) == (turn ^ f)) & (turn < F)
+    before = one_hot(iota((STRIP, STRIP), 0) < iota((STRIP, STRIP), 1))
+    rank = jnp.dot(one_hot(wanted), before, preferred_element_type=F32)
+    rank = jnp.where(wanted, rank, -1.0)
+    slot = iota((PART, 1), 0).astype(F32)
+    pick = jnp.concatenate([one_hot(rank[k : k + 1] == slot) for k in range(F)], axis=0)
+    pick_out[...] = pick
+    kinds = jnp.where(turn == 0, ids >> 6, jnp.where(turn == 1, ids & 63, 1))
+    found = lax.dot_general(
+        kinds.astype(F32).astype(BF16), pick, (((1,), (1,)), ((), ())), preferred_element_type=F32
+    )
+    found = jnp.where(found[2:3] > 0, found[0:1] * 64.0 + found[1:2], -1.0)
+    for k in range(F):
+        numbers_out[k * EXTRA : (k + 1) * EXTRA] = in_both_halves(found, k)
+
+
+def in_both_halves(rows, k):
+    at = k * PART // STRIP * STRIP
+    pair = jnp.broadcast_to(rows[:, at : at + STRIP], (EXTRA, STRIP))
+    low = iota((EXTRA, STRIP), 1) < PART
+    return jnp.where(low == (k % 2 == 0), pair, pltpu.roll(pair, PART, 1))
+
+
+def join_kernel(*refs):
+    got, out = refs[:-1], refs[-1]
+    F = len(got)
+    rows = got[0].shape[0] - EXTRA
+    number_rows = F * rows // STRIP
+    row, lane = iota((EXTRA, STRIP), 0), iota((EXTRA, STRIP), 1)
+    extra = jnp.zeros((EXTRA, STRIP), I32)
+    for k in range(F):
+        out[k * rows : (k + 1) * rows] = got[k][:rows]
+        here = got[k][rows:].astype(I32)
+        first, at = k * rows % STRIP, k * rows // STRIP
+        own = (lane >= first) & (lane < first + rows)
+        extra = jnp.where(own & (row == at), here[0:1], extra)
+        extra = jnp.where(own & (row == number_rows + at), here[1:2], extra)
+    out[F * rows :] = extra.astype(I16)
+
+
+def decode(F, block, chips):
+    ids, scales, values = [], [], []
+    size = block.shape[0] // chips
+    rows = size - EXTRA
+    number_rows = rows // STRIP
     for at in range(0, block.shape[0], size):
-        extra = block[at + STRIP : at + size].astype(I32)
-        ids.append(extra[0:1])
-        scale = jnp.exp2(extra[1:2].astype(F32))
-        value = block[at : at + STRIP].astype(I32).astype(F32) * scale
-        rows.append(jnp.concatenate(split(value, 2), axis=1))
-    return jnp.concatenate(ids, axis=1), jnp.concatenate(rows, axis=0)
-
-
-def summed(ids, values, strips):
-    both = jnp.dot(one_hot(ids == strips), values, preferred_element_type=F32)
+        extra = block[at + rows : at + size].astype(I32)
+        ids += [extra[j : j + 1] for j in range(number_rows)]
+        scales += [extra[j : j + 1] for j in range(number_rows, 2 * number_rows)]
+        values.append(table_of(block[at : at + rows].astype(I32).astype(F32)))
+    scale = scale_of(jnp.concatenate(scales, axis=1).astype(F32))
+    return ids, scale, jnp.concatenate(values, axis=0)
+
+
+def summed(decoded, strips):
+    ids, scale, values = decoded
+    wide = strips if len(ids) * STRIP == strips.shape[1] else jnp.concatenate([strips] * len(ids), axis=1)
+    hit = jnp.concatenate(ids, axis=1) == wide
+    both = jnp.dot(jnp.where(hit, scale, 0.0).astype(BF16), values, preferred_element_type=F32)
     return both[:, :STRIP] + both[:, STRIP:]
 
 
-def part_kernel(L, scalars, block, out):
-    out[...] = summed(*decode(block), ref_column(scalars[...], L))
-
-
-def next_kernel(L, step, scalars_in, seen, kernels, est_in, part, block, msg):
-    scalars = scalars_in[...]
-    col = ref_column(scalars, L)
-    gradient = part[...] + summed(*decode(block), col)
+def crowd_of(ids, F, per_facet):
+    facets = jnp.concatenate(ids, axis=0) >> log2(per_facet)
+    hits = jnp.concatenate([one_hot(facets == f) for f in range(F)], axis=0)
+    ones = jnp.ones((STRIP, STRIP), BF16)
+    counts = jnp.dot(hits, ones, preferred_element_type=F32)
+    return jnp.max(counts, axis=0, keepdims=True)
+
+
+def part_kernel(F, chips, refs, block, out):
+    out[...] = summed(decode(F, block, chips), refs[...].astype(I32))
+
+
+def next_kernel(
+    F, chips, step, refs, live, seen, kernels, turned, est_in, part, block, pick, numbers, msg, *msgs
+):
+    gradient = part[...] + summed(decode(F, block, chips), refs[...].astype(I32))
     est = jnp.maximum(est_in[...] - step * gradient - shrinkage, 0.0)
-    encode(measure(est, seen[...].astype(F32), scalars, kernels, L), col, msg)
-
-
-def facet_part_kernel(place, block, out):
-    ids, values = decode(block)
+    adjoint = measure(est, seen[...].astype(F32), live[...], kernels, turned)
+    code, half = encode(adjoint, refs[...], msg)
+    both = jnp.dot(pick[...], table_of(code), preferred_element_type=F32)
+    rows = both[:, :STRIP] + both[:, STRIP:]
+    halves_of = lax.dot_general(
+        jnp.broadcast_to(half, (TILE, STRIP)).astype(BF16),
+        pick[...],
+        (((1,), (1,)), ((), ())),
+        preferred_element_type=F32,
+    )[0:1]
+    for k, short in enumerate(msgs):
+        put(
+            short,
+            rows[k * PART : (k + 1) * PART],
+            numbers[k * EXTRA : (k + 1) * EXTRA],
+            in_both_halves(halves_of, k),
+        )
+
+
+def facet_part_kernel(F, chips, place, block, out, *crowd):
+    decoded = decode(F, block, chips)
     count = out.shape[0]
-    chunk = min(256, count)
-    for at in range(0, count, chunk):
-        out[at : at + chunk] = summed(ids, values, iota((chunk, 1), 0) + (place[1] * count + at))
-
-
-def settle_kernel(step, place, image, part, block, out):
-    ids, values = decode(block)
+    out[...] = summed(decoded, iota((count, STRIP), 0) + place[1] * count)
+    for most in crowd:
+        most[...] = jnp.broadcast_to(crowd_of(decoded[0], F, count), most.shape)
+
+
+def settle_kernel(F, chips, step, place, image, part, block, *refs):
+    decoded = decode(F, block, chips)
     height, width = image.shape
     count = part.shape[0]
+    if len(refs) == 3:
+        crowd, out, most = refs
+        most[0] = jnp.max(jnp.maximum(crowd[0:1], crowd_of(decoded[0], F, count))).astype(I32)
+    else:
+        (out,) = refs
     per_band = width // STRIP * TILE
     chunk = min(256, count)
     for at in range(0, count, chunk):
-        strips = iota((chunk, 1), 0) + (place[1] * count + at)
-        gradient = part[at : at + chunk] + summed(ids, values, strips)
+        strips = iota((chunk, STRIP), 0) + (place[1] * count + at)
+        gradient = part[at : at + chunk] + summed(decoded, strips)
         for t in range(0, chunk, TILE):
             r = (at + t) // per_band * TILE
             c = (at + t) % per_band // TILE * STRIP
@@ -360,54 +506,116 @@
 
     at_refs = jax.ShapeDtypeStruct((refs, STRIP), F32)
     message = jax.ShapeDtypeStruct((refs + EXTRA, STRIP), I16)
+    short = jax.ShapeDtypeStruct((PART + EXTRA, STRIP), I16)
     facet_strips = jax.ShapeDtypeStruct((per_facet, STRIP), F32)
-    est, observed, scalars, msg = call(
+    known, seen_part, whole_part, turned = call(
+        functools.partial(ready_kernel, C, F, L),
+        [
+            jax.ShapeDtypeStruct((per_facet + chips * (F - 1) * piece, 2 * STRIP), BF16),
+            at_refs,
+            jax.ShapeDtypeStruct(((TERMS + 1) * C * F, 2 * STRIP), F32),
+            jax.ShapeDtypeStruct(kernels.shape, BF16),
+        ],
+        [place, start_image, kernels, mine],
+        10**8,
+        smem=1,
+    )
+    est, observed, at, live, msg = call(
         functools.partial(first_kernel, C, F, L),
         [
             at_refs,
             jax.ShapeDtypeStruct((refs, STRIP), BF16),
-            jax.ShapeDtypeStruct((C * F, STRIP), F32),
+            at_refs,
+            jax.ShapeDtypeStruct((L * C * F, STRIP), F32),
             message,
         ],
-        [place, start_image, kernels, mine, other],
+        [place, known, seen_part, whole_part, kernels, turned, other],
         5 * 10**8,
         smem=1,
     )
 
-    image = start_image
-    held = None
-    for iteration in range(ITERS):
-        last = iteration + 1 == ITERS
-        near = jnp.concatenate([msg] + [swap(msg, "facet", k) for k in range(1, F)], axis=0)
-        if held is not None:
-            image = settle(step, place, image, *held)
-            near, image = lax.optimization_barrier((near, image))
-        mine = jnp.concatenate([near] + [swap(near, "chan", 2 * j) for j in range(chips - 1, 0, -1)], axis=0)
-        other = swap(mine, "chan", 1)
-        if not last:
-            (part,) = call(
-                functools.partial(part_kernel, L), [at_refs], [scalars, mine], 3 * 10**8
-            )
-            (msg,) = call(
-                functools.partial(next_kernel, L, step),
-                [message],
-                [scalars, observed, kernels, est, part, other],
-                3 * 10**8,
-            )
-        (part,) = call(facet_part_kernel, [facet_strips], [place, mine], 2 * 10**9, smem=1)
-        held = part, other
-    return settle(step, place, image, *held)
-
-
-def settle(step, place, image, part, other):
-    (image,) = call(
-        functools.partial(settle_kernel, step),
-        [jax.ShapeDtypeStruct(image.shape, F32)],
+    def along_facet(msgs):
+        got = [msgs[0]] + [swap(msgs[k], "facet", k) for k in range(1, F)]
+        rows = got[0].shape[0] - EXTRA
+        return call(
+            join_kernel, [jax.ShapeDtypeStruct((F * rows + EXTRA, STRIP), I16)], got, 10**6
+        )[0]
+
+    def around_chan(near):
+        around = [swap(near, "chan", 2 * j) for j in range(chips - 1, 0, -1)]
+        return jnp.concatenate([near] + around, axis=0)
+
+    def along_chan(near):
+        mine = around_chan(near)
+        return mine, swap(mine, "chan", 1)
+
+    def facet_part(mine, *crowd):
+        return call(
+            functools.partial(facet_part_kernel, F, chips),
+            [facet_strips, *crowd],
+            [place, mine],
+            2 * 10**9,
+            smem=1,
+        )
+
+    settle = functools.partial(settle_kernel, F, chips, step)
+    whole = jax.ShapeDtypeStruct(start_image.shape, F32)
+
+    near = along_facet([msg] * F)
+    pick, numbers = call(
+        functools.partial(sort_kernel, F, per_facet),
+        [
+            jax.ShapeDtypeStruct((F * PART, refs), BF16),
+            jax.ShapeDtypeStruct((F * EXTRA, STRIP), F32),
+        ],
+        [place, at],
+        10**8,
+        smem=1,
+    )
+    near, pick, numbers = lax.optimization_barrier((near, pick, numbers))
+    mine, other = along_chan(near)
+    (part,) = call(
+        functools.partial(part_kernel, F, chips), [at_refs], [at, mine], 3 * 10**8
+    )
+    msg, *msgs = call(
+        functools.partial(next_kernel, F, chips, step),
+        [message] + [short] * F,
+        [at, live, observed, kernels, turned, est, part, other, pick, numbers],
+        3 * 10**8,
+    )
+    msg, mine, *msgs = lax.optimization_barrier((msg, mine, *msgs))
+    near = along_facet(msgs)
+    part, crowd = facet_part(mine, jax.ShapeDtypeStruct((TILE, STRIP), F32))
+    near, part, crowd = lax.optimization_barrier((near, part, crowd))
+    around = around_chan(near)
+    image, crowd = call(
+        settle,
+        [whole, jax.ShapeDtypeStruct((1,), I32)],
+        [place, start_image, part, other, crowd],
+        2 * 10**9,
+        smem=1,
+        scalars=1,
+    )
+    crowded = crowd[0] > PART
+    around, image, crowded = lax.optimization_barrier((around, image, crowded))
+
+    other = swap(around, "chan", 1)
+    (part,) = facet_part(around)
+
+    def in_full():
+        mine, other = along_chan(along_facet([msg] * F))
+        (part,) = facet_part(mine)
+        (rest,) = facet_part(other)
+        return part + rest, jnp.zeros((chips * (F * PART + EXTRA), STRIP), I16)
+
+    part, other = lax.cond(crowded, in_full, lambda: (part, other))
+    return call(
+        settle,
+        [whole],
         [place, image, part, other],
         2 * 10**9,
         smem=1,
-    )
-    return image
+    )[0]
 
 
 def dense_device(start_image, visibilities, strip_index, live_counts, uv_kernels):
@@ -453,7 +661,9 @@
         and C & (C - 1) == 0
         and F & (F - 1) == 0
         and C >= 4
+        and ITERS == 2
         and F >= 2
+        and F <= TILE and F * PART % STRIP == 0
         and C * F * L * TERMS == STRIP
         and 4 * L + TERMS + 1 <= BLOCK
         and 4 * L == TILE

time: 66.7 us -> 62.6 us (0.939)
  waiting for transfers between devices: 26.9 us -> 21.3 us
  Pallas kernels: 13.6 us -> 14.5 us
    ppermute x21, waiting for transfers between devices: 26.9 us -> 21.3 us  [swap(): lax.ppermute(x, axis, [(i, i ^ k) for i in range(lax.axis_size(axis))])]
    pallas_call x9 -> x13, Pallas kernels: 13.6 us -> 14.5 us  [call(): pl.pallas_call(kernel, out_shape=list(outs), in_specs=spaces, out_specs=[...]
  transfers between devices with their start and end apart: 21 -> 21, of which waited for: 14 -> 15; matrix products, arithmetic and copies ran while one was open for 0% -> 0% of each run, Pallas kernels for 9% -> 12%
where the time goes in v4:
time: 62.6 us; the launch traced here: 62.4 us
  starting transfers between devices  25.5 us (41%)
  waiting for transfers between devices  21.3 us (34%)
  Pallas kernels  14.5 us (23%)
  between operations  0.84 us (1%)
    ppermute x21, starting transfers between devices, swap(): lax.ppermute(x, axis, [(i, i ^ k) for i in range(lax.axis_size(axis))])  25.5 us
    ppermute x21, waiting for transfers between devices, swap(): lax.ppermute(x, axis, [(i, i ^ k) for i in range(lax.axis_size(axis))])  21.3 us
    pallas_call x13, Pallas kernels, call(): pl.pallas_call(kernel, out_shape=list(outs), in_specs=spaces, out_specs=[...  14.5 us
  transfers between devices with their start and end apart: 21, of which 15 were waited for; matrix products, arithmetic and copies ran while one was open for 0% of the time, Pallas kernels for 12%

profile of v4, /device:TPU:0, one launch (start us, length us, event | category | flops | bytes accessed | tf_op | source)
XLA Modules:
  0.0 62.4 jit_solution(12402522763910345602)
XLA Ops:
  0.1 1.7 %shard_map.55 = (s16[64,128]{1,0:T(8,128)(2,1)S(1)}, s16[192,128]{1,0:T(8,128)(2,1)S(1)}, s16[192,128]{1,0:T(8,128)(2,1)S(1)}, s16[192,128]{1,0:T(8,128)(2,1)S(1)}) custom-call(s32[2]{0:T(128)S(1)} %pad_add_fusion.2.place, f32[64,2048]{1,0:T(8,128)} %image.5, bf16[16,4,256]{2,1,0:T(4,128)(2,1)} %bitcast.14, s32[4,2,16]{2,1,0:T(2,128)} %bitcast.15, ...), custom_call_target="tpu_custom_call" | custom-call | flops 100000000 | bytes 721672 | tf_op jit(solution)/shard_map/pallas_call | solution.py:35
  1.8 5.1 %collective-permute-start.7 = (s16[192,128]{1,0:T(8,128)(2,1)S(1)}, s16[192,128]{1,0:T(8,128)(2,1)S(1)}, u32[]{:S(2)}, u32[]{:S(2)}) collective-permute-start(s16[192,128]{1,0:T(8,128)(2,1)S(1)} %get-tuple-element.60), channel_id=1, source_target_pairs={{0,3},{1,2},{2,1},{3,0},{4,7},{5,6},{6,5},{7,4},{8,11},{9,10},{10,... | collective-permute-start | bytes 147464 | tf_op jit(solution)/shard_map/ppermute | solution.py:457
  7.5 1.6 %collective-permute-done.7.refs_0_ = s16[192,128]{1,0:T(8,128)(2,1)S(1)} collective-permute-done((s16[192,128]{1,0:T(8,128)(2,1)S(1)}, s16[192,128]{1,0:T(8,128)(2,1)S(1)}, u32[]{:S(2)}, u32[]{:S(2)}) %collective-permute-start.7) | collective-permute-done | bytes 49184 | tf_op jit(solution)/shard_map/ppermute | solution.py:457
  9.1 2.8 %collective-permute-done.8.refs_1_ = s16[192,128]{1,0:T(8,128)(2,1)S(1)} collective-permute-done((s16[192,128]{1,0:T(8,128)(2,1)S(1)}, s16[192,128]{1,0:T(8,128)(2,1)S(1)}, u32[]{:S(2)}, u32[]{:S(2)}) %collective-permute-start.8) | collective-permute-done | bytes 49184 | tf_op jit(solution)/shard_map/ppermute | solution.py:457
  12.0 1.6 %collective-permute-start.10 = (s16[448,128]{1,0:T(8,128)(2,1)S(1)}, s16[448,128]{1,0:T(8,128)(2,1)S(1)}, u32[]{:S(2)}, u32[]{:S(2)}) collective-permute-start(s16[448,128]{1,0:T(8,128)(2,1)S(1)} %get-tuple-element.65), channel_id=1, source_target_pairs={{0,8},{4,12},{8,0},{12,4},{16,24},{20,28},{24,16},{28,20},{1,9},{5... | collective-permute-start | bytes 344072 | tf_op jit(solution)/shard_map/ppermute | solution.py:457
  13.5 1.5 %collective-permute-start.11 = (s16[448,128]{1,0:T(8,128)(2,1)S(1)}, s16[448,128]{1,0:T(8,128)(2,1)S(1)}, u32[]{:S(2)}, u32[]{:S(2)}) collective-permute-start(s16[448,128]{1,0:T(8,128)(2,1)S(1)} %get-tuple-element.66), channel_id=1, source_target_pairs={{0,16},{4,20},{8,24},{12,28},{16,0},{20,4},{24,8},{28,12},{1,17},{... | collective-permute-start | bytes 344072 | tf_op jit(solution)/shard_map/ppermute | solution.py:457
  15.5 2.2 %collective-permute-done.10 = s16[448,128]{1,0:T(8,128)(2,1)S(1)} collective-permute-done((s16[448,128]{1,0:T(8,128)(2,1)S(1)}, s16[448,128]{1,0:T(8,128)(2,1)S(1)}, u32[]{:S(2)}, u32[]{:S(2)}) %collective-permute-start.10) | collective-permute-done | bytes 114720 | tf_op jit(solution)/shard_map/ppermute | solution.py:457
  17.8 1.6 %collective-permute-done.11 = s16[448,128]{1,0:T(8,128)(2,1)S(1)} collective-permute-done((s16[448,128]{1,0:T(8,128)(2,1)S(1)}, s16[448,128]{1,0:T(8,128)(2,1)S(1)}, u32[]{:S(2)}, u32[]{:S(2)}) %collective-permute-start.11) | collective-permute-done | bytes 114720 | tf_op jit(solution)/shard_map/ppermute | solution.py:457
  19.4 1.3 %collective-permute-done.12 = s16[448,128]{1,0:T(8,128)(2,1)S(1)} collective-permute-done((s16[448,128]{1,0:T(8,128)(2,1)S(1)}, s16[448,128]{1,0:T(8,128)(2,1)S(1)}, u32[]{:S(2)}, u32[]{:S(2)}) %collective-permute-start.12) | collective-permute-done | bytes 114720 | tf_op jit(solution)/shard_map/ppermute | solution.py:457
  22.6 2.0 %shard_map.58 = (f32[128,128]{1,0:T(8,128)S(1)}, bf16[128,128]{1,0:T(8,128)(2,1)S(1)}, f32[128,128]{1,0:T(8,128)S(1)}, f32[64,128]{1,0:T(8,128)S(1)}, s16[144,128]{1,0:T(8,128)(2,1)S(1)}) custom-call(s32[2]{0:T(128)S(1)} %pad_add_fusion.2.place, bf16[2560,256]{1,0:T(8,128)(2,1)S(1)} %get-tuple-element.68.known, f32[128,128]{1,0:T(8,128)S(1)} %get-tuple-element.69.seen_in, ...), custom_call_target="tpu_custom_call" | custom-call | flops 500000000 | bytes 2691080 | tf_op jit(solution)/shard_map/pallas_call | solution.py:35
  25.4 2.0 %collective-permute-start.15 = (s16[144,128]{1,0:T(8,128)(2,1)S(1)}, s16[144,128]{1,0:T(8,128)(2,1)S(1)}, u32[]{:S(2)}, u32[]{:S(2)}) collective-permute-start(s16[144,128]{1,0:T(8,128)(2,1)S(1)} %get-tuple-element.76.refs_0_), channel_id=1, source_target_pairs={{0,2},{1,3},{2,0},{3,1},{4,6},{5,7},{6,4},{7,5},{8,10},{9,11},{10,... | collective-permute-start | bytes 110600 | tf_op jit(solution)/shard_map/ppermute | solution.py:457
  27.4 1.7 %collective-permute-start.16 = (s16[144,128]{1,0:T(8,128)(2,1)S(1)}, s16[144,128]{1,0:T(8,128)(2,1)S(1)}, u32[]{:S(2)}, u32[]{:S(2)}) collective-permute-start(s16[144,128]{1,0:T(8,128)(2,1)S(1)} %get-tuple-element.76.refs_0_), channel_id=1, source_target_pairs={{0,3},{1,2},{2,1},{3,0},{4,7},{5,6},{6,5},{7,4},{8,11},{9,10},{10,... | collective-permute-start | bytes 110600 | tf_op jit(solution)/shard_map/ppermute | solution.py:457
  30.4 2.8 %collective-permute-done.16.refs_3_ = s16[144,128]{1,0:T(8,128)(2,1)S(1)} collective-permute-done((s16[144,128]{1,0:T(8,128)(2,1)S(1)}, s16[144,128]{1,0:T(8,128)(2,1)S(1)}, u32[]{:S(2)}, u32[]{:S(2)}) %collective-permute-start.16) | collective-permute-done | bytes 36896 | tf_op jit(solution)/shard_map/ppermute | solution.py:457
  33.7 1.5 %collective-permute-start.18 = (s16[528,128]{1,0:T(8,128)(2,1)S(1)}, s16[528,128]{1,0:T(8,128)(2,1)S(1)}, u32[]{:S(2)}, u32[]{:S(2)}) collective-permute-start(s16[528,128]{1,0:T(8,128)(2,1)S(1)} %shard_map.59), channel_id=1, source_target_pairs={{0,16},{4,20},{8,24},{12,28},{16,0},{20,4},{24,8},{28,12},{1,17},{... | collective-permute-start | bytes 405512 | tf_op jit(solution)/shard_map/ppermute | solution.py:457
  35.2 1.6 %collective-permute-start.19 = (s16[528,128]{1,0:T(8,128)(2,1)S(1)}, s16[528,128]{1,0:T(8,128)(2,1)S(1)}, u32[]{:S(2)}, u32[]{:S(2)}) collective-permute-start(s16[528,128]{1,0:T(8,128)(2,1)S(1)} %shard_map.59), channel_id=1, source_target_pairs={{0,8},{4,12},{8,0},{12,4},{16,24},{20,28},{24,16},{28,20},{1,9},{5... | collective-permute-start | bytes 405512 | tf_op jit(solution)/shard_map/ppermute | solution.py:457
  36.8 2.8 %collective-permute-done.17 = s16[528,128]{1,0:T(8,128)(2,1)S(1)} collective-permute-done((s16[528,128]{1,0:T(8,128)(2,1)S(1)}, s16[528,128]{1,0:T(8,128)(2,1)S(1)}, u32[]{:S(2)}, u32[]{:S(2)}) %collective-permute-start.17) | collective-permute-done | bytes 135200 | tf_op jit(solution)/shard_map/ppermute | solution.py:457
  40.9 1.5 %collective-permute-done.20.block = s16[2112,128]{1,0:T(8,128)(2,1)S(1)} collective-permute-done((s16[2112,128]{1,0:T(8,128)(2,1)S(1)}, s16[2112,128]{1,0:T(8,128)(2,1)S(1)}, u32[]{:S(2)}, u32[]{:S(2)}) %collective-permute-start.20) | collective-permute-done | bytes 540704 | tf_op jit(solution)/shard_map/ppermute | solution.py:457
  44.3 1.7 %collective-permute-start.22 = (s16[80,128]{1,0:T(8,128)(2,1)S(1)}, s16[80,128]{1,0:T(8,128)(2,1)S(1)}, u32[]{:S(2)}, u32[]{:S(2)}) collective-permute-start(s16[80,128]{1,0:T(8,128)(2,1)S(1)} %get-tuple-element.89), channel_id=1, source_target_pairs={{0,2},{1,3},{2,0},{3,1},{4,6},{5,7},{6,4},{7,5},{8,10},{9,11},{10,... | collective-permute-start | bytes 61448 | tf_op jit(solution)/shard_map/ppermute | solution.py:457
  46.0 1.9 %collective-permute-start.23 = (s16[80,128]{1,0:T(8,128)(2,1)S(1)}, s16[80,128]{1,0:T(8,128)(2,1)S(1)}, u32[]{:S(2)}, u32[]{:S(2)}) collective-permute-start(s16[80,128]{1,0:T(8,128)(2,1)S(1)} %get-tuple-element.90), channel_id=1, source_target_pairs={{0,3},{1,2},{2,1},{3,0},{4,7},{5,6},{6,5},{7,4},{8,11},{9,10},{10,... | collective-permute-start | bytes 61448 | tf_op jit(solution)/shard_map/ppermute | solution.py:457
  47.9 1.8 %shard_map.64 = (f32[1024,128]{1,0:T(8,128)S(1)}, f32[8,128]{1,0:T(8,128)S(1)}) custom-call(s32[2]{0:T(128)S(1)} %pad_add_fusion.2.place, s16[2112,128]{1,0:T(8,128)(2,1)S(1)} %constant_dynamic-update-slice_fusion.4.block), custom_call_target="tpu_custom_call" | custom-call | flops 2000000000 | bytes 1069064 | tf_op jit(solution)/shard_map/pallas_call | solution.py:35
  49.8 1.9 %collective-permute-done.23.refs_3_ = s16[80,128]{1,0:T(8,128)(2,1)S(1)} collective-permute-done((s16[80,128]{1,0:T(8,128)(2,1)S(1)}, s16[80,128]{1,0:T(8,128)(2,1)S(1)}, u32[]{:S(2)}, u32[]{:S(2)}) %collective-permute-start.23) | collective-permute-done | bytes 20512 | tf_op jit(solution)/shard_map/ppermute | solution.py:457
  51.6 1.7 %collective-permute-start.24 = (s16[272,128]{1,0:T(8,128)(2,1)S(1)}, s16[272,128]{1,0:T(8,128)(2,1)S(1)}, u32[]{:S(2)}, u32[]{:S(2)}) collective-permute-start(s16[272,128]{1,0:T(8,128)(2,1)S(1)} %shard_map.63), channel_id=1, source_target_pairs={{0,24},{4,28},{8,16},{12,20},{16,8},{20,12},{24,0},{28,4},{1,25},{... | collective-permute-start | bytes 208904 | tf_op jit(solution)/shard_map/ppermute | solution.py:457
  55.2 1.8 %shard_map.65 = (f32[64,2048]{1,0:T(8,128)S(1)}, s32[1]{0:T(128)}) custom-call(s32[2]{0:T(128)S(1)} %pad_add_fusion.2.place, f32[64,2048]{1,0:T(8,128)S(1)} %copy-done.1, f32[1024,128]{1,0:T(8,128)S(1)} %get-tuple-element.95.part, s16[2112,128]{1,0:T(8,128)(2,1)S(1)} %collective-permute-done.20.block, f32[8,128]{1,0:T(8,128)S(1)} %get-tuple-element.96.refs_0_), custom_call_target="tpu_custom_call" | custom-call | flops 2000000000 | bytes 2117644 | tf_op jit(solution)/shard_map/pallas_call | solution.py:35
  60.4 2.1 %shard_map.67 = f32[64,2048]{1,0:T(8,128)} custom-call(s32[2]{0:T(128)S(1)} %pad_add_fusion.2.place, f32[64,2048]{1,0:T(8,128)S(1)} %get-tuple-element.99.image, f32[1024,128]{1,0:T(8,128)S(1)} %get-tuple-element.103.part, s16[1088,128]{1,0:T(8,128)(2,1)S(1)} %get-tuple-element.104.block), custom_call_target="tpu_custom_call" | custom-call | flops 2000000000 | bytes 1851400 | tf_op jit(solution)/shard_map/pallas_call | solution.py:35
  (46 shorter events, 13.3 us)
Async XLA Ops:
  0.0 20.8 %copy-start.1 = (f32[64,2048]{1,0:T(8,128)S(1)}, f32[64,2048]{1,0:T(8,128)}, u32[]{:S(2)}) copy-start(f32[64,2048]{1,0:T(8,128)} %image.5) | copy-start | bytes 1572868
  0.0 20.8 %copy-start = (bf16[2,1,256,256]{3,2,1,0:T(8,128)(2,1)S(1)}, bf16[2,1,256,256]{3,2,1,0:T(8,128)(2,1)}, u32[]{:S(2)}) copy-start(bf16[2,1,256,256]{3,2,1,0:T(8,128)(2,1)} %param.11) | copy-start | bytes 786436
  1.8 7.3 %collective-permute-start.7 = (s16[192,128]{1,0:T(8,128)(2,1)S(1)}, s16[192,128]{1,0:T(8,128)(2,1)S(1)}, u32[]{:S(2)}, u32[]{:S(2)}) collective-permute-start(s16[192,128]{1,0:T(8,128)(2,1)S(1)} %get-tuple-element.60), channel_id=1, source_target_pairs={{0,3},{1,2},{2,1},{3,0},{4,7},{5,6},{6,5},{7,4},{8,11},{9,10},{10,... | collective-permute-start | bytes 147464 | tf_op jit(solution)/shard_map/ppermute | solution.py:457
  6.9 5.0 %collective-permute-start.8 = (s16[192,128]{1,0:T(8,128)(2,1)S(1)}, s16[192,128]{1,0:T(8,128)(2,1)S(1)}, u32[]{:S(2)}, u32[]{:S(2)}) collective-permute-start(s16[192,128]{1,0:T(8,128)(2,1)S(1)} %get-tuple-element.61), channel_id=1, source_target_pairs={{0,2},{1,3},{2,0},{3,1},{4,6},{5,7},{6,4},{7,5},{8,10},{9,11},{10,... | collective-permute-start | bytes 147464 | tf_op jit(solution)/shard_map/ppermute | solution.py:457
  6.9 5.0 %collective-permute-start.9 = (s16[192,128]{1,0:T(8,128)(2,1)S(1)}, s16[192,128]{1,0:T(8,128)(2,1)S(1)}, u32[]{:S(2)}, u32[]{:S(2)}) collective-permute-start(s16[192,128]{1,0:T(8,128)(2,1)S(1)} %get-tuple-element.62), channel_id=1, source_target_pairs={{0,1},{1,0},{2,3},{3,2},{4,5},{5,4},{6,7},{7,6},{8,9},{9,8},{10,11... | collective-permute-start | bytes 147464 | tf_op jit(solution)/shard_map/ppermute | solution.py:457
  12.0 5.8 %collective-permute-start.10 = (s16[448,128]{1,0:T(8,128)(2,1)S(1)}, s16[448,128]{1,0:T(8,128)(2,1)S(1)}, u32[]{:S(2)}, u32[]{:S(2)}) collective-permute-start(s16[448,128]{1,0:T(8,128)(2,1)S(1)} %get-tuple-element.65), channel_id=1, source_target_pairs={{0,8},{4,12},{8,0},{12,4},{16,24},{20,28},{24,16},{28,20},{1,9},{5... | collective-permute-start | bytes 344072 | tf_op jit(solution)/shard_map/ppermute | solution.py:457
  13.5 5.9 %collective-permute-start.11 = (s16[448,128]{1,0:T(8,128)(2,1)S(1)}, s16[448,128]{1,0:T(8,128)(2,1)S(1)}, u32[]{:S(2)}, u32[]{:S(2)}) collective-permute-start(s16[448,128]{1,0:T(8,128)(2,1)S(1)} %get-tuple-element.66), channel_id=1, source_target_pairs={{0,16},{4,20},{8,24},{12,28},{16,0},{20,4},{24,8},{28,12},{1,17},{... | collective-permute-start | bytes 344072 | tf_op jit(solution)/shard_map/ppermute | solution.py:457
  15.0 5.7 %collective-permute-start.12 = (s16[448,128]{1,0:T(8,128)(2,1)S(1)}, s16[448,128]{1,0:T(8,128)(2,1)S(1)}, u32[]{:S(2)}, u32[]{:S(2)}) collective-permute-start(s16[448,128]{1,0:T(8,128)(2,1)S(1)} %get-tuple-element.67), channel_id=1, source_target_pairs={{0,24},{4,28},{8,16},{12,20},{16,8},{20,12},{24,0},{28,4},{1,25},{... | collective-permute-start | bytes 344072 | tf_op jit(solution)/shard_map/ppermute | solution.py:457
  20.7 1.9 %collective-permute-start.13 = (s16[1792,128]{1,0:T(8,128)(2,1)S(1)}, s16[1792,128]{1,0:T(8,128)(2,1)S(1)}, u32[]{:S(2)}, u32[]{:S(2)}) collective-permute-start(s16[1792,128]{1,0:T(8,128)(2,1)S(1)} %constant_dynamic-update-slice_fusion.mine), channel_id=1, source_target_pairs={{0,4},{4,0},{8,12},{12,8},{16,20},{20,16},{24,28},{28,24},{1,5},{5... | collective-permute-start | bytes 1376264 | tf_op jit(solution)/shard_map/ppermute | solution.py:457
  24.6 5.3 %collective-permute-start.14 = (s16[144,128]{1,0:T(8,128)(2,1)S(1)}, s16[144,128]{1,0:T(8,128)(2,1)S(1)}, u32[]{:S(2)}, u32[]{:S(2)}) collective-permute-start(s16[144,128]{1,0:T(8,128)(2,1)S(1)} %get-tuple-element.76.refs_0_), channel_id=1, source_target_pairs={{0,1},{1,0},{2,3},{3,2},{4,5},{5,4},{6,7},{7,6},{8,9},{9,8},{10,11... | collective-permute-start | bytes 110600 | tf_op jit(solution)/shard_map/ppermute | solution.py:457
  25.4 5.0 %collective-permute-start.15 = (s16[144,128]{1,0:T(8,128)(2,1)S(1)}, s16[144,128]{1,0:T(8,128)(2,1)S(1)}, u32[]{:S(2)}, u32[]{:S(2)}) collective-permute-start(s16[144,128]{1,0:T(8,128)(2,1)S(1)} %get-tuple-element.76.refs_0_), channel_id=1, source_target_pairs={{0,2},{1,3},{2,0},{3,1},{4,6},{5,7},{6,4},{7,5},{8,10},{9,11},{10,... | collective-permute-start | bytes 110600 | tf_op jit(solution)/shard_map/ppermute | solution.py:457
  27.4 5.8 %collective-permute-start.16 = (s16[144,128]{1,0:T(8,128)(2,1)S(1)}, s16[144,128]{1,0:T(8,128)(2,1)S(1)}, u32[]{:S(2)}, u32[]{:S(2)}) collective-permute-start(s16[144,128]{1,0:T(8,128)(2,1)S(1)} %get-tuple-element.76.refs_0_), channel_id=1, source_target_pairs={{0,3},{1,2},{2,1},{3,0},{4,7},{5,6},{6,5},{7,4},{8,11},{9,10},{10,... | collective-permute-start | bytes 110600 | tf_op jit(solution)/shard_map/ppermute | solution.py:457
  33.2 6.5 %collective-permute-start.17 = (s16[528,128]{1,0:T(8,128)(2,1)S(1)}, s16[528,128]{1,0:T(8,128)(2,1)S(1)}, u32[]{:S(2)}, u32[]{:S(2)}) collective-permute-start(s16[528,128]{1,0:T(8,128)(2,1)S(1)} %shard_map.59), channel_id=1, source_target_pairs={{0,24},{4,28},{8,16},{12,20},{16,8},{20,12},{24,0},{28,4},{1,25},{... | collective-permute-start | bytes 405512 | tf_op jit(solution)/shard_map/ppermute | solution.py:457
  33.7 6.5 %collective-permute-start.18 = (s16[528,128]{1,0:T(8,128)(2,1)S(1)}, s16[528,128]{1,0:T(8,128)(2,1)S(1)}, u32[]{:S(2)}, u32[]{:S(2)}) collective-permute-start(s16[528,128]{1,0:T(8,128)(2,1)S(1)} %shard_map.59), channel_id=1, source_target_pairs={{0,16},{4,20},{8,24},{12,28},{16,0},{20,4},{24,8},{28,12},{1,17},{... | collective-permute-start | bytes 405512 | tf_op jit(solution)/shard_map/ppermute | solution.py:457
  35.2 5.1 %collective-permute-start.19 = (s16[528,128]{1,0:T(8,128)(2,1)S(1)}, s16[528,128]{1,0:T(8,128)(2,1)S(1)}, u32[]{:S(2)}, u32[]{:S(2)}) collective-permute-start(s16[528,128]{1,0:T(8,128)(2,1)S(1)} %shard_map.59), channel_id=1, source_target_pairs={{0,8},{4,12},{8,0},{12,4},{16,24},{20,28},{24,16},{28,20},{1,9},{5... | collective-permute-start | bytes 405512 | tf_op jit(solution)/shard_map/ppermute | solution.py:457
  40.4 2.0 %collective-permute-start.20 = (s16[2112,128]{1,0:T(8,128)(2,1)S(1)}, s16[2112,128]{1,0:T(8,128)(2,1)S(1)}, u32[]{:S(2)}, u32[]{:S(2)}) collective-permute-start(s16[2112,128]{1,0:T(8,128)(2,1)S(1)} %constant_dynamic-update-slice_fusion.4.block), channel_id=1, source_target_pairs={{0,4},{4,0},{8,12},{12,8},{16,20},{20,16},{24,28},{28,24},{1,5},{5... | collective-permute-start | bytes 1622024 | tf_op jit(solution)/shard_map/ppermute | solution.py:457
  43.5 6.2 %collective-permute-start.21 = (s16[80,128]{1,0:T(8,128)(2,1)S(1)}, s16[80,128]{1,0:T(8,128)(2,1)S(1)}, u32[]{:S(2)}, u32[]{:S(2)}) collective-permute-start(s16[80,128]{1,0:T(8,128)(2,1)S(1)} %get-tuple-element.88), channel_id=1, source_target_pairs={{0,1},{1,0},{2,3},{3,2},{4,5},{5,4},{6,7},{7,6},{8,9},{9,8},{10,11... | collective-permute-start | bytes 61448 | tf_op jit(solution)/shard_map/ppermute | solution.py:457
  44.3 5.5 %collective-permute-start.22 = (s16[80,128]{1,0:T(8,128)(2,1)S(1)}, s16[80,128]{1,0:T(8,128)(2,1)S(1)}, u32[]{:S(2)}, u32[]{:S(2)}) collective-permute-start(s16[80,128]{1,0:T(8,128)(2,1)S(1)} %get-tuple-element.89), channel_id=1, source_target_pairs={{0,2},{1,3},{2,0},{3,1},{4,6},{5,7},{6,4},{7,5},{8,10},{9,11},{10,... | collective-permute-start | bytes 61448 | tf_op jit(solution)/shard_map/ppermute | solution.py:457
  46.0 5.6 %collective-permute-start.23 = (s16[80,128]{1,0:T(8,128)(2,1)S(1)}, s16[80,128]{1,0:T(8,128)(2,1)S(1)}, u32[]{:S(2)}, u32[]{:S(2)}) collective-permute-start(s16[80,128]{1,0:T(8,128)(2,1)S(1)} %get-tuple-element.90), channel_id=1, source_target_pairs={{0,3},{1,2},{2,1},{3,0},{4,7},{5,6},{6,5},{7,4},{8,11},{9,10},{10,... | collective-permute-start | bytes 61448 | tf_op jit(solution)/shard_map/ppermute | solution.py:457
  51.6 6.1 %collective-permute-start.24 = (s16[272,128]{1,0:T(8,128)(2,1)S(1)}, s16[272,128]{1,0:T(8,128)(2,1)S(1)}, u32[]{:S(2)}, u32[]{:S(2)}) collective-permute-start(s16[272,128]{1,0:T(8,128)(2,1)S(1)} %shard_map.63), channel_id=1, source_target_pairs={{0,24},{4,28},{8,16},{12,20},{16,8},{20,12},{24,0},{28,4},{1,25},{... | collective-permute-start | bytes 208904 | tf_op jit(solution)/shard_map/ppermute | solution.py:457
  53.3 4.4 %collective-permute-start.25 = (s16[272,128]{1,0:T(8,128)(2,1)S(1)}, s16[272,128]{1,0:T(8,128)(2,1)S(1)}, u32[]{:S(2)}, u32[]{:S(2)}) collective-permute-start(s16[272,128]{1,0:T(8,128)(2,1)S(1)} %shard_map.63), channel_id=1, source_target_pairs={{0,16},{4,20},{8,24},{12,28},{16,0},{20,4},{24,8},{28,12},{1,17},{... | collective-permute-start | bytes 208904 | tf_op jit(solution)/shard_map/ppermute | solution.py:457
  54.4 4.3 %collective-permute-start.26 = (s16[272,128]{1,0:T(8,128)(2,1)S(1)}, s16[272,128]{1,0:T(8,128)(2,1)S(1)}, u32[]{:S(2)}, u32[]{:S(2)}) collective-permute-start(s16[272,128]{1,0:T(8,128)(2,1)S(1)} %shard_map.63), channel_id=1, source_target_pairs={{0,8},{4,12},{8,0},{12,4},{16,24},{20,28},{24,16},{28,20},{1,9},{5... | collective-permute-start | bytes 208904 | tf_op jit(solution)/shard_map/ppermute | solution.py:457
  58.7 1.6 %collective-permute-start.27 = (s16[1088,128]{1,0:T(8,128)(2,1)S(1)}, s16[1088,128]{1,0:T(8,128)(2,1)S(1)}, u32[]{:S(2)}, u32[]{:S(2)}) collective-permute-start(s16[1088,128]{1,0:T(8,128)(2,1)S(1)} %pad_add_fusion.1.block), channel_id=1, source_target_pairs={{0,4},{4,0},{8,12},{12,8},{16,20},{20,16},{24,28},{28,24},{1,5},{5... | collective-permute-start | bytes 835592 | tf_op jit(solution)/shard_map/ppermute | solution.py:457

commit v5 on v4

--- a/solution.py
+++ b/solution.py
@@ -394,14 +394,17 @@
     return jnp.max(counts, axis=0, keepdims=True)
 
 
-def part_kernel(F, chips, refs, block, out):
-    out[...] = summed(decode(F, block, chips), refs[...].astype(I32))
+def part_kernel(F, chips, refs, other_refs, block, out, other_out):
+    strips = jnp.concatenate([refs[...], other_refs[...]], axis=0).astype(I32)
+    total = summed(decode(F, block, chips), strips)
+    out[...] = total[: refs.shape[0]]
+    other_out[...] = total[refs.shape[0] :]
 
 
 def next_kernel(
-    F, chips, step, refs, live, seen, kernels, turned, est_in, part, block, pick, numbers, msg, *msgs
+    step, refs, live, seen, kernels, turned, est_in, part, rest, pick, numbers, msg, *msgs
 ):
-    gradient = part[...] + summed(decode(F, block, chips), refs[...].astype(I32))
+    gradient = part[...] + rest[...]
     est = jnp.maximum(est_in[...] - step * gradient - shrinkage, 0.0)
     adjoint = measure(est, seen[...].astype(F32), live[...], kernels, turned)
     code, half = encode(adjoint, refs[...], msg)
@@ -453,8 +456,12 @@
             )
 
 
-def swap(x, axis, k):
-    return lax.ppermute(x, axis, [(i, i ^ k) for i in range(lax.axis_size(axis))])
+def swap(x, along_chan, along_facet=0):
+    C, F = lax.axis_size("chan"), lax.axis_size("facet")
+    pairs = [
+        (c * F + f, (c ^ along_chan) * F + (f ^ along_facet)) for c in range(C) for f in range(F)
+    ]
+    return lax.ppermute(x, ("chan", "facet"), pairs)
 
 
 def sparse_device(start_image, visibilities, strip_index, live_counts, uv_kernels):
@@ -492,7 +499,7 @@
             pltpu.SemaphoreType.DMA((4,)),
         ],
     )
-    got = [packed[0]] + [swap(packed[k], "facet", k) for k in range(F - 1, 0, -1)][::-1]
+    got = [packed[0]] + [swap(packed[k], 0, k) for k in range(F - 1, 0, -1)][::-1]
     passed = call(
         functools.partial(pass_kernel, F, piece),
         [jax.ShapeDtypeStruct(((F - 1) * piece + F * BLOCK, STRIP), I16)] * chips,
@@ -500,9 +507,9 @@
         10**6,
     )
     mine = jnp.concatenate(
-        [passed[0]] + [swap(passed[j], "chan", 2 * j) for j in range(1, chips)], axis=0
-    )
-    other = swap(mine, "chan", 1)
+        [passed[0]] + [swap(passed[j], 2 * j) for j in range(1, chips)], axis=0
+    )
+    other = swap(mine, 1)
 
     at_refs = jax.ShapeDtypeStruct((refs, STRIP), F32)
     message = jax.ShapeDtypeStruct((refs + EXTRA, STRIP), I16)
@@ -534,20 +541,20 @@
         smem=1,
     )
 
-    def along_facet(msgs):
-        got = [msgs[0]] + [swap(msgs[k], "facet", k) for k in range(1, F)]
+    def along_facet(msgs, cross=0):
+        got = [msgs[0]] + [swap(msgs[k], cross, k) for k in range(1, F)]
         rows = got[0].shape[0] - EXTRA
         return call(
             join_kernel, [jax.ShapeDtypeStruct((F * rows + EXTRA, STRIP), I16)], got, 10**6
         )[0]
 
-    def around_chan(near):
-        around = [swap(near, "chan", 2 * j) for j in range(chips - 1, 0, -1)]
+    def around_chan(near, cross=0):
+        around = [swap(near, 2 * j + cross) for j in range(chips - 1, 0, -1)]
         return jnp.concatenate([near] + around, axis=0)
 
     def along_chan(near):
         mine = around_chan(near)
-        return mine, swap(mine, "chan", 1)
+        return mine, swap(mine, 1)
 
     def facet_part(mine, *crowd):
         return call(
@@ -572,22 +579,28 @@
         10**8,
         smem=1,
     )
-    near, pick, numbers = lax.optimization_barrier((near, pick, numbers))
-    mine, other = along_chan(near)
-    (part,) = call(
-        functools.partial(part_kernel, F, chips), [at_refs], [at, mine], 3 * 10**8
+    near, pick, numbers, at, other_at = lax.optimization_barrier(
+        (near, pick, numbers, at, swap(at, 1))
+    )
+    mine = around_chan(near)
+    part, other_part = call(
+        functools.partial(part_kernel, F, chips),
+        [at_refs, at_refs],
+        [at, other_at, mine],
+        3 * 10**8,
     )
     msg, *msgs = call(
-        functools.partial(next_kernel, F, chips, step),
+        functools.partial(next_kernel, step),
         [message] + [short] * F,
-        [at, live, observed, kernels, turned, est, part, other, pick, numbers],
+        [at, live, observed, kernels, turned, est, part, swap(other_part, 1), pick, numbers],
         3 * 10**8,
     )
     msg, mine, *msgs = lax.optimization_barrier((msg, mine, *msgs))
-    near = along_facet(msgs)
+    near = along_facet(msgs, 1)
+    other = swap(mine, 1)
     part, crowd = facet_part(mine, jax.ShapeDtypeStruct((TILE, STRIP), F32))
-    near, part, crowd = lax.optimization_barrier((near, part, crowd))
-    around = around_chan(near)
+    near, part, crowd, other = lax.optimization_barrier((near, part, crowd, other))
+    around = around_chan(near, 1)
     image, crowd = call(
         settle,
         [whole, jax.ShapeDtypeStruct((1,), I32)],
@@ -599,7 +612,7 @@
     crowded = crowd[0] > PART
     around, image, crowded = lax.optimization_barrier((around, image, crowded))
 
-    other = swap(around, "chan", 1)
+    other = swap(around, 1)
     (part,) = facet_part(around)
 
     def in_full():

time: 62.6 us -> 61.4 us (0.981)
    ppermute x21 -> x23, waiting for transfers between devices: 21.3 us -> 20.8 us  [swap(): return lax.ppermute(x, ('chan', 'facet'), pairs)]
    ppermute x21 -> x23, starting transfers between devices: 25.5 us -> 25.3 us  [swap(): return lax.ppermute(x, ('chan', 'facet'), pairs)]
  transfers between devices with their start and end apart: 21 -> 23, of which waited for: 15 -> 15; matrix products, arithmetic and copies ran while one was open for 0% -> 0% of each run, Pallas kernels for 12% -> 12%
where the time goes in v5:
time: 61.4 us; the launch traced here: 61.3 us
  starting transfers between devices  25.3 us (41%)
  waiting for transfers between devices  20.8 us (34%)
  Pallas kernels  14.1 us (23%)
  between operations  0.84 us (1%)
    ppermute x23, starting transfers between devices, swap(): return lax.ppermute(x, ('chan', 'facet'), pairs)  25.3 us
    ppermute x23, waiting for transfers between devices, swap(): return lax.ppermute(x, ('chan', 'facet'), pairs)  20.8 us
    pallas_call x13, Pallas kernels, call(): pl.pallas_call(kernel, out_shape=list(outs), in_specs=spaces, out_specs=[...  14.1 us
  transfers between devices with their start and end apart: 23, of which 15 were waited for; matrix products, arithmetic and copies ran while one was open for 0% of the time, Pallas kernels for 12%

profile of v5, /device:TPU:0, one launch (start us, length us, event | category | flops | bytes accessed | tf_op | source)
XLA Modules:
  0.0 61.3 jit_solution(4734477998116077585)
XLA Ops:
  0.1 1.7 %shard_map.55 = (s16[64,128]{1,0:T(8,128)(2,1)S(1)}, s16[192,128]{1,0:T(8,128)(2,1)S(1)}, s16[192,128]{1,0:T(8,128)(2,1)S(1)}, s16[192,128]{1,0:T(8,128)(2,1)S(1)}) custom-call(s32[2]{0:T(128)S(1)} %pad_add_fusion.2.place, f32[64,2048]{1,0:T(8,128)} %image.5, bf16[16,4,256]{2,1,0:T(4,128)(2,1)} %bitcast.14, s32[4,2,16]{2,1,0:T(2,128)} %bitcast.15, ...), custom_call_target="tpu_custom_call" | custom-call | flops 100000000 | bytes 721672 | tf_op jit(solution)/shard_map/pallas_call | solution.py:35
  1.8 5.1 %collective-permute-start.7 = (s16[192,128]{1,0:T(8,128)(2,1)S(1)}, s16[192,128]{1,0:T(8,128)(2,1)S(1)}, u32[]{:S(2)}, u32[]{:S(2)}) collective-permute-start(s16[192,128]{1,0:T(8,128)(2,1)S(1)} %get-tuple-element.65), channel_id=1, source_target_pairs={{0,3},{1,2},{2,1},{3,0},{4,7},{5,6},{6,5},{7,4},{8,11},{9,10},{10,... | collective-permute-start | bytes 147464 | tf_op jit(solution)/shard_map/ppermute | solution.py:464
  7.5 1.6 %collective-permute-done.7.refs_0_ = s16[192,128]{1,0:T(8,128)(2,1)S(1)} collective-permute-done((s16[192,128]{1,0:T(8,128)(2,1)S(1)}, s16[192,128]{1,0:T(8,128)(2,1)S(1)}, u32[]{:S(2)}, u32[]{:S(2)}) %collective-permute-start.7) | collective-permute-done | bytes 49184 | tf_op jit(solution)/shard_map/ppermute | solution.py:464
  9.1 2.8 %collective-permute-done.8.refs_1_ = s16[192,128]{1,0:T(8,128)(2,1)S(1)} collective-permute-done((s16[192,128]{1,0:T(8,128)(2,1)S(1)}, s16[192,128]{1,0:T(8,128)(2,1)S(1)}, u32[]{:S(2)}, u32[]{:S(2)}) %collective-permute-start.8) | collective-permute-done | bytes 49184 | tf_op jit(solution)/shard_map/ppermute | solution.py:464
  12.0 1.6 %collective-permute-start.10 = (s16[448,128]{1,0:T(8,128)(2,1)S(1)}, s16[448,128]{1,0:T(8,128)(2,1)S(1)}, u32[]{:S(2)}, u32[]{:S(2)}) collective-permute-start(s16[448,128]{1,0:T(8,128)(2,1)S(1)} %get-tuple-element.70), channel_id=1, source_target_pairs={{0,8},{1,9},{2,10},{3,11},{4,12},{5,13},{6,14},{7,15},{8,0},{9,1},... | collective-permute-start | bytes 344072 | tf_op jit(solution)/shard_map/ppermute | solution.py:464
  13.5 1.5 %collective-permute-start.11 = (s16[448,128]{1,0:T(8,128)(2,1)S(1)}, s16[448,128]{1,0:T(8,128)(2,1)S(1)}, u32[]{:S(2)}, u32[]{:S(2)}) collective-permute-start(s16[448,128]{1,0:T(8,128)(2,1)S(1)} %get-tuple-element.71), channel_id=1, source_target_pairs={{0,16},{1,17},{2,18},{3,19},{4,20},{5,21},{6,22},{7,23},{8,24},{9,... | collective-permute-start | bytes 344072 | tf_op jit(solution)/shard_map/ppermute | solution.py:464
  15.5 2.2 %collective-permute-done.10 = s16[448,128]{1,0:T(8,128)(2,1)S(1)} collective-permute-done((s16[448,128]{1,0:T(8,128)(2,1)S(1)}, s16[448,128]{1,0:T(8,128)(2,1)S(1)}, u32[]{:S(2)}, u32[]{:S(2)}) %collective-permute-start.10) | collective-permute-done | bytes 114720 | tf_op jit(solution)/shard_map/ppermute | solution.py:464
  17.8 1.6 %collective-permute-done.11 = s16[448,128]{1,0:T(8,128)(2,1)S(1)} collective-permute-done((s16[448,128]{1,0:T(8,128)(2,1)S(1)}, s16[448,128]{1,0:T(8,128)(2,1)S(1)}, u32[]{:S(2)}, u32[]{:S(2)}) %collective-permute-start.11) | collective-permute-done | bytes 114720 | tf_op jit(solution)/shard_map/ppermute | solution.py:464
  19.4 1.3 %collective-permute-done.12 = s16[448,128]{1,0:T(8,128)(2,1)S(1)} collective-permute-done((s16[448,128]{1,0:T(8,128)(2,1)S(1)}, s16[448,128]{1,0:T(8,128)(2,1)S(1)}, u32[]{:S(2)}, u32[]{:S(2)}) %collective-permute-start.12) | collective-permute-done | bytes 114720 | tf_op jit(solution)/shard_map/ppermute | solution.py:464
  22.6 2.0 %shard_map.58 = (f32[128,128]{1,0:T(8,128)S(1)}, bf16[128,128]{1,0:T(8,128)(2,1)S(1)}, f32[128,128]{1,0:T(8,128)S(1)}, f32[64,128]{1,0:T(8,128)S(1)}, s16[144,128]{1,0:T(8,128)(2,1)S(1)}) custom-call(s32[2]{0:T(128)S(1)} %pad_add_fusion.2.place, bf16[2560,256]{1,0:T(8,128)(2,1)S(1)} %get-tuple-element.73.known, f32[128,128]{1,0:T(8,128)S(1)} %get-tuple-element.74.seen_in, ...), custom_call_target="tpu_custom_call" | custom-call | flops 500000000 | bytes 2691080 | tf_op jit(solution)/shard_map/pallas_call | solution.py:35
  25.5 2.0 %collective-permute-start.15 = (s16[144,128]{1,0:T(8,128)(2,1)S(1)}, s16[144,128]{1,0:T(8,128)(2,1)S(1)}, u32[]{:S(2)}, u32[]{:S(2)}) collective-permute-start(s16[144,128]{1,0:T(8,128)(2,1)S(1)} %get-tuple-element.77.refs_0_), channel_id=1, source_target_pairs={{0,2},{1,3},{2,0},{3,1},{4,6},{5,7},{6,4},{7,5},{8,10},{9,11},{10,... | collective-permute-start | bytes 110600 | tf_op jit(solution)/shard_map/ppermute | solution.py:464
  27.5 1.7 %collective-permute-start.16 = (s16[144,128]{1,0:T(8,128)(2,1)S(1)}, s16[144,128]{1,0:T(8,128)(2,1)S(1)}, u32[]{:S(2)}, u32[]{:S(2)}) collective-permute-start(s16[144,128]{1,0:T(8,128)(2,1)S(1)} %get-tuple-element.77.refs_0_), channel_id=1, source_target_pairs={{0,3},{1,2},{2,1},{3,0},{4,7},{5,6},{6,5},{7,4},{8,11},{9,10},{10,... | collective-permute-start | bytes 110600 | tf_op jit(solution)/shard_map/ppermute | solution.py:464
  30.7 2.6 %collective-permute-done.16.refs_3_ = s16[144,128]{1,0:T(8,128)(2,1)S(1)} collective-permute-done((s16[144,128]{1,0:T(8,128)(2,1)S(1)}, s16[144,128]{1,0:T(8,128)(2,1)S(1)}, u32[]{:S(2)}, u32[]{:S(2)}) %collective-permute-start.16) | collective-permute-done | bytes 36896 | tf_op jit(solution)/shard_map/ppermute | solution.py:464
  33.9 1.5 %collective-permute-start.19 = (s16[528,128]{1,0:T(8,128)(2,1)S(1)}, s16[528,128]{1,0:T(8,128)(2,1)S(1)}, u32[]{:S(2)}, u32[]{:S(2)}) collective-permute-start(s16[528,128]{1,0:T(8,128)(2,1)S(1)} %shard_map.59), channel_id=1, source_target_pairs={{0,16},{1,17},{2,18},{3,19},{4,20},{5,21},{6,22},{7,23},{8,24},{9,... | collective-permute-start | bytes 405512 | tf_op jit(solution)/shard_map/ppermute | solution.py:464
  35.4 1.6 %collective-permute-start.20 = (s16[528,128]{1,0:T(8,128)(2,1)S(1)}, s16[528,128]{1,0:T(8,128)(2,1)S(1)}, u32[]{:S(2)}, u32[]{:S(2)}) collective-permute-start(s16[528,128]{1,0:T(8,128)(2,1)S(1)} %shard_map.59), channel_id=1, source_target_pairs={{0,8},{1,9},{2,10},{3,11},{4,12},{5,13},{6,14},{7,15},{8,0},{9,1},... | collective-permute-start | bytes 405512 | tf_op jit(solution)/shard_map/ppermute | solution.py:464
  37.0 3.1 %collective-permute-done.18 = s16[528,128]{1,0:T(8,128)(2,1)S(1)} collective-permute-done((s16[528,128]{1,0:T(8,128)(2,1)S(1)}, s16[528,128]{1,0:T(8,128)(2,1)S(1)}, u32[]{:S(2)}, u32[]{:S(2)}) %collective-permute-start.18) | collective-permute-done | bytes 135200 | tf_op jit(solution)/shard_map/ppermute | solution.py:464
  41.4 1.2 %collective-permute-done.21.rest = f32[128,128]{1,0:T(8,128)S(1)} collective-permute-done((f32[128,128]{1,0:T(8,128)S(1)}, f32[128,128]{1,0:T(8,128)S(1)}, u32[]{:S(2)}, u32[]{:S(2)}) %collective-permute-start.21) | collective-permute-done | bytes 65568 | tf_op jit(solution)/shard_map/ppermute | solution.py:464
  44.0 1.6 %collective-permute-start.23 = (s16[80,128]{1,0:T(8,128)(2,1)S(1)}, s16[80,128]{1,0:T(8,128)(2,1)S(1)}, u32[]{:S(2)}, u32[]{:S(2)}) collective-permute-start(s16[80,128]{1,0:T(8,128)(2,1)S(1)} %get-tuple-element.98), channel_id=1, source_target_pairs={{0,6},{1,7},{2,4},{3,5},{4,2},{5,3},{6,0},{7,1},{8,14},{9,15},{10,... | collective-permute-start | bytes 61448 | tf_op jit(solution)/shard_map/ppermute | solution.py:464
  45.6 1.9 %collective-permute-start.24 = (s16[80,128]{1,0:T(8,128)(2,1)S(1)}, s16[80,128]{1,0:T(8,128)(2,1)S(1)}, u32[]{:S(2)}, u32[]{:S(2)}) collective-permute-start(s16[80,128]{1,0:T(8,128)(2,1)S(1)} %get-tuple-element.99), channel_id=1, source_target_pairs={{0,7},{1,6},{2,5},{3,4},{4,3},{5,2},{6,1},{7,0},{8,15},{9,14},{10,... | collective-permute-start | bytes 61448 | tf_op jit(solution)/shard_map/ppermute | solution.py:464
  47.5 1.8 %shard_map.64 = (f32[1024,128]{1,0:T(8,128)S(1)}, f32[8,128]{1,0:T(8,128)S(1)}) custom-call(s32[2]{0:T(128)S(1)} %pad_add_fusion.2.place, s16[2112,128]{1,0:T(8,128)(2,1)S(1)} %constant_dynamic-update-slice_fusion.4.block), custom_call_target="tpu_custom_call" | custom-call | flops 2000000000 | bytes 1069064 | tf_op jit(solution)/shard_map/pallas_call | solution.py:35
  50.6 1.5 %collective-permute-start.26 = (s16[272,128]{1,0:T(8,128)(2,1)S(1)}, s16[272,128]{1,0:T(8,128)(2,1)S(1)}, u32[]{:S(2)}, u32[]{:S(2)}) collective-permute-start(s16[272,128]{1,0:T(8,128)(2,1)S(1)} %shard_map.63), channel_id=1, source_target_pairs={{0,28},{1,29},{2,30},{3,31},{4,24},{5,25},{6,26},{7,27},{8,20},{9,... | collective-permute-start | bytes 208904 | tf_op jit(solution)/shard_map/ppermute | solution.py:464
  53.9 1.9 %shard_map.65 = (f32[64,2048]{1,0:T(8,128)S(1)}, s32[1]{0:T(128)}) custom-call(s32[2]{0:T(128)S(1)} %pad_add_fusion.2.place, f32[64,2048]{1,0:T(8,128)S(1)} %copy-done, f32[1024,128]{1,0:T(8,128)S(1)} %get-tuple-element.104.part, s16[2112,128]{1,0:T(8,128)(2,1)S(1)} %collective-permute-done.25.block, f32[8,128]{1,0:T(8,128)S(1)} %get-tuple-element.106.refs_0_), custom_call_target="tpu_custom_call" | custom-call | flops 2000000000 | bytes 2117644 | tf_op jit(solution)/shard_map/pallas_call | solution.py:35
  57.7 1.3 %shard_map.66 = f32[1024,128]{1,0:T(8,128)S(1)} custom-call(s32[2]{0:T(128)S(1)} %pad_add_fusion.2.place, s16[1088,128]{1,0:T(8,128)(2,1)S(1)} %pad_add_fusion.1.block), custom_call_target="tpu_custom_call" | custom-call | flops 2000000000 | bytes 802824 | tf_op jit(solution)/shard_map/pallas_call | solution.py:35
  59.2 2.1 %shard_map.67 = f32[64,2048]{1,0:T(8,128)} custom-call(s32[2]{0:T(128)S(1)} %pad_add_fusion.2.place, f32[64,2048]{1,0:T(8,128)S(1)} %get-tuple-element.109.image, f32[1024,128]{1,0:T(8,128)S(1)} %get-tuple-element.113.part, s16[1088,128]{1,0:T(8,128)(2,1)S(1)} %get-tuple-element.114.block), custom_call_target="tpu_custom_call" | custom-call | flops 2000000000 | bytes 1851400 | tf_op jit(solution)/shard_map/pallas_call | solution.py:35
  (50 shorter events, 13.2 us)
Async XLA Ops:
  0.0 20.8 %copy-start.1 = (bf16[2,1,256,256]{3,2,1,0:T(8,128)(2,1)S(1)}, bf16[2,1,256,256]{3,2,1,0:T(8,128)(2,1)}, u32[]{:S(2)}) copy-start(bf16[2,1,256,256]{3,2,1,0:T(8,128)(2,1)} %param.11) | copy-start | bytes 786436
  1.8 7.3 %collective-permute-start.7 = (s16[192,128]{1,0:T(8,128)(2,1)S(1)}, s16[192,128]{1,0:T(8,128)(2,1)S(1)}, u32[]{:S(2)}, u32[]{:S(2)}) collective-permute-start(s16[192,128]{1,0:T(8,128)(2,1)S(1)} %get-tuple-element.65), channel_id=1, source_target_pairs={{0,3},{1,2},{2,1},{3,0},{4,7},{5,6},{6,5},{7,4},{8,11},{9,10},{10,... | collective-permute-start | bytes 147464 | tf_op jit(solution)/shard_map/ppermute | solution.py:464
  6.9 5.0 %collective-permute-start.8 = (s16[192,128]{1,0:T(8,128)(2,1)S(1)}, s16[192,128]{1,0:T(8,128)(2,1)S(1)}, u32[]{:S(2)}, u32[]{:S(2)}) collective-permute-start(s16[192,128]{1,0:T(8,128)(2,1)S(1)} %get-tuple-element.66), channel_id=1, source_target_pairs={{0,2},{1,3},{2,0},{3,1},{4,6},{5,7},{6,4},{7,5},{8,10},{9,11},{10,... | collective-permute-start | bytes 147464 | tf_op jit(solution)/shard_map/ppermute | solution.py:464
  6.9 5.0 %collective-permute-start.9 = (s16[192,128]{1,0:T(8,128)(2,1)S(1)}, s16[192,128]{1,0:T(8,128)(2,1)S(1)}, u32[]{:S(2)}, u32[]{:S(2)}) collective-permute-start(s16[192,128]{1,0:T(8,128)(2,1)S(1)} %get-tuple-element.67), channel_id=1, source_target_pairs={{0,1},{1,0},{2,3},{3,2},{4,5},{5,4},{6,7},{7,6},{8,9},{9,8},{10,11... | collective-permute-start | bytes 147464 | tf_op jit(solution)/shard_map/ppermute | solution.py:464
  12.0 5.8 %collective-permute-start.10 = (s16[448,128]{1,0:T(8,128)(2,1)S(1)}, s16[448,128]{1,0:T(8,128)(2,1)S(1)}, u32[]{:S(2)}, u32[]{:S(2)}) collective-permute-start(s16[448,128]{1,0:T(8,128)(2,1)S(1)} %get-tuple-element.70), channel_id=1, source_target_pairs={{0,8},{1,9},{2,10},{3,11},{4,12},{5,13},{6,14},{7,15},{8,0},{9,1},... | collective-permute-start | bytes 344072 | tf_op jit(solution)/shard_map/ppermute | solution.py:464
  13.5 5.9 %collective-permute-start.11 = (s16[448,128]{1,0:T(8,128)(2,1)S(1)}, s16[448,128]{1,0:T(8,128)(2,1)S(1)}, u32[]{:S(2)}, u32[]{:S(2)}) collective-permute-start(s16[448,128]{1,0:T(8,128)(2,1)S(1)} %get-tuple-element.71), channel_id=1, source_target_pairs={{0,16},{1,17},{2,18},{3,19},{4,20},{5,21},{6,22},{7,23},{8,24},{9,... | collective-permute-start | bytes 344072 | tf_op jit(solution)/shard_map/ppermute | solution.py:464
  15.0 5.7 %collective-permute-start.12 = (s16[448,128]{1,0:T(8,128)(2,1)S(1)}, s16[448,128]{1,0:T(8,128)(2,1)S(1)}, u32[]{:S(2)}, u32[]{:S(2)}) collective-permute-start(s16[448,128]{1,0:T(8,128)(2,1)S(1)} %get-tuple-element.72), channel_id=1, source_target_pairs={{0,24},{1,25},{2,26},{3,27},{4,28},{5,29},{6,30},{7,31},{8,16},{9,... | collective-permute-start | bytes 344072 | tf_op jit(solution)/shard_map/ppermute | solution.py:464
  20.7 1.9 %collective-permute-start.13 = (s16[1792,128]{1,0:T(8,128)(2,1)S(1)}, s16[1792,128]{1,0:T(8,128)(2,1)S(1)}, u32[]{:S(2)}, u32[]{:S(2)}) collective-permute-start(s16[1792,128]{1,0:T(8,128)(2,1)S(1)} %constant_dynamic-update-slice_fusion.mine), channel_id=1, source_target_pairs={{0,4},{1,5},{2,6},{3,7},{4,0},{5,1},{6,2},{7,3},{8,12},{9,13},{10,... | collective-permute-start | bytes 1376264 | tf_op jit(solution)/shard_map/ppermute | solution.py:464
  24.7 8.7 %collective-permute-start.17 = (f32[128,128]{1,0:T(8,128)S(1)}, f32[128,128]{1,0:T(8,128)S(1)}, u32[]{:S(2)}, u32[]{:S(2)}) collective-permute-start(f32[128,128]{1,0:T(8,128)S(1)} %get-tuple-element.81.refs), channel_id=1, source_target_pairs={{0,4},{1,5},{2,6},{3,7},{4,0},{5,1},{6,2},{7,3},{8,12},{9,13},{10,... | collective-permute-start | bytes 196616 | tf_op jit(solution)/shard_map/ppermute | solution.py:464
  24.9 5.3 %collective-permute-start.14 = (s16[144,128]{1,0:T(8,128)(2,1)S(1)}, s16[144,128]{1,0:T(8,128)(2,1)S(1)}, u32[]{:S(2)}, u32[]{:S(2)}) collective-permute-start(s16[144,128]{1,0:T(8,128)(2,1)S(1)} %get-tuple-element.77.refs_0_), channel_id=1, source_target_pairs={{0,1},{1,0},{2,3},{3,2},{4,5},{5,4},{6,7},{7,6},{8,9},{9,8},{10,11... | collective-permute-start | bytes 110600 | tf_op jit(solution)/shard_map/ppermute | solution.py:464
  25.5 5.2 %collective-permute-start.15 = (s16[144,128]{1,0:T(8,128)(2,1)S(1)}, s16[144,128]{1,0:T(8,128)(2,1)S(1)}, u32[]{:S(2)}, u32[]{:S(2)}) collective-permute-start(s16[144,128]{1,0:T(8,128)(2,1)S(1)} %get-tuple-element.77.refs_0_), channel_id=1, source_target_pairs={{0,2},{1,3},{2,0},{3,1},{4,6},{5,7},{6,4},{7,5},{8,10},{9,11},{10,... | collective-permute-start | bytes 110600 | tf_op jit(solution)/shard_map/ppermute | solution.py:464
  27.5 5.8 %collective-permute-start.16 = (s16[144,128]{1,0:T(8,128)(2,1)S(1)}, s16[144,128]{1,0:T(8,128)(2,1)S(1)}, u32[]{:S(2)}, u32[]{:S(2)}) collective-permute-start(s16[144,128]{1,0:T(8,128)(2,1)S(1)} %get-tuple-element.77.refs_0_), channel_id=1, source_target_pairs={{0,3},{1,2},{2,1},{3,0},{4,7},{5,6},{6,5},{7,4},{8,11},{9,10},{10,... | collective-permute-start | bytes 110600 | tf_op jit(solution)/shard_map/ppermute | solution.py:464
  33.3 6.7 %collective-permute-start.18 = (s16[528,128]{1,0:T(8,128)(2,1)S(1)}, s16[528,128]{1,0:T(8,128)(2,1)S(1)}, u32[]{:S(2)}, u32[]{:S(2)}) collective-permute-start(s16[528,128]{1,0:T(8,128)(2,1)S(1)} %shard_map.59), channel_id=1, source_target_pairs={{0,24},{1,25},{2,26},{3,27},{4,28},{5,29},{6,30},{7,31},{8,16},{9,... | collective-permute-start | bytes 405512 | tf_op jit(solution)/shard_map/ppermute | solution.py:464
  33.9 6.8 %collective-permute-start.19 = (s16[528,128]{1,0:T(8,128)(2,1)S(1)}, s16[528,128]{1,0:T(8,128)(2,1)S(1)}, u32[]{:S(2)}, u32[]{:S(2)}) collective-permute-start(s16[528,128]{1,0:T(8,128)(2,1)S(1)} %shard_map.59), channel_id=1, source_target_pairs={{0,16},{1,17},{2,18},{3,19},{4,20},{5,21},{6,22},{7,23},{8,24},{9,... | collective-permute-start | bytes 405512 | tf_op jit(solution)/shard_map/ppermute | solution.py:464
  35.4 5.4 %collective-permute-start.20 = (s16[528,128]{1,0:T(8,128)(2,1)S(1)}, s16[528,128]{1,0:T(8,128)(2,1)S(1)}, u32[]{:S(2)}, u32[]{:S(2)}) collective-permute-start(s16[528,128]{1,0:T(8,128)(2,1)S(1)} %shard_map.59), channel_id=1, source_target_pairs={{0,8},{1,9},{2,10},{3,11},{4,12},{5,13},{6,14},{7,15},{8,0},{9,1},... | collective-permute-start | bytes 405512 | tf_op jit(solution)/shard_map/ppermute | solution.py:464
  41.3 1.3 %collective-permute-start.21 = (f32[128,128]{1,0:T(8,128)S(1)}, f32[128,128]{1,0:T(8,128)S(1)}, u32[]{:S(2)}, u32[]{:S(2)}) collective-permute-start(f32[128,128]{1,0:T(8,128)S(1)} %get-tuple-element.88), channel_id=1, source_target_pairs={{0,4},{1,5},{2,6},{3,7},{4,0},{5,1},{6,2},{7,3},{8,12},{9,13},{10,... | collective-permute-start | bytes 196616 | tf_op jit(solution)/shard_map/ppermute | solution.py:464
  43.3 7.3 %collective-permute-start.25 = (s16[2112,128]{1,0:T(8,128)(2,1)S(1)}, s16[2112,128]{1,0:T(8,128)(2,1)S(1)}, u32[]{:S(2)}, u32[]{:S(2)}) collective-permute-start(s16[2112,128]{1,0:T(8,128)(2,1)S(1)} %constant_dynamic-update-slice_fusion.4.block), channel_id=1, source_target_pairs={{0,4},{1,5},{2,6},{3,7},{4,0},{5,1},{6,2},{7,3},{8,12},{9,13},{10,... | collective-permute-start | bytes 1622024 | tf_op jit(solution)/shard_map/ppermute | solution.py:464
  43.4 5.9 %collective-permute-start.22 = (s16[80,128]{1,0:T(8,128)(2,1)S(1)}, s16[80,128]{1,0:T(8,128)(2,1)S(1)}, u32[]{:S(2)}, u32[]{:S(2)}) collective-permute-start(s16[80,128]{1,0:T(8,128)(2,1)S(1)} %get-tuple-element.97), channel_id=1, source_target_pairs={{0,5},{1,4},{2,7},{3,6},{4,1},{5,0},{6,3},{7,2},{8,13},{9,12},{10,... | collective-permute-start | bytes 61448 | tf_op jit(solution)/shard_map/ppermute | solution.py:464
  44.0 5.4 %collective-permute-start.23 = (s16[80,128]{1,0:T(8,128)(2,1)S(1)}, s16[80,128]{1,0:T(8,128)(2,1)S(1)}, u32[]{:S(2)}, u32[]{:S(2)}) collective-permute-start(s16[80,128]{1,0:T(8,128)(2,1)S(1)} %get-tuple-element.98), channel_id=1, source_target_pairs={{0,6},{1,7},{2,4},{3,5},{4,2},{5,3},{6,0},{7,1},{8,14},{9,15},{10,... | collective-permute-start | bytes 61448 | tf_op jit(solution)/shard_map/ppermute | solution.py:464
  45.6 5.0 %collective-permute-start.24 = (s16[80,128]{1,0:T(8,128)(2,1)S(1)}, s16[80,128]{1,0:T(8,128)(2,1)S(1)}, u32[]{:S(2)}, u32[]{:S(2)}) collective-permute-start(s16[80,128]{1,0:T(8,128)(2,1)S(1)} %get-tuple-element.99), channel_id=1, source_target_pairs={{0,7},{1,6},{2,5},{3,4},{4,3},{5,2},{6,1},{7,0},{8,15},{9,14},{10,... | collective-permute-start | bytes 61448 | tf_op jit(solution)/shard_map/ppermute | solution.py:464
  50.6 5.7 %collective-permute-start.26 = (s16[272,128]{1,0:T(8,128)(2,1)S(1)}, s16[272,128]{1,0:T(8,128)(2,1)S(1)}, u32[]{:S(2)}, u32[]{:S(2)}) collective-permute-start(s16[272,128]{1,0:T(8,128)(2,1)S(1)} %shard_map.63), channel_id=1, source_target_pairs={{0,28},{1,29},{2,30},{3,31},{4,24},{5,25},{6,26},{7,27},{8,20},{9,... | collective-permute-start | bytes 208904 | tf_op jit(solution)/shard_map/ppermute | solution.py:464
  52.2 5.4 %collective-permute-start.27 = (s16[272,128]{1,0:T(8,128)(2,1)S(1)}, s16[272,128]{1,0:T(8,128)(2,1)S(1)}, u32[]{:S(2)}, u32[]{:S(2)}) collective-permute-start(s16[272,128]{1,0:T(8,128)(2,1)S(1)} %shard_map.63), channel_id=1, source_target_pairs={{0,20},{1,21},{2,22},{3,23},{4,16},{5,17},{6,18},{7,19},{8,28},{9,... | collective-permute-start | bytes 208904 | tf_op jit(solution)/shard_map/ppermute | solution.py:464
  53.0 4.5 %collective-permute-start.28 = (s16[272,128]{1,0:T(8,128)(2,1)S(1)}, s16[272,128]{1,0:T(8,128)(2,1)S(1)}, u32[]{:S(2)}, u32[]{:S(2)}) collective-permute-start(s16[272,128]{1,0:T(8,128)(2,1)S(1)} %shard_map.63), channel_id=1, source_target_pairs={{0,12},{1,13},{2,14},{3,15},{4,8},{5,9},{6,10},{7,11},{8,4},{9,5},... | collective-permute-start | bytes 208904 | tf_op jit(solution)/shard_map/ppermute | solution.py:464
  57.6 1.6 %collective-permute-start.29 = (s16[1088,128]{1,0:T(8,128)(2,1)S(1)}, s16[1088,128]{1,0:T(8,128)(2,1)S(1)}, u32[]{:S(2)}, u32[]{:S(2)}) collective-permute-start(s16[1088,128]{1,0:T(8,128)(2,1)S(1)} %pad_add_fusion.1.block), channel_id=1, source_target_pairs={{0,4},{1,5},{2,6},{3,7},{4,0},{5,1},{6,2},{7,3},{8,12},{9,13},{10,... | collective-permute-start | bytes 835592 | tf_op jit(solution)/shard_map/ppermute | solution.py:464
  (1 other events, 20.8 us)

commit v6 on v5

--- a/solution.py
+++ b/solution.py
@@ -24,16 +24,21 @@
 VMEM_LIMIT = 48 * 1024 * 1024
 
 
-def call(kernel, outs, args, flops, smem=0, hbm=0, scratch=(), scalars=0):
-    spaces = [pl.BlockSpec(memory_space=pltpu.SMEM)] * smem
-    spaces += [pl.BlockSpec(memory_space=pltpu.HBM)] * hbm
-    spaces += [pl.BlockSpec(memory_space=pltpu.VMEM)] * (len(args) - smem - hbm)
+def call(kernel, outs, args, flops, placed=False, hbm=0, scratch=(), scalars=0):
+    spaces = [pl.BlockSpec(memory_space=pltpu.HBM)] * hbm
+    spaces += [pl.BlockSpec(memory_space=pltpu.VMEM)] * (len(args) - hbm)
     moved = sum(a.size * a.dtype.itemsize for a in list(args) + list(outs))
     args = list(args)
-    for i in range(smem, smem + hbm):
+    for i in range(hbm):
         args[i] = pltpu.with_memory_space_constraint(args[i], pltpu.HBM)
+    body = kernel
+    if placed:
+
+        def body(*refs):
+            kernel((lax.axis_index("chan"), lax.axis_index("facet")), *refs)
+
     return pl.pallas_call(
-        kernel,
+        body,
         out_shape=list(outs),
         in_specs=spaces,
         out_specs=[pl.BlockSpec(memory_space=pltpu.VMEM)] * (len(outs) - scalars)
@@ -472,7 +477,6 @@
     piece = per_facet // C
     chips = C // 2
     step = float(per_facet * F / (2.5 * C * F * (L * C) * F))
-    place = jnp.stack([lax.axis_index("chan"), lax.axis_index("facet")]).astype(I32)
     kernels = uv_kernels[:, 0]
 
     blocks = jax.ShapeDtypeStruct((chips * BLOCK, STRIP), I16)
@@ -481,14 +485,13 @@
         functools.partial(pack_kernel, C, F, L),
         [blocks] + [both] * (F - 1),
         [
-            place,
             start_image,
             visibilities[0],
             strip_index[0].transpose(1, 2, 0),
             live_counts[0].T,
         ],
         10**8,
-        smem=1,
+        placed=True,
         hbm=4,
         scratch=[
             pltpu.VMEM((start_image.shape[0] // C, start_image.shape[1]), F32),
@@ -523,9 +526,9 @@
             jax.ShapeDtypeStruct(((TERMS + 1) * C * F, 2 * STRIP), F32),
             jax.ShapeDtypeStruct(kernels.shape, BF16),
         ],
-        [place, start_image, kernels, mine],
+        [start_image, kernels, mine],
         10**8,
-        smem=1,
+        placed=True,
     )
     est, observed, at, live, msg = call(
         functools.partial(first_kernel, C, F, L),
@@ -536,9 +539,9 @@
             jax.ShapeDtypeStruct((L * C * F, STRIP), F32),
             message,
         ],
-        [place, known, seen_part, whole_part, kernels, turned, other],
+        [known, seen_part, whole_part, kernels, turned, other],
         5 * 10**8,
-        smem=1,
+        placed=True,
     )
 
     def along_facet(msgs, cross=0):
@@ -560,9 +563,9 @@
         return call(
             functools.partial(facet_part_kernel, F, chips),
             [facet_strips, *crowd],
-            [place, mine],
+            [mine],
             2 * 10**9,
-            smem=1,
+            placed=True,
         )
 
     settle = functools.partial(settle_kernel, F, chips, step)
@@ -575,9 +578,9 @@
             jax.ShapeDtypeStruct((F * PART, refs), BF16),
             jax.ShapeDtypeStruct((F * EXTRA, STRIP), F32),
         ],
-        [place, at],
+        [at],
         10**8,
-        smem=1,
+        placed=True,
     )
     near, pick, numbers, at, other_at = lax.optimization_barrier(
         (near, pick, numbers, at, swap(at, 1))
@@ -604,9 +607,9 @@
     image, crowd = call(
         settle,
         [whole, jax.ShapeDtypeStruct((1,), I32)],
-        [place, start_image, part, other, crowd],
+        [start_image, part, other, crowd],
         2 * 10**9,
-        smem=1,
+        placed=True,
         scalars=1,
     )
     crowded = crowd[0] > PART
@@ -625,9 +628,9 @@
     return call(
         settle,
         [whole],
-        [place, image, part, other],
+        [image, part, other],
         2 * 10**9,
-        smem=1,
+        placed=True,
     )[0]
 
 

time: 61.4 us -> 59.8 us (0.974)
  Pallas kernels: 14.1 us -> 9.86 us
  waiting for transfers between devices: 20.8 us -> 23.5 us
    pallas_call x13, Pallas kernels: 14.1 us -> 9.86 us  [call(): pl.pallas_call(body, out_shape=list(outs), in_specs=spaces, out_specs=[pl...]
    ppermute x23, waiting for transfers between devices: 20.8 us -> 23.5 us  [swap(): return lax.ppermute(x, ('chan', 'facet'), pairs)]
  transfers between devices with their start and end apart: 23 -> 23, of which waited for: 15 -> 15; matrix products, arithmetic and copies ran while one was open for 0% -> 0% of each run, Pallas kernels for 12% -> 7%
where the time goes in v6:
time: 59.8 us; the launch traced here: 59.6 us
  starting transfers between devices  25.3 us (42%)
  waiting for transfers between devices  23.5 us (39%)
  Pallas kernels  9.86 us (16%)
  between operations  0.84 us (1%)
    ppermute x23, starting transfers between devices, swap(): return lax.ppermute(x, ('chan', 'facet'), pairs)  25.3 us
    ppermute x23, waiting for transfers between devices, swap(): return lax.ppermute(x, ('chan', 'facet'), pairs)  23.5 us
    pallas_call x13, Pallas kernels, call(): pl.pallas_call(body, out_shape=list(outs), in_specs=spaces, out_specs=[pl...  9.86 us
  transfers between devices with their start and end apart: 23, of which 15 were waited for; matrix products, arithmetic and copies ran while one was open for 0% of the time, Pallas kernels for 7%

profile of v6, /device:TPU:0, one launch (start us, length us, event | category | flops | bytes accessed | tf_op | source)
XLA Modules:
  0.0 59.6 jit_solution(8004011712529527872)
XLA Ops:
  1.3 5.1 %collective-permute-start.7 = (s16[192,128]{1,0:T(8,128)(2,1)S(1)}, s16[192,128]{1,0:T(8,128)(2,1)S(1)}, u32[]{:S(2)}, u32[]{:S(2)}) collective-permute-start(s16[192,128]{1,0:T(8,128)(2,1)S(1)} %get-tuple-element.60), channel_id=1, source_target_pairs={{0,3},{1,2},{2,1},{3,0},{4,7},{5,6},{6,5},{7,4},{8,11},{9,10},{10,... | collective-permute-start | bytes 147464 | tf_op jit(solution)/shard_map/ppermute | solution.py:469
  7.0 1.6 %collective-permute-done.7.refs_0_ = s16[192,128]{1,0:T(8,128)(2,1)S(1)} collective-permute-done((s16[192,128]{1,0:T(8,128)(2,1)S(1)}, s16[192,128]{1,0:T(8,128)(2,1)S(1)}, u32[]{:S(2)}, u32[]{:S(2)}) %collective-permute-start.7) | collective-permute-done | bytes 49184 | tf_op jit(solution)/shard_map/ppermute | solution.py:469
  8.6 2.8 %collective-permute-done.8.refs_1_ = s16[192,128]{1,0:T(8,128)(2,1)S(1)} collective-permute-done((s16[192,128]{1,0:T(8,128)(2,1)S(1)}, s16[192,128]{1,0:T(8,128)(2,1)S(1)}, u32[]{:S(2)}, u32[]{:S(2)}) %collective-permute-start.8) | collective-permute-done | bytes 49184 | tf_op jit(solution)/shard_map/ppermute | solution.py:469
  11.4 1.6 %collective-permute-start.10 = (s16[448,128]{1,0:T(8,128)(2,1)S(1)}, s16[448,128]{1,0:T(8,128)(2,1)S(1)}, u32[]{:S(2)}, u32[]{:S(2)}) collective-permute-start(s16[448,128]{1,0:T(8,128)(2,1)S(1)} %get-tuple-element.65), channel_id=1, source_target_pairs={{0,8},{1,9},{2,10},{3,11},{4,12},{5,13},{6,14},{7,15},{8,0},{9,1},... | collective-permute-start | bytes 344072 | tf_op jit(solution)/shard_map/ppermute | solution.py:469
  13.0 1.5 %collective-permute-start.11 = (s16[448,128]{1,0:T(8,128)(2,1)S(1)}, s16[448,128]{1,0:T(8,128)(2,1)S(1)}, u32[]{:S(2)}, u32[]{:S(2)}) collective-permute-start(s16[448,128]{1,0:T(8,128)(2,1)S(1)} %get-tuple-element.66), channel_id=1, source_target_pairs={{0,16},{1,17},{2,18},{3,19},{4,20},{5,21},{6,22},{7,23},{8,24},{9,... | collective-permute-start | bytes 344072 | tf_op jit(solution)/shard_map/ppermute | solution.py:469
  15.0 2.2 %collective-permute-done.10 = s16[448,128]{1,0:T(8,128)(2,1)S(1)} collective-permute-done((s16[448,128]{1,0:T(8,128)(2,1)S(1)}, s16[448,128]{1,0:T(8,128)(2,1)S(1)}, u32[]{:S(2)}, u32[]{:S(2)}) %collective-permute-start.10) | collective-permute-done | bytes 114720 | tf_op jit(solution)/shard_map/ppermute | solution.py:469
  17.2 1.6 %collective-permute-done.11 = s16[448,128]{1,0:T(8,128)(2,1)S(1)} collective-permute-done((s16[448,128]{1,0:T(8,128)(2,1)S(1)}, s16[448,128]{1,0:T(8,128)(2,1)S(1)}, u32[]{:S(2)}, u32[]{:S(2)}) %collective-permute-start.11) | collective-permute-done | bytes 114720 | tf_op jit(solution)/shard_map/ppermute | solution.py:469
  18.9 1.3 %collective-permute-done.12 = s16[448,128]{1,0:T(8,128)(2,1)S(1)} collective-permute-done((s16[448,128]{1,0:T(8,128)(2,1)S(1)}, s16[448,128]{1,0:T(8,128)(2,1)S(1)}, u32[]{:S(2)}, u32[]{:S(2)}) %collective-permute-start.12) | collective-permute-done | bytes 114720 | tf_op jit(solution)/shard_map/ppermute | solution.py:469
  22.1 1.5 %shard_map.58 = (f32[128,128]{1,0:T(8,128)S(1)}, bf16[128,128]{1,0:T(8,128)(2,1)S(1)}, f32[128,128]{1,0:T(8,128)S(1)}, f32[64,128]{1,0:T(8,128)S(1)}, s16[144,128]{1,0:T(8,128)(2,1)S(1)}) custom-call(bf16[2560,256]{1,0:T(8,128)(2,1)S(1)} %get-tuple-element.68.refs_0_, f32[128,128]{1,0:T(8,128)S(1)} %get-tuple-element.69.refs_1_, ...), custom_call_target="tpu_custom_call" | custom-call | flops 500000000 | bytes 2691072 | tf_op jit(solution)/shard_map/pallas_call | solution.py:40
  24.4 2.0 %collective-permute-start.15 = (s16[144,128]{1,0:T(8,128)(2,1)S(1)}, s16[144,128]{1,0:T(8,128)(2,1)S(1)}, u32[]{:S(2)}, u32[]{:S(2)}) collective-permute-start(s16[144,128]{1,0:T(8,128)(2,1)S(1)} %get-tuple-element.72.refs_0_), channel_id=1, source_target_pairs={{0,2},{1,3},{2,0},{3,1},{4,6},{5,7},{6,4},{7,5},{8,10},{9,11},{10,... | collective-permute-start | bytes 110600 | tf_op jit(solution)/shard_map/ppermute | solution.py:469
  26.5 1.7 %collective-permute-start.16 = (s16[144,128]{1,0:T(8,128)(2,1)S(1)}, s16[144,128]{1,0:T(8,128)(2,1)S(1)}, u32[]{:S(2)}, u32[]{:S(2)}) collective-permute-start(s16[144,128]{1,0:T(8,128)(2,1)S(1)} %get-tuple-element.72.refs_0_), channel_id=1, source_target_pairs={{0,3},{1,2},{2,1},{3,0},{4,7},{5,6},{6,5},{7,4},{8,11},{9,10},{10,... | collective-permute-start | bytes 110600 | tf_op jit(solution)/shard_map/ppermute | solution.py:469
  29.6 2.6 %collective-permute-done.16.refs_3_ = s16[144,128]{1,0:T(8,128)(2,1)S(1)} collective-permute-done((s16[144,128]{1,0:T(8,128)(2,1)S(1)}, s16[144,128]{1,0:T(8,128)(2,1)S(1)}, u32[]{:S(2)}, u32[]{:S(2)}) %collective-permute-start.16) | collective-permute-done | bytes 36896 | tf_op jit(solution)/shard_map/ppermute | solution.py:469
  32.8 1.5 %collective-permute-start.19 = (s16[528,128]{1,0:T(8,128)(2,1)S(1)}, s16[528,128]{1,0:T(8,128)(2,1)S(1)}, u32[]{:S(2)}, u32[]{:S(2)}) collective-permute-start(s16[528,128]{1,0:T(8,128)(2,1)S(1)} %shard_map.59), channel_id=1, source_target_pairs={{0,16},{1,17},{2,18},{3,19},{4,20},{5,21},{6,22},{7,23},{8,24},{9,... | collective-permute-start | bytes 405512 | tf_op jit(solution)/shard_map/ppermute | solution.py:469
  34.3 1.6 %collective-permute-start.20 = (s16[528,128]{1,0:T(8,128)(2,1)S(1)}, s16[528,128]{1,0:T(8,128)(2,1)S(1)}, u32[]{:S(2)}, u32[]{:S(2)}) collective-permute-start(s16[528,128]{1,0:T(8,128)(2,1)S(1)} %shard_map.59), channel_id=1, source_target_pairs={{0,8},{1,9},{2,10},{3,11},{4,12},{5,13},{6,14},{7,15},{8,0},{9,1},... | collective-permute-start | bytes 405512 | tf_op jit(solution)/shard_map/ppermute | solution.py:469
  35.9 3.1 %collective-permute-done.18 = s16[528,128]{1,0:T(8,128)(2,1)S(1)} collective-permute-done((s16[528,128]{1,0:T(8,128)(2,1)S(1)}, s16[528,128]{1,0:T(8,128)(2,1)S(1)}, u32[]{:S(2)}, u32[]{:S(2)}) %collective-permute-start.18) | collective-permute-done | bytes 135200 | tf_op jit(solution)/shard_map/ppermute | solution.py:469
  40.3 1.2 %collective-permute-done.21.rest = f32[128,128]{1,0:T(8,128)S(1)} collective-permute-done((f32[128,128]{1,0:T(8,128)S(1)}, f32[128,128]{1,0:T(8,128)S(1)}, u32[]{:S(2)}, u32[]{:S(2)}) %collective-permute-start.21) | collective-permute-done | bytes 65568 | tf_op jit(solution)/shard_map/ppermute | solution.py:469
  42.9 1.6 %collective-permute-start.23 = (s16[80,128]{1,0:T(8,128)(2,1)S(1)}, s16[80,128]{1,0:T(8,128)(2,1)S(1)}, u32[]{:S(2)}, u32[]{:S(2)}) collective-permute-start(s16[80,128]{1,0:T(8,128)(2,1)S(1)} %get-tuple-element.93), channel_id=1, source_target_pairs={{0,6},{1,7},{2,4},{3,5},{4,2},{5,3},{6,0},{7,1},{8,14},{9,15},{10,... | collective-permute-start | bytes 61448 | tf_op jit(solution)/shard_map/ppermute | solution.py:469
  44.5 1.9 %collective-permute-start.24 = (s16[80,128]{1,0:T(8,128)(2,1)S(1)}, s16[80,128]{1,0:T(8,128)(2,1)S(1)}, u32[]{:S(2)}, u32[]{:S(2)}) collective-permute-start(s16[80,128]{1,0:T(8,128)(2,1)S(1)} %get-tuple-element.94), channel_id=1, source_target_pairs={{0,7},{1,6},{2,5},{3,4},{4,3},{5,2},{6,1},{7,0},{8,15},{9,14},{10,... | collective-permute-start | bytes 61448 | tf_op jit(solution)/shard_map/ppermute | solution.py:469
  46.4 1.3 %shard_map.64 = (f32[1024,128]{1,0:T(8,128)S(1)}, f32[8,128]{1,0:T(8,128)S(1)}) custom-call(s16[2112,128]{1,0:T(8,128)(2,1)S(1)} %constant_dynamic-update-slice_fusion.4.block.refs_0_), custom_call_target="tpu_custom_call" | custom-call | flops 2000000000 | bytes 1069056 | tf_op jit(solution)/shard_map/pallas_call | solution.py:40
  47.7 1.8 %collective-permute-done.24.refs_3_ = s16[80,128]{1,0:T(8,128)(2,1)S(1)} collective-permute-done((s16[80,128]{1,0:T(8,128)(2,1)S(1)}, s16[80,128]{1,0:T(8,128)(2,1)S(1)}, u32[]{:S(2)}, u32[]{:S(2)}) %collective-permute-start.24) | collective-permute-done | bytes 20512 | tf_op jit(solution)/shard_map/ppermute | solution.py:469
  49.5 1.5 %collective-permute-start.26 = (s16[272,128]{1,0:T(8,128)(2,1)S(1)}, s16[272,128]{1,0:T(8,128)(2,1)S(1)}, u32[]{:S(2)}, u32[]{:S(2)}) collective-permute-start(s16[272,128]{1,0:T(8,128)(2,1)S(1)} %shard_map.63), channel_id=1, source_target_pairs={{0,28},{1,29},{2,30},{3,31},{4,24},{5,25},{6,26},{7,27},{8,20},{9,... | collective-permute-start | bytes 208904 | tf_op jit(solution)/shard_map/ppermute | solution.py:469
  52.8 1.3 %shard_map.65 = (f32[64,2048]{1,0:T(8,128)S(1)}, s32[1]{0:T(128)}) custom-call(f32[64,2048]{1,0:T(8,128)S(1)} %copy-done, f32[1024,128]{1,0:T(8,128)S(1)} %get-tuple-element.99.refs_1_, s16[2112,128]{1,0:T(8,128)(2,1)S(1)} %collective-permute-done.25.refs_2_, f32[8,128]{1,0:T(8,128)S(1)} %get-tuple-element.101.refs_3_), custom_call_target="tpu_custom_call" | custom-call | flops 2000000000 | bytes 2117636 | tf_op jit(solution)/shard_map/pallas_call | solution.py:40
  54.7 1.7 %collective-permute-done.27 = s16[272,128]{1,0:T(8,128)(2,1)S(1)} collective-permute-done((s16[272,128]{1,0:T(8,128)(2,1)S(1)}, s16[272,128]{1,0:T(8,128)(2,1)S(1)}, u32[]{:S(2)}, u32[]{:S(2)}) %collective-permute-start.27) | collective-permute-done | bytes 69664 | tf_op jit(solution)/shard_map/ppermute | solution.py:469
  58.1 1.5 %shard_map.67 = f32[64,2048]{1,0:T(8,128)} custom-call(f32[64,2048]{1,0:T(8,128)S(1)} %get-tuple-element.104.refs_0_, f32[1024,128]{1,0:T(8,128)S(1)} %get-tuple-element.108.refs_1_, s16[1088,128]{1,0:T(8,128)(2,1)S(1)} %get-tuple-element.109.refs_2_), custom_call_target="tpu_custom_call" | custom-call | flops 2000000000 | bytes 1851392 | tf_op jit(solution)/shard_map/pallas_call | solution.py:40
  (49 shorter events, 13.2 us)
Async XLA Ops:
  0.0 20.3 %copy-start.1 = (bf16[2,1,256,256]{3,2,1,0:T(8,128)(2,1)S(1)}, bf16[2,1,256,256]{3,2,1,0:T(8,128)(2,1)}, u32[]{:S(2)}) copy-start(bf16[2,1,256,256]{3,2,1,0:T(8,128)(2,1)} %param.11) | copy-start | bytes 786436
  1.3 7.3 %collective-permute-start.7 = (s16[192,128]{1,0:T(8,128)(2,1)S(1)}, s16[192,128]{1,0:T(8,128)(2,1)S(1)}, u32[]{:S(2)}, u32[]{:S(2)}) collective-permute-start(s16[192,128]{1,0:T(8,128)(2,1)S(1)} %get-tuple-element.60), channel_id=1, source_target_pairs={{0,3},{1,2},{2,1},{3,0},{4,7},{5,6},{6,5},{7,4},{8,11},{9,10},{10,... | collective-permute-start | bytes 147464 | tf_op jit(solution)/shard_map/ppermute | solution.py:469
  6.4 5.0 %collective-permute-start.8 = (s16[192,128]{1,0:T(8,128)(2,1)S(1)}, s16[192,128]{1,0:T(8,128)(2,1)S(1)}, u32[]{:S(2)}, u32[]{:S(2)}) collective-permute-start(s16[192,128]{1,0:T(8,128)(2,1)S(1)} %get-tuple-element.61), channel_id=1, source_target_pairs={{0,2},{1,3},{2,0},{3,1},{4,6},{5,7},{6,4},{7,5},{8,10},{9,11},{10,... | collective-permute-start | bytes 147464 | tf_op jit(solution)/shard_map/ppermute | solution.py:469
  6.4 5.0 %collective-permute-start.9 = (s16[192,128]{1,0:T(8,128)(2,1)S(1)}, s16[192,128]{1,0:T(8,128)(2,1)S(1)}, u32[]{:S(2)}, u32[]{:S(2)}) collective-permute-start(s16[192,128]{1,0:T(8,128)(2,1)S(1)} %get-tuple-element.62), channel_id=1, source_target_pairs={{0,1},{1,0},{2,3},{3,2},{4,5},{5,4},{6,7},{7,6},{8,9},{9,8},{10,11... | collective-permute-start | bytes 147464 | tf_op jit(solution)/shard_map/ppermute | solution.py:469
  11.4 5.8 %collective-permute-start.10 = (s16[448,128]{1,0:T(8,128)(2,1)S(1)}, s16[448,128]{1,0:T(8,128)(2,1)S(1)}, u32[]{:S(2)}, u32[]{:S(2)}) collective-permute-start(s16[448,128]{1,0:T(8,128)(2,1)S(1)} %get-tuple-element.65), channel_id=1, source_target_pairs={{0,8},{1,9},{2,10},{3,11},{4,12},{5,13},{6,14},{7,15},{8,0},{9,1},... | collective-permute-start | bytes 344072 | tf_op jit(solution)/shard_map/ppermute | solution.py:469
  13.0 5.9 %collective-permute-start.11 = (s16[448,128]{1,0:T(8,128)(2,1)S(1)}, s16[448,128]{1,0:T(8,128)(2,1)S(1)}, u32[]{:S(2)}, u32[]{:S(2)}) collective-permute-start(s16[448,128]{1,0:T(8,128)(2,1)S(1)} %get-tuple-element.66), channel_id=1, source_target_pairs={{0,16},{1,17},{2,18},{3,19},{4,20},{5,21},{6,22},{7,23},{8,24},{9,... | collective-permute-start | bytes 344072 | tf_op jit(solution)/shard_map/ppermute | solution.py:469
  14.5 5.7 %collective-permute-start.12 = (s16[448,128]{1,0:T(8,128)(2,1)S(1)}, s16[448,128]{1,0:T(8,128)(2,1)S(1)}, u32[]{:S(2)}, u32[]{:S(2)}) collective-permute-start(s16[448,128]{1,0:T(8,128)(2,1)S(1)} %get-tuple-element.67), channel_id=1, source_target_pairs={{0,24},{1,25},{2,26},{3,27},{4,28},{5,29},{6,30},{7,31},{8,16},{9,... | collective-permute-start | bytes 344072 | tf_op jit(solution)/shard_map/ppermute | solution.py:469
  20.2 1.9 %collective-permute-start.13 = (s16[1792,128]{1,0:T(8,128)(2,1)S(1)}, s16[1792,128]{1,0:T(8,128)(2,1)S(1)}, u32[]{:S(2)}, u32[]{:S(2)}) collective-permute-start(s16[1792,128]{1,0:T(8,128)(2,1)S(1)} %constant_dynamic-update-slice_fusion.refs_2_), channel_id=1, source_target_pairs={{0,4},{1,5},{2,6},{3,7},{4,0},{5,1},{6,2},{7,3},{8,12},{9,13},{10,... | collective-permute-start | bytes 1376264 | tf_op jit(solution)/shard_map/ppermute | solution.py:469
  23.6 8.7 %collective-permute-start.17 = (f32[128,128]{1,0:T(8,128)S(1)}, f32[128,128]{1,0:T(8,128)S(1)}, u32[]{:S(2)}, u32[]{:S(2)}) collective-permute-start(f32[128,128]{1,0:T(8,128)S(1)} %get-tuple-element.76.refs_0_.refs), channel_id=1, source_target_pairs={{0,4},{1,5},{2,6},{3,7},{4,0},{5,1},{6,2},{7,3},{8,12},{9,13},{10,... | collective-permute-start | bytes 196616 | tf_op jit(solution)/shard_map/ppermute | solution.py:469
  23.8 4.8 %collective-permute-start.14 = (s16[144,128]{1,0:T(8,128)(2,1)S(1)}, s16[144,128]{1,0:T(8,128)(2,1)S(1)}, u32[]{:S(2)}, u32[]{:S(2)}) collective-permute-start(s16[144,128]{1,0:T(8,128)(2,1)S(1)} %get-tuple-element.72.refs_0_), channel_id=1, source_target_pairs={{0,1},{1,0},{2,3},{3,2},{4,5},{5,4},{6,7},{7,6},{8,9},{9,8},{10,11... | collective-permute-start | bytes 110600 | tf_op jit(solution)/shard_map/ppermute | solution.py:469
  24.4 5.2 %collective-permute-start.15 = (s16[144,128]{1,0:T(8,128)(2,1)S(1)}, s16[144,128]{1,0:T(8,128)(2,1)S(1)}, u32[]{:S(2)}, u32[]{:S(2)}) collective-permute-start(s16[144,128]{1,0:T(8,128)(2,1)S(1)} %get-tuple-element.72.refs_0_), channel_id=1, source_target_pairs={{0,2},{1,3},{2,0},{3,1},{4,6},{5,7},{6,4},{7,5},{8,10},{9,11},{10,... | collective-permute-start | bytes 110600 | tf_op jit(solution)/shard_map/ppermute | solution.py:469
  26.5 5.8 %collective-permute-start.16 = (s16[144,128]{1,0:T(8,128)(2,1)S(1)}, s16[144,128]{1,0:T(8,128)(2,1)S(1)}, u32[]{:S(2)}, u32[]{:S(2)}) collective-permute-start(s16[144,128]{1,0:T(8,128)(2,1)S(1)} %get-tuple-element.72.refs_0_), channel_id=1, source_target_pairs={{0,3},{1,2},{2,1},{3,0},{4,7},{5,6},{6,5},{7,4},{8,11},{9,10},{10,... | collective-permute-start | bytes 110600 | tf_op jit(solution)/shard_map/ppermute | solution.py:469
  32.2 6.7 %collective-permute-start.18 = (s16[528,128]{1,0:T(8,128)(2,1)S(1)}, s16[528,128]{1,0:T(8,128)(2,1)S(1)}, u32[]{:S(2)}, u32[]{:S(2)}) collective-permute-start(s16[528,128]{1,0:T(8,128)(2,1)S(1)} %shard_map.59), channel_id=1, source_target_pairs={{0,24},{1,25},{2,26},{3,27},{4,28},{5,29},{6,30},{7,31},{8,16},{9,... | collective-permute-start | bytes 405512 | tf_op jit(solution)/shard_map/ppermute | solution.py:469
  32.8 6.8 %collective-permute-start.19 = (s16[528,128]{1,0:T(8,128)(2,1)S(1)}, s16[528,128]{1,0:T(8,128)(2,1)S(1)}, u32[]{:S(2)}, u32[]{:S(2)}) collective-permute-start(s16[528,128]{1,0:T(8,128)(2,1)S(1)} %shard_map.59), channel_id=1, source_target_pairs={{0,16},{1,17},{2,18},{3,19},{4,20},{5,21},{6,22},{7,23},{8,24},{9,... | collective-permute-start | bytes 405512 | tf_op jit(solution)/shard_map/ppermute | solution.py:469
  34.3 5.4 %collective-permute-start.20 = (s16[528,128]{1,0:T(8,128)(2,1)S(1)}, s16[528,128]{1,0:T(8,128)(2,1)S(1)}, u32[]{:S(2)}, u32[]{:S(2)}) collective-permute-start(s16[528,128]{1,0:T(8,128)(2,1)S(1)} %shard_map.59), channel_id=1, source_target_pairs={{0,8},{1,9},{2,10},{3,11},{4,12},{5,13},{6,14},{7,15},{8,0},{9,1},... | collective-permute-start | bytes 405512 | tf_op jit(solution)/shard_map/ppermute | solution.py:469
  40.2 1.3 %collective-permute-start.21 = (f32[128,128]{1,0:T(8,128)S(1)}, f32[128,128]{1,0:T(8,128)S(1)}, u32[]{:S(2)}, u32[]{:S(2)}) collective-permute-start(f32[128,128]{1,0:T(8,128)S(1)} %get-tuple-element.83), channel_id=1, source_target_pairs={{0,4},{1,5},{2,6},{3,7},{4,0},{5,1},{6,2},{7,3},{8,12},{9,13},{10,... | collective-permute-start | bytes 196616 | tf_op jit(solution)/shard_map/ppermute | solution.py:469
  42.2 7.4 %collective-permute-start.25 = (s16[2112,128]{1,0:T(8,128)(2,1)S(1)}, s16[2112,128]{1,0:T(8,128)(2,1)S(1)}, u32[]{:S(2)}, u32[]{:S(2)}) collective-permute-start(s16[2112,128]{1,0:T(8,128)(2,1)S(1)} %constant_dynamic-update-slice_fusion.4.block.refs_0_), channel_id=1, source_target_pairs={{0,4},{1,5},{2,6},{3,7},{4,0},{5,1},{6,2},{7,3},{8,12},{9,13},{10,... | collective-permute-start | bytes 1622024 | tf_op jit(solution)/shard_map/ppermute | solution.py:469
  42.3 5.4 %collective-permute-start.22 = (s16[80,128]{1,0:T(8,128)(2,1)S(1)}, s16[80,128]{1,0:T(8,128)(2,1)S(1)}, u32[]{:S(2)}, u32[]{:S(2)}) collective-permute-start(s16[80,128]{1,0:T(8,128)(2,1)S(1)} %get-tuple-element.92), channel_id=1, source_target_pairs={{0,5},{1,4},{2,7},{3,6},{4,1},{5,0},{6,3},{7,2},{8,13},{9,12},{10,... | collective-permute-start | bytes 61448 | tf_op jit(solution)/shard_map/ppermute | solution.py:469
  42.9 4.8 %collective-permute-start.23 = (s16[80,128]{1,0:T(8,128)(2,1)S(1)}, s16[80,128]{1,0:T(8,128)(2,1)S(1)}, u32[]{:S(2)}, u32[]{:S(2)}) collective-permute-start(s16[80,128]{1,0:T(8,128)(2,1)S(1)} %get-tuple-element.93), channel_id=1, source_target_pairs={{0,6},{1,7},{2,4},{3,5},{4,2},{5,3},{6,0},{7,1},{8,14},{9,15},{10,... | collective-permute-start | bytes 61448 | tf_op jit(solution)/shard_map/ppermute | solution.py:469
  44.5 5.0 %collective-permute-start.24 = (s16[80,128]{1,0:T(8,128)(2,1)S(1)}, s16[80,128]{1,0:T(8,128)(2,1)S(1)}, u32[]{:S(2)}, u32[]{:S(2)}) collective-permute-start(s16[80,128]{1,0:T(8,128)(2,1)S(1)} %get-tuple-element.94), channel_id=1, source_target_pairs={{0,7},{1,6},{2,5},{3,4},{4,3},{5,2},{6,1},{7,0},{8,15},{9,14},{10,... | collective-permute-start | bytes 61448 | tf_op jit(solution)/shard_map/ppermute | solution.py:469
  49.5 5.2 %collective-permute-start.26 = (s16[272,128]{1,0:T(8,128)(2,1)S(1)}, s16[272,128]{1,0:T(8,128)(2,1)S(1)}, u32[]{:S(2)}, u32[]{:S(2)}) collective-permute-start(s16[272,128]{1,0:T(8,128)(2,1)S(1)} %shard_map.63), channel_id=1, source_target_pairs={{0,28},{1,29},{2,30},{3,31},{4,24},{5,25},{6,26},{7,27},{8,20},{9,... | collective-permute-start | bytes 208904 | tf_op jit(solution)/shard_map/ppermute | solution.py:469
  51.1 5.4 %collective-permute-start.27 = (s16[272,128]{1,0:T(8,128)(2,1)S(1)}, s16[272,128]{1,0:T(8,128)(2,1)S(1)}, u32[]{:S(2)}, u32[]{:S(2)}) collective-permute-start(s16[272,128]{1,0:T(8,128)(2,1)S(1)} %shard_map.63), channel_id=1, source_target_pairs={{0,20},{1,21},{2,22},{3,23},{4,16},{5,17},{6,18},{7,19},{8,28},{9,... | collective-permute-start | bytes 208904 | tf_op jit(solution)/shard_map/ppermute | solution.py:469
  51.9 4.5 %collective-permute-start.28 = (s16[272,128]{1,0:T(8,128)(2,1)S(1)}, s16[272,128]{1,0:T(8,128)(2,1)S(1)}, u32[]{:S(2)}, u32[]{:S(2)}) collective-permute-start(s16[272,128]{1,0:T(8,128)(2,1)S(1)} %shard_map.63), channel_id=1, source_target_pairs={{0,12},{1,13},{2,14},{3,15},{4,8},{5,9},{6,10},{7,11},{8,4},{9,5},... | collective-permute-start | bytes 208904 | tf_op jit(solution)/shard_map/ppermute | solution.py:469
  56.5 1.6 %collective-permute-start.29 = (s16[1088,128]{1,0:T(8,128)(2,1)S(1)}, s16[1088,128]{1,0:T(8,128)(2,1)S(1)}, u32[]{:S(2)}, u32[]{:S(2)}) collective-permute-start(s16[1088,128]{1,0:T(8,128)(2,1)S(1)} %pad_add_fusion.1.refs_0_), channel_id=1, source_target_pairs={{0,4},{1,5},{2,6},{3,7},{4,0},{5,1},{6,2},{7,3},{8,12},{9,13},{10,... | collective-permute-start | bytes 835592 | tf_op jit(solution)/shard_map/ppermute | solution.py:469
  (1 other events, 20.3 us)

commit v7 on v6

--- a/solution.py
+++ b/solution.py
@@ -231,7 +231,7 @@
 
 
 def first_kernel(
-    C, F, L, place, known, seen_in, whole_in, kernels, turned, other, start_out, seen_out, refs_out, live_out, msg
+    C, F, L, place, known, seen_in, whole_in, kernels, turned, other, start_out, seen_out, refs_out, near_out, live_out, msg
 ):
     c, f = place[0], place[1]
     chips, slots = C // 2, C * F
@@ -241,19 +241,28 @@
     piece = per_facet // C
     seen, whole = sorted_blocks(C, F, L, c, other, slots // 2)
     seen = seen + seen_in[...]
-    row, column = iota((2 * STRIP, L * STRIP), 0), iota((2 * STRIP, L * STRIP), 1)
-    channel = c * L + column // STRIP
+    row, column = iota((2 * STRIP, 2 * L * STRIP), 0), iota((2 * STRIP, 2 * L * STRIP), 1)
+    channel = (c ^ (column // (L * STRIP))) * L + column // STRIP % L
     lanes = jnp.where(row == channel, 64.0, jnp.where(row == channel + STRIP, 1.0, 0.0))
     whole = jnp.dot(
         (whole + whole_in[...]).astype(BF16), lanes.astype(BF16), preferred_element_type=F32
     )
     kinds = [
         whole[kind * slots : (kind + 1) * slots, ch * STRIP : (ch + 1) * STRIP]
-        for ch in range(L)
+        for ch in range(2 * L)
         for kind in range(TERMS + 1)
     ]
-    refs = jnp.concatenate([x for i, x in enumerate(kinds) if i % (TERMS + 1) < TERMS], axis=0)
-    live = jnp.concatenate(kinds[TERMS :: TERMS + 1], axis=0)
+    both_refs = jnp.concatenate([x for i, x in enumerate(kinds) if i % (TERMS + 1) < TERMS], axis=0)
+    refs = both_refs[: both_refs.shape[0] // 2]
+    near_out[...] = jnp.concatenate(
+        [
+            both_refs[at : at + slots // 2]
+            for first in range(both_refs.shape[0] // 2, both_refs.shape[0], slots)
+            for at in (first + slots // 2, first)
+        ],
+        axis=0,
+    )
+    live = jnp.concatenate(kinds[TERMS : L * (TERMS + 1) : TERMS + 1], axis=0)
     col = refs.astype(I32)
     facet, local = col >> log2(per_facet), col & (per_facet - 1)
     k, d = facet ^ f, (local >> log2(piece)) ^ c
@@ -530,11 +539,12 @@
         10**8,
         placed=True,
     )
-    est, observed, at, live, msg = call(
+    est, observed, at, other_at, live, msg = call(
         functools.partial(first_kernel, C, F, L),
         [
             at_refs,
             jax.ShapeDtypeStruct((refs, STRIP), BF16),
+            at_refs,
             at_refs,
             jax.ShapeDtypeStruct((L * C * F, STRIP), F32),
             message,
@@ -582,9 +592,7 @@
         10**8,
         placed=True,
     )
-    near, pick, numbers, at, other_at = lax.optimization_barrier(
-        (near, pick, numbers, at, swap(at, 1))
-    )
+    near, pick, numbers = lax.optimization_barrier((near, pick, numbers))
     mine = around_chan(near)
     part, other_part = call(
         functools.partial(part_kernel, F, chips),

time: 59.8 us -> 59.4 us (level)
    ppermute x23 -> x22, waiting for transfers between devices: 23.5 us -> 23.3 us  [swap(): return lax.ppermute(x, ('chan', 'facet'), pairs)]
    ppermute x23 -> x22, starting transfers between devices: 25.3 us -> 25.2 us  [swap(): return lax.ppermute(x, ('chan', 'facet'), pairs)]
  transfers between devices with their start and end apart: 23 -> 22, of which waited for: 15 -> 15; matrix products, arithmetic and copies ran while one was open for 0% -> 0% of each run, Pallas kernels for 7% -> 7%
where the time goes in v7:
time: 59.4 us; the launch traced here: 59.3 us
  starting transfers between devices  25.2 us (42%)
  waiting for transfers between devices  23.3 us (39%)
  Pallas kernels  9.82 us (17%)
  between operations  0.83 us (1%)
    ppermute x22, starting transfers between devices, swap(): return lax.ppermute(x, ('chan', 'facet'), pairs)  25.2 us
    ppermute x22, waiting for transfers between devices, swap(): return lax.ppermute(x, ('chan', 'facet'), pairs)  23.3 us
    pallas_call x13, Pallas kernels, call(): pl.pallas_call(body, out_shape=list(outs), in_specs=spaces, out_specs=[pl...  9.82 us
  transfers between devices with their start and end apart: 22, of which 15 were waited for; matrix products, arithmetic and copies ran while one was open for 0% of the time, Pallas kernels for 7%

profile of v7, /device:TPU:0, one launch (start us, length us, event | category | flops | bytes accessed | tf_op | source)
XLA Modules:
  0.0 59.3 jit_solution(5916598350240884721)
XLA Ops:
  1.3 5.1 %collective-permute-start.7 = (s16[192,128]{1,0:T(8,128)(2,1)S(1)}, s16[192,128]{1,0:T(8,128)(2,1)S(1)}, u32[]{:S(2)}, u32[]{:S(2)}) collective-permute-start(s16[192,128]{1,0:T(8,128)(2,1)S(1)} %get-tuple-element.59), channel_id=1, source_target_pairs={{0,3},{1,2},{2,1},{3,0},{4,7},{5,6},{6,5},{7,4},{8,11},{9,10},{10,... | collective-permute-start | bytes 147464 | tf_op jit(solution)/shard_map/ppermute | solution.py:478
  7.0 1.6 %collective-permute-done.7.refs_0_ = s16[192,128]{1,0:T(8,128)(2,1)S(1)} collective-permute-done((s16[192,128]{1,0:T(8,128)(2,1)S(1)}, s16[192,128]{1,0:T(8,128)(2,1)S(1)}, u32[]{:S(2)}, u32[]{:S(2)}) %collective-permute-start.7) | collective-permute-done | bytes 49184 | tf_op jit(solution)/shard_map/ppermute | solution.py:478
  8.6 2.8 %collective-permute-done.8.refs_1_ = s16[192,128]{1,0:T(8,128)(2,1)S(1)} collective-permute-done((s16[192,128]{1,0:T(8,128)(2,1)S(1)}, s16[192,128]{1,0:T(8,128)(2,1)S(1)}, u32[]{:S(2)}, u32[]{:S(2)}) %collective-permute-start.8) | collective-permute-done | bytes 49184 | tf_op jit(solution)/shard_map/ppermute | solution.py:478
  11.4 1.6 %collective-permute-start.10 = (s16[448,128]{1,0:T(8,128)(2,1)S(1)}, s16[448,128]{1,0:T(8,128)(2,1)S(1)}, u32[]{:S(2)}, u32[]{:S(2)}) collective-permute-start(s16[448,128]{1,0:T(8,128)(2,1)S(1)} %get-tuple-element.64), channel_id=1, source_target_pairs={{0,8},{1,9},{2,10},{3,11},{4,12},{5,13},{6,14},{7,15},{8,0},{9,1},... | collective-permute-start | bytes 344072 | tf_op jit(solution)/shard_map/ppermute | solution.py:478
  13.0 1.5 %collective-permute-start.11 = (s16[448,128]{1,0:T(8,128)(2,1)S(1)}, s16[448,128]{1,0:T(8,128)(2,1)S(1)}, u32[]{:S(2)}, u32[]{:S(2)}) collective-permute-start(s16[448,128]{1,0:T(8,128)(2,1)S(1)} %get-tuple-element.65), channel_id=1, source_target_pairs={{0,16},{1,17},{2,18},{3,19},{4,20},{5,21},{6,22},{7,23},{8,24},{9,... | collective-permute-start | bytes 344072 | tf_op jit(solution)/shard_map/ppermute | solution.py:478
  15.0 2.2 %collective-permute-done.10 = s16[448,128]{1,0:T(8,128)(2,1)S(1)} collective-permute-done((s16[448,128]{1,0:T(8,128)(2,1)S(1)}, s16[448,128]{1,0:T(8,128)(2,1)S(1)}, u32[]{:S(2)}, u32[]{:S(2)}) %collective-permute-start.10) | collective-permute-done | bytes 114720 | tf_op jit(solution)/shard_map/ppermute | solution.py:478
  17.2 1.6 %collective-permute-done.11 = s16[448,128]{1,0:T(8,128)(2,1)S(1)} collective-permute-done((s16[448,128]{1,0:T(8,128)(2,1)S(1)}, s16[448,128]{1,0:T(8,128)(2,1)S(1)}, u32[]{:S(2)}, u32[]{:S(2)}) %collective-permute-start.11) | collective-permute-done | bytes 114720 | tf_op jit(solution)/shard_map/ppermute | solution.py:478
  18.9 1.3 %collective-permute-done.12 = s16[448,128]{1,0:T(8,128)(2,1)S(1)} collective-permute-done((s16[448,128]{1,0:T(8,128)(2,1)S(1)}, s16[448,128]{1,0:T(8,128)(2,1)S(1)}, u32[]{:S(2)}, u32[]{:S(2)}) %collective-permute-start.12) | collective-permute-done | bytes 114720 | tf_op jit(solution)/shard_map/ppermute | solution.py:478
  22.1 1.4 %shard_map.58 = (f32[128,128]{1,0:T(8,128)S(1)}, bf16[128,128]{1,0:T(8,128)(2,1)S(1)}, f32[128,128]{1,0:T(8,128)S(1)}, f32[128,128]{1,0:T(8,128)S(1)}, f32[64,12...) custom-call(bf16[2560,256]{1,0:T(8,128)(2,1)S(1)} %get-tuple-element.67.refs_0_, f32[128,128]{1,0:T(8,128)S(1)} %get-tuple-element.68.refs_1_, ...), custom_call_target="tpu_custom_call" | custom-call | flops 500000000 | bytes 2756608 | tf_op jit(solution)/shard_map/pallas_call | solution.py:40
  24.2 2.0 %collective-permute-start.15 = (s16[144,128]{1,0:T(8,128)(2,1)S(1)}, s16[144,128]{1,0:T(8,128)(2,1)S(1)}, u32[]{:S(2)}, u32[]{:S(2)}) collective-permute-start(s16[144,128]{1,0:T(8,128)(2,1)S(1)} %get-tuple-element.76.refs_0_), channel_id=1, source_target_pairs={{0,2},{1,3},{2,0},{3,1},{4,6},{5,7},{6,4},{7,5},{8,10},{9,11},{10,... | collective-permute-start | bytes 110600 | tf_op jit(solution)/shard_map/ppermute | solution.py:478
  26.3 1.7 %collective-permute-start.16 = (s16[144,128]{1,0:T(8,128)(2,1)S(1)}, s16[144,128]{1,0:T(8,128)(2,1)S(1)}, u32[]{:S(2)}, u32[]{:S(2)}) collective-permute-start(s16[144,128]{1,0:T(8,128)(2,1)S(1)} %get-tuple-element.76.refs_0_), channel_id=1, source_target_pairs={{0,3},{1,2},{2,1},{3,0},{4,7},{5,6},{6,5},{7,4},{8,11},{9,10},{10,... | collective-permute-start | bytes 110600 | tf_op jit(solution)/shard_map/ppermute | solution.py:478
  29.2 2.8 %collective-permute-done.16.refs_3_ = s16[144,128]{1,0:T(8,128)(2,1)S(1)} collective-permute-done((s16[144,128]{1,0:T(8,128)(2,1)S(1)}, s16[144,128]{1,0:T(8,128)(2,1)S(1)}, u32[]{:S(2)}, u32[]{:S(2)}) %collective-permute-start.16) | collective-permute-done | bytes 36896 | tf_op jit(solution)/shard_map/ppermute | solution.py:478
  32.6 1.5 %collective-permute-start.18 = (s16[528,128]{1,0:T(8,128)(2,1)S(1)}, s16[528,128]{1,0:T(8,128)(2,1)S(1)}, u32[]{:S(2)}, u32[]{:S(2)}) collective-permute-start(s16[528,128]{1,0:T(8,128)(2,1)S(1)} %shard_map.59), channel_id=1, source_target_pairs={{0,16},{1,17},{2,18},{3,19},{4,20},{5,21},{6,22},{7,23},{8,24},{9,... | collective-permute-start | bytes 405512 | tf_op jit(solution)/shard_map/ppermute | solution.py:478
  34.1 1.6 %collective-permute-start.19 = (s16[528,128]{1,0:T(8,128)(2,1)S(1)}, s16[528,128]{1,0:T(8,128)(2,1)S(1)}, u32[]{:S(2)}, u32[]{:S(2)}) collective-permute-start(s16[528,128]{1,0:T(8,128)(2,1)S(1)} %shard_map.59), channel_id=1, source_target_pairs={{0,8},{1,9},{2,10},{3,11},{4,12},{5,13},{6,14},{7,15},{8,0},{9,1},... | collective-permute-start | bytes 405512 | tf_op jit(solution)/shard_map/ppermute | solution.py:478
  35.7 2.9 %collective-permute-done.17 = s16[528,128]{1,0:T(8,128)(2,1)S(1)} collective-permute-done((s16[528,128]{1,0:T(8,128)(2,1)S(1)}, s16[528,128]{1,0:T(8,128)(2,1)S(1)}, u32[]{:S(2)}, u32[]{:S(2)}) %collective-permute-start.17) | collective-permute-done | bytes 135200 | tf_op jit(solution)/shard_map/ppermute | solution.py:478
  39.8 1.2 %collective-permute-done.20.rest = f32[128,128]{1,0:T(8,128)S(1)} collective-permute-done((f32[128,128]{1,0:T(8,128)S(1)}, f32[128,128]{1,0:T(8,128)S(1)}, u32[]{:S(2)}, u32[]{:S(2)}) %collective-permute-start.20) | collective-permute-done | bytes 65568 | tf_op jit(solution)/shard_map/ppermute | solution.py:478
  42.6 1.5 %collective-permute-start.22 = (s16[80,128]{1,0:T(8,128)(2,1)S(1)}, s16[80,128]{1,0:T(8,128)(2,1)S(1)}, u32[]{:S(2)}, u32[]{:S(2)}) collective-permute-start(s16[80,128]{1,0:T(8,128)(2,1)S(1)} %get-tuple-element.91), channel_id=1, source_target_pairs={{0,6},{1,7},{2,4},{3,5},{4,2},{5,3},{6,0},{7,1},{8,14},{9,15},{10,... | collective-permute-start | bytes 61448 | tf_op jit(solution)/shard_map/ppermute | solution.py:478
  44.1 1.8 %collective-permute-start.23 = (s16[80,128]{1,0:T(8,128)(2,1)S(1)}, s16[80,128]{1,0:T(8,128)(2,1)S(1)}, u32[]{:S(2)}, u32[]{:S(2)}) collective-permute-start(s16[80,128]{1,0:T(8,128)(2,1)S(1)} %get-tuple-element.92), channel_id=1, source_target_pairs={{0,7},{1,6},{2,5},{3,4},{4,3},{5,2},{6,1},{7,0},{8,15},{9,14},{10,... | collective-permute-start | bytes 61448 | tf_op jit(solution)/shard_map/ppermute | solution.py:478
  45.9 1.3 %shard_map.64 = (f32[1024,128]{1,0:T(8,128)S(1)}, f32[8,128]{1,0:T(8,128)S(1)}) custom-call(s16[2112,128]{1,0:T(8,128)(2,1)S(1)} %constant_dynamic-update-slice_fusion.4.block.refs_0_), custom_call_target="tpu_custom_call" | custom-call | flops 2000000000 | bytes 1069056 | tf_op jit(solution)/shard_map/pallas_call | solution.py:40
  47.3 1.9 %collective-permute-done.23.refs_3_ = s16[80,128]{1,0:T(8,128)(2,1)S(1)} collective-permute-done((s16[80,128]{1,0:T(8,128)(2,1)S(1)}, s16[80,128]{1,0:T(8,128)(2,1)S(1)}, u32[]{:S(2)}, u32[]{:S(2)}) %collective-permute-start.23) | collective-permute-done | bytes 20512 | tf_op jit(solution)/shard_map/ppermute | solution.py:478
  49.2 1.6 %collective-permute-start.25 = (s16[272,128]{1,0:T(8,128)(2,1)S(1)}, s16[272,128]{1,0:T(8,128)(2,1)S(1)}, u32[]{:S(2)}, u32[]{:S(2)}) collective-permute-start(s16[272,128]{1,0:T(8,128)(2,1)S(1)} %shard_map.63), channel_id=1, source_target_pairs={{0,28},{1,29},{2,30},{3,31},{4,24},{5,25},{6,26},{7,27},{8,20},{9,... | collective-permute-start | bytes 208904 | tf_op jit(solution)/shard_map/ppermute | solution.py:478
  52.4 1.3 %shard_map.65 = (f32[64,2048]{1,0:T(8,128)S(1)}, s32[1]{0:T(128)}) custom-call(f32[64,2048]{1,0:T(8,128)S(1)} %copy-done, f32[1024,128]{1,0:T(8,128)S(1)} %get-tuple-element.97.refs_1_, s16[2112,128]{1,0:T(8,128)(2,1)S(1)} %collective-permute-done.24.refs_2_, f32[8,128]{1,0:T(8,128)S(1)} %get-tuple-element.99.refs_3_), custom_call_target="tpu_custom_call" | custom-call | flops 2000000000 | bytes 2117636 | tf_op jit(solution)/shard_map/pallas_call | solution.py:40
  54.4 1.7 %collective-permute-done.26 = s16[272,128]{1,0:T(8,128)(2,1)S(1)} collective-permute-done((s16[272,128]{1,0:T(8,128)(2,1)S(1)}, s16[272,128]{1,0:T(8,128)(2,1)S(1)}, u32[]{:S(2)}, u32[]{:S(2)}) %collective-permute-start.26) | collective-permute-done | bytes 69664 | tf_op jit(solution)/shard_map/ppermute | solution.py:478
  57.7 1.5 %shard_map.67 = f32[64,2048]{1,0:T(8,128)} custom-call(f32[64,2048]{1,0:T(8,128)S(1)} %get-tuple-element.102.refs_0_, f32[1024,128]{1,0:T(8,128)S(1)} %get-tuple-element.106.refs_1_, s16[1088,128]{1,0:T(8,128)(2,1)S(1)} %get-tuple-element.107.refs_2_), custom_call_target="tpu_custom_call" | custom-call | flops 2000000000 | bytes 1851392 | tf_op jit(solution)/shard_map/pallas_call | solution.py:40
  (47 shorter events, 12.9 us)
Async XLA Ops:
  0.0 20.3 %copy-start = (f32[64,2048]{1,0:T(8,128)S(1)}, f32[64,2048]{1,0:T(8,128)}, u32[]{:S(2)}) copy-start(f32[64,2048]{1,0:T(8,128)} %refs_0_.6) | copy-start | bytes 1572868
  0.0 20.3 %copy-start.1 = (bf16[2,1,256,256]{3,2,1,0:T(8,128)(2,1)S(1)}, bf16[2,1,256,256]{3,2,1,0:T(8,128)(2,1)}, u32[]{:S(2)}) copy-start(bf16[2,1,256,256]{3,2,1,0:T(8,128)(2,1)} %param.11) | copy-start | bytes 786436
  1.3 7.3 %collective-permute-start.7 = (s16[192,128]{1,0:T(8,128)(2,1)S(1)}, s16[192,128]{1,0:T(8,128)(2,1)S(1)}, u32[]{:S(2)}, u32[]{:S(2)}) collective-permute-start(s16[192,128]{1,0:T(8,128)(2,1)S(1)} %get-tuple-element.59), channel_id=1, source_target_pairs={{0,3},{1,2},{2,1},{3,0},{4,7},{5,6},{6,5},{7,4},{8,11},{9,10},{10,... | collective-permute-start | bytes 147464 | tf_op jit(solution)/shard_map/ppermute | solution.py:478
  6.4 5.0 %collective-permute-start.8 = (s16[192,128]{1,0:T(8,128)(2,1)S(1)}, s16[192,128]{1,0:T(8,128)(2,1)S(1)}, u32[]{:S(2)}, u32[]{:S(2)}) collective-permute-start(s16[192,128]{1,0:T(8,128)(2,1)S(1)} %get-tuple-element.60), channel_id=1, source_target_pairs={{0,2},{1,3},{2,0},{3,1},{4,6},{5,7},{6,4},{7,5},{8,10},{9,11},{10,... | collective-permute-start | bytes 147464 | tf_op jit(solution)/shard_map/ppermute | solution.py:478
  6.4 5.0 %collective-permute-start.9 = (s16[192,128]{1,0:T(8,128)(2,1)S(1)}, s16[192,128]{1,0:T(8,128)(2,1)S(1)}, u32[]{:S(2)}, u32[]{:S(2)}) collective-permute-start(s16[192,128]{1,0:T(8,128)(2,1)S(1)} %get-tuple-element.61), channel_id=1, source_target_pairs={{0,1},{1,0},{2,3},{3,2},{4,5},{5,4},{6,7},{7,6},{8,9},{9,8},{10,11... | collective-permute-start | bytes 147464 | tf_op jit(solution)/shard_map/ppermute | solution.py:478
  11.4 5.8 %collective-permute-start.10 = (s16[448,128]{1,0:T(8,128)(2,1)S(1)}, s16[448,128]{1,0:T(8,128)(2,1)S(1)}, u32[]{:S(2)}, u32[]{:S(2)}) collective-permute-start(s16[448,128]{1,0:T(8,128)(2,1)S(1)} %get-tuple-element.64), channel_id=1, source_target_pairs={{0,8},{1,9},{2,10},{3,11},{4,12},{5,13},{6,14},{7,15},{8,0},{9,1},... | collective-permute-start | bytes 344072 | tf_op jit(solution)/shard_map/ppermute | solution.py:478
  13.0 5.9 %collective-permute-start.11 = (s16[448,128]{1,0:T(8,128)(2,1)S(1)}, s16[448,128]{1,0:T(8,128)(2,1)S(1)}, u32[]{:S(2)}, u32[]{:S(2)}) collective-permute-start(s16[448,128]{1,0:T(8,128)(2,1)S(1)} %get-tuple-element.65), channel_id=1, source_target_pairs={{0,16},{1,17},{2,18},{3,19},{4,20},{5,21},{6,22},{7,23},{8,24},{9,... | collective-permute-start | bytes 344072 | tf_op jit(solution)/shard_map/ppermute | solution.py:478
  14.5 5.7 %collective-permute-start.12 = (s16[448,128]{1,0:T(8,128)(2,1)S(1)}, s16[448,128]{1,0:T(8,128)(2,1)S(1)}, u32[]{:S(2)}, u32[]{:S(2)}) collective-permute-start(s16[448,128]{1,0:T(8,128)(2,1)S(1)} %get-tuple-element.66), channel_id=1, source_target_pairs={{0,24},{1,25},{2,26},{3,27},{4,28},{5,29},{6,30},{7,31},{8,16},{9,... | collective-permute-start | bytes 344072 | tf_op jit(solution)/shard_map/ppermute | solution.py:478
  20.2 1.9 %collective-permute-start.13 = (s16[1792,128]{1,0:T(8,128)(2,1)S(1)}, s16[1792,128]{1,0:T(8,128)(2,1)S(1)}, u32[]{:S(2)}, u32[]{:S(2)}) collective-permute-start(s16[1792,128]{1,0:T(8,128)(2,1)S(1)} %constant_dynamic-update-slice_fusion.refs_2_), channel_id=1, source_target_pairs={{0,4},{1,5},{2,6},{3,7},{4,0},{5,1},{6,2},{7,3},{8,12},{9,13},{10,... | collective-permute-start | bytes 1376264 | tf_op jit(solution)/shard_map/ppermute | solution.py:478
  23.5 4.8 %collective-permute-start.14 = (s16[144,128]{1,0:T(8,128)(2,1)S(1)}, s16[144,128]{1,0:T(8,128)(2,1)S(1)}, u32[]{:S(2)}, u32[]{:S(2)}) collective-permute-start(s16[144,128]{1,0:T(8,128)(2,1)S(1)} %get-tuple-element.76.refs_0_), channel_id=1, source_target_pairs={{0,1},{1,0},{2,3},{3,2},{4,5},{5,4},{6,7},{7,6},{8,9},{9,8},{10,11... | collective-permute-start | bytes 110600 | tf_op jit(solution)/shard_map/ppermute | solution.py:478
  24.2 5.0 %collective-permute-start.15 = (s16[144,128]{1,0:T(8,128)(2,1)S(1)}, s16[144,128]{1,0:T(8,128)(2,1)S(1)}, u32[]{:S(2)}, u32[]{:S(2)}) collective-permute-start(s16[144,128]{1,0:T(8,128)(2,1)S(1)} %get-tuple-element.76.refs_0_), channel_id=1, source_target_pairs={{0,2},{1,3},{2,0},{3,1},{4,6},{5,7},{6,4},{7,5},{8,10},{9,11},{10,... | collective-permute-start | bytes 110600 | tf_op jit(solution)/shard_map/ppermute | solution.py:478
  26.3 5.8 %collective-permute-start.16 = (s16[144,128]{1,0:T(8,128)(2,1)S(1)}, s16[144,128]{1,0:T(8,128)(2,1)S(1)}, u32[]{:S(2)}, u32[]{:S(2)}) collective-permute-start(s16[144,128]{1,0:T(8,128)(2,1)S(1)} %get-tuple-element.76.refs_0_), channel_id=1, source_target_pairs={{0,3},{1,2},{2,1},{3,0},{4,7},{5,6},{6,5},{7,4},{8,11},{9,10},{10,... | collective-permute-start | bytes 110600 | tf_op jit(solution)/shard_map/ppermute | solution.py:478
  32.0 6.5 %collective-permute-start.17 = (s16[528,128]{1,0:T(8,128)(2,1)S(1)}, s16[528,128]{1,0:T(8,128)(2,1)S(1)}, u32[]{:S(2)}, u32[]{:S(2)}) collective-permute-start(s16[528,128]{1,0:T(8,128)(2,1)S(1)} %shard_map.59), channel_id=1, source_target_pairs={{0,24},{1,25},{2,26},{3,27},{4,28},{5,29},{6,30},{7,31},{8,16},{9,... | collective-permute-start | bytes 405512 | tf_op jit(solution)/shard_map/ppermute | solution.py:478
  32.6 6.5 %collective-permute-start.18 = (s16[528,128]{1,0:T(8,128)(2,1)S(1)}, s16[528,128]{1,0:T(8,128)(2,1)S(1)}, u32[]{:S(2)}, u32[]{:S(2)}) collective-permute-start(s16[528,128]{1,0:T(8,128)(2,1)S(1)} %shard_map.59), channel_id=1, source_target_pairs={{0,16},{1,17},{2,18},{3,19},{4,20},{5,21},{6,22},{7,23},{8,24},{9,... | collective-permute-start | bytes 405512 | tf_op jit(solution)/shard_map/ppermute | solution.py:478
  34.1 5.1 %collective-permute-start.19 = (s16[528,128]{1,0:T(8,128)(2,1)S(1)}, s16[528,128]{1,0:T(8,128)(2,1)S(1)}, u32[]{:S(2)}, u32[]{:S(2)}) collective-permute-start(s16[528,128]{1,0:T(8,128)(2,1)S(1)} %shard_map.59), channel_id=1, source_target_pairs={{0,8},{1,9},{2,10},{3,11},{4,12},{5,13},{6,14},{7,15},{8,0},{9,1},... | collective-permute-start | bytes 405512 | tf_op jit(solution)/shard_map/ppermute | solution.py:478
  39.7 1.3 %collective-permute-start.20 = (f32[128,128]{1,0:T(8,128)S(1)}, f32[128,128]{1,0:T(8,128)S(1)}, u32[]{:S(2)}, u32[]{:S(2)}) collective-permute-start(f32[128,128]{1,0:T(8,128)S(1)} %get-tuple-element.81), channel_id=1, source_target_pairs={{0,4},{1,5},{2,6},{3,7},{4,0},{5,1},{6,2},{7,3},{8,12},{9,13},{10,... | collective-permute-start | bytes 196616 | tf_op jit(solution)/shard_map/ppermute | solution.py:478
  41.7 7.5 %collective-permute-start.24 = (s16[2112,128]{1,0:T(8,128)(2,1)S(1)}, s16[2112,128]{1,0:T(8,128)(2,1)S(1)}, u32[]{:S(2)}, u32[]{:S(2)}) collective-permute-start(s16[2112,128]{1,0:T(8,128)(2,1)S(1)} %constant_dynamic-update-slice_fusion.4.block.refs_0_), channel_id=1, source_target_pairs={{0,4},{1,5},{2,6},{3,7},{4,0},{5,1},{6,2},{7,3},{8,12},{9,13},{10,... | collective-permute-start | bytes 1622024 | tf_op jit(solution)/shard_map/ppermute | solution.py:478
  41.9 5.4 %collective-permute-start.21 = (s16[80,128]{1,0:T(8,128)(2,1)S(1)}, s16[80,128]{1,0:T(8,128)(2,1)S(1)}, u32[]{:S(2)}, u32[]{:S(2)}) collective-permute-start(s16[80,128]{1,0:T(8,128)(2,1)S(1)} %get-tuple-element.90), channel_id=1, source_target_pairs={{0,5},{1,4},{2,7},{3,6},{4,1},{5,0},{6,3},{7,2},{8,13},{9,12},{10,... | collective-permute-start | bytes 61448 | tf_op jit(solution)/shard_map/ppermute | solution.py:478
  42.6 4.6 %collective-permute-start.22 = (s16[80,128]{1,0:T(8,128)(2,1)S(1)}, s16[80,128]{1,0:T(8,128)(2,1)S(1)}, u32[]{:S(2)}, u32[]{:S(2)}) collective-permute-start(s16[80,128]{1,0:T(8,128)(2,1)S(1)} %get-tuple-element.91), channel_id=1, source_target_pairs={{0,6},{1,7},{2,4},{3,5},{4,2},{5,3},{6,0},{7,1},{8,14},{9,15},{10,... | collective-permute-start | bytes 61448 | tf_op jit(solution)/shard_map/ppermute | solution.py:478
  44.1 5.0 %collective-permute-start.23 = (s16[80,128]{1,0:T(8,128)(2,1)S(1)}, s16[80,128]{1,0:T(8,128)(2,1)S(1)}, u32[]{:S(2)}, u32[]{:S(2)}) collective-permute-start(s16[80,128]{1,0:T(8,128)(2,1)S(1)} %get-tuple-element.92), channel_id=1, source_target_pairs={{0,7},{1,6},{2,5},{3,4},{4,3},{5,2},{6,1},{7,0},{8,15},{9,14},{10,... | collective-permute-start | bytes 61448 | tf_op jit(solution)/shard_map/ppermute | solution.py:478
  49.2 5.2 %collective-permute-start.25 = (s16[272,128]{1,0:T(8,128)(2,1)S(1)}, s16[272,128]{1,0:T(8,128)(2,1)S(1)}, u32[]{:S(2)}, u32[]{:S(2)}) collective-permute-start(s16[272,128]{1,0:T(8,128)(2,1)S(1)} %shard_map.63), channel_id=1, source_target_pairs={{0,28},{1,29},{2,30},{3,31},{4,24},{5,25},{6,26},{7,27},{8,20},{9,... | collective-permute-start | bytes 208904 | tf_op jit(solution)/shard_map/ppermute | solution.py:478
  50.8 5.3 %collective-permute-start.26 = (s16[272,128]{1,0:T(8,128)(2,1)S(1)}, s16[272,128]{1,0:T(8,128)(2,1)S(1)}, u32[]{:S(2)}, u32[]{:S(2)}) collective-permute-start(s16[272,128]{1,0:T(8,128)(2,1)S(1)} %shard_map.63), channel_id=1, source_target_pairs={{0,20},{1,21},{2,22},{3,23},{4,16},{5,17},{6,18},{7,19},{8,28},{9,... | collective-permute-start | bytes 208904 | tf_op jit(solution)/shard_map/ppermute | solution.py:478
  51.6 4.4 %collective-permute-start.27 = (s16[272,128]{1,0:T(8,128)(2,1)S(1)}, s16[272,128]{1,0:T(8,128)(2,1)S(1)}, u32[]{:S(2)}, u32[]{:S(2)}) collective-permute-start(s16[272,128]{1,0:T(8,128)(2,1)S(1)} %shard_map.63), channel_id=1, source_target_pairs={{0,12},{1,13},{2,14},{3,15},{4,8},{5,9},{6,10},{7,11},{8,4},{9,5},... | collective-permute-start | bytes 208904 | tf_op jit(solution)/shard_map/ppermute | solution.py:478
  56.1 1.6 %collective-permute-start.28 = (s16[1088,128]{1,0:T(8,128)(2,1)S(1)}, s16[1088,128]{1,0:T(8,128)(2,1)S(1)}, u32[]{:S(2)}, u32[]{:S(2)}) collective-permute-start(s16[1088,128]{1,0:T(8,128)(2,1)S(1)} %pad_add_fusion.1.refs_0_), channel_id=1, source_target_pairs={{0,4},{1,5},{2,6},{3,7},{4,0},{5,1},{6,2},{7,3},{8,12},{9,13},{10,... | collective-permute-start | bytes 835592 | tf_op jit(solution)/shard_map/ppermute | solution.py:478

commit v8 on v7

--- a/solution.py
+++ b/solution.py
@@ -266,7 +266,8 @@
     col = refs.astype(I32)
     facet, local = col >> log2(per_facet), col & (per_facet - 1)
     k, d = facet ^ f, (local >> log2(piece)) ^ c
-    turn = ((d & 1) * chips + (d >> 1)) * (F - 1) + k - 1
+    block = (chips - (d >> 1)) & (chips - 1)
+    turn = ((d & 1) * chips + block) * (F - 1) + k - 1
     place_of = jnp.where(k == 0, local, per_facet + turn * piece + (local & (piece - 1)))
     rest = table_of(jnp.concatenate(shares_of(other, chips, size, used), axis=0))
 
@@ -519,7 +520,7 @@
         10**6,
     )
     mine = jnp.concatenate(
-        [passed[0]] + [swap(passed[j], 2 * j) for j in range(1, chips)], axis=0
+        [passed[0]] + [swap(passed[j], 2 * j) for j in range(chips - 1, 0, -1)], axis=0
     )
     other = swap(mine, 1)
 
@@ -555,7 +556,7 @@
     )
 
     def along_facet(msgs, cross=0):
-        got = [msgs[0]] + [swap(msgs[k], cross, k) for k in range(1, F)]
+        got = [msgs[0]] + [swap(msgs[k], cross, k) for k in range(F - 1, 0, -1)][::-1]
         rows = got[0].shape[0] - EXTRA
         return call(
             join_kernel, [jax.ShapeDtypeStruct((F * rows + EXTRA, STRIP), I16)], got, 10**6

time: 59.4 us -> 59.1 us (level)
  no operation moved by 1% of the time
where the time goes in v8:
time: 59.1 us; the launch traced here: 58.9 us
  starting transfers between devices  25.2 us (43%)
  waiting for transfers between devices  23 us (39%)
  Pallas kernels  9.83 us (17%)
  between operations  0.83 us (1%)
    ppermute x22, starting transfers between devices, swap(): return lax.ppermute(x, ('chan', 'facet'), pairs)  25.2 us
    ppermute x22, waiting for transfers between devices, swap(): return lax.ppermute(x, ('chan', 'facet'), pairs)  23 us
    pallas_call x13, Pallas kernels, call(): pl.pallas_call(body, out_shape=list(outs), in_specs=spaces, out_specs=[pl...  9.83 us
  transfers between devices with their start and end apart: 22, of which 15 were waited for; matrix products, arithmetic and copies ran while one was open for 0% of the time, Pallas kernels for 7%

profile of v8, /device:TPU:0, one launch (start us, length us, event | category | flops | bytes accessed | tf_op | source)
XLA Modules:
  0.0 58.9 jit_solution(4560050812567670277)
XLA Ops:
  0.0 1.2 %shard_map.55 = (s16[64,128]{1,0:T(8,128)(2,1)S(1)}, s16[192,128]{1,0:T(8,128)(2,1)S(1)}, s16[192,128]{1,0:T(8,128)(2,1)S(1)}, s16[192,128]{1,0:T(8,128)(2,1)S(1)}) custom-call(f32[64,2048]{1,0:T(8,128)} %refs_0_.6, bf16[16,4,256]{2,1,0:T(4,128)(2,1)} %bitcast.12, s32[4,2,16]{2,1,0:T(2,128)} %bitcast.13, s32[4,16]{1,0:T(4,128)} %bitcast.14), custom_call_target="tpu_custom_call" | custom-call | flops 100000000 | bytes 721664 | tf_op jit(solution)/shard_map/pallas_call | solution.py:40
  1.3 5.1 %collective-permute-start.7 = (s16[192,128]{1,0:T(8,128)(2,1)S(1)}, s16[192,128]{1,0:T(8,128)(2,1)S(1)}, u32[]{:S(2)}, u32[]{:S(2)}) collective-permute-start(s16[192,128]{1,0:T(8,128)(2,1)S(1)} %get-tuple-element.59), channel_id=1, source_target_pairs={{0,3},{1,2},{2,1},{3,0},{4,7},{5,6},{6,5},{7,4},{8,11},{9,10},{10,... | collective-permute-start | bytes 147464 | tf_op jit(solution)/shard_map/ppermute | solution.py:479
  7.0 1.6 %collective-permute-done.7.refs_0_ = s16[192,128]{1,0:T(8,128)(2,1)S(1)} collective-permute-done((s16[192,128]{1,0:T(8,128)(2,1)S(1)}, s16[192,128]{1,0:T(8,128)(2,1)S(1)}, u32[]{:S(2)}, u32[]{:S(2)}) %collective-permute-start.7) | collective-permute-done | bytes 49184 | tf_op jit(solution)/shard_map/ppermute | solution.py:479
  8.6 2.8 %collective-permute-done.8.refs_1_ = s16[192,128]{1,0:T(8,128)(2,1)S(1)} collective-permute-done((s16[192,128]{1,0:T(8,128)(2,1)S(1)}, s16[192,128]{1,0:T(8,128)(2,1)S(1)}, u32[]{:S(2)}, u32[]{:S(2)}) %collective-permute-start.8) | collective-permute-done | bytes 49184 | tf_op jit(solution)/shard_map/ppermute | solution.py:479
  11.4 2.5 %collective-permute-start.10 = (s16[448,128]{1,0:T(8,128)(2,1)S(1)}, s16[448,128]{1,0:T(8,128)(2,1)S(1)}, u32[]{:S(2)}, u32[]{:S(2)}) collective-permute-start(s16[448,128]{1,0:T(8,128)(2,1)S(1)} %get-tuple-element.64), channel_id=1, source_target_pairs={{0,24},{1,25},{2,26},{3,27},{4,28},{5,29},{6,30},{7,31},{8,16},{9,... | collective-permute-start | bytes 344072 | tf_op jit(solution)/shard_map/ppermute | solution.py:479
  15.0 3.1 %collective-permute-done.10 = s16[448,128]{1,0:T(8,128)(2,1)S(1)} collective-permute-done((s16[448,128]{1,0:T(8,128)(2,1)S(1)}, s16[448,128]{1,0:T(8,128)(2,1)S(1)}, u32[]{:S(2)}, u32[]{:S(2)}) %collective-permute-start.10) | collective-permute-done | bytes 114720 | tf_op jit(solution)/shard_map/ppermute | solution.py:479
  20.0 1.1 %collective-permute-done.13.refs_5_ = s16[1792,128]{1,0:T(8,128)(2,1)S(1)} collective-permute-done((s16[1792,128]{1,0:T(8,128)(2,1)S(1)}, s16[1792,128]{1,0:T(8,128)(2,1)S(1)}, u32[]{:S(2)}, u32[]{:S(2)}) %collective-permute-start.13) | collective-permute-done | bytes 458784 | tf_op jit(solution)/shard_map/ppermute | solution.py:479
  21.1 1.4 %shard_map.58 = (f32[128,128]{1,0:T(8,128)S(1)}, bf16[128,128]{1,0:T(8,128)(2,1)S(1)}, f32[128,128]{1,0:T(8,128)S(1)}, f32[128,128]{1,0:T(8,128)S(1)}, f32[64,12...) custom-call(bf16[2560,256]{1,0:T(8,128)(2,1)S(1)} %get-tuple-element.67.refs_0_, f32[128,128]{1,0:T(8,128)S(1)} %get-tuple-element.68.refs_1_, ...), custom_call_target="tpu_custom_call" | custom-call | flops 500000000 | bytes 2756608 | tf_op jit(solution)/shard_map/pallas_call | solution.py:40
  23.3 2.0 %collective-permute-start.15 = (s16[144,128]{1,0:T(8,128)(2,1)S(1)}, s16[144,128]{1,0:T(8,128)(2,1)S(1)}, u32[]{:S(2)}, u32[]{:S(2)}) collective-permute-start(s16[144,128]{1,0:T(8,128)(2,1)S(1)} %get-tuple-element.76.refs_0_), channel_id=1, source_target_pairs={{0,2},{1,3},{2,0},{3,1},{4,6},{5,7},{6,4},{7,5},{8,10},{9,11},{10,... | collective-permute-start | bytes 110600 | tf_op jit(solution)/shard_map/ppermute | solution.py:479
  25.3 1.7 %collective-permute-start.16 = (s16[144,128]{1,0:T(8,128)(2,1)S(1)}, s16[144,128]{1,0:T(8,128)(2,1)S(1)}, u32[]{:S(2)}, u32[]{:S(2)}) collective-permute-start(s16[144,128]{1,0:T(8,128)(2,1)S(1)} %get-tuple-element.76.refs_0_), channel_id=1, source_target_pairs={{0,3},{1,2},{2,1},{3,0},{4,7},{5,6},{6,5},{7,4},{8,11},{9,10},{10,... | collective-permute-start | bytes 110600 | tf_op jit(solution)/shard_map/ppermute | solution.py:479
  28.3 2.8 %collective-permute-done.16.refs_3_ = s16[144,128]{1,0:T(8,128)(2,1)S(1)} collective-permute-done((s16[144,128]{1,0:T(8,128)(2,1)S(1)}, s16[144,128]{1,0:T(8,128)(2,1)S(1)}, u32[]{:S(2)}, u32[]{:S(2)}) %collective-permute-start.16) | collective-permute-done | bytes 36896 | tf_op jit(solution)/shard_map/ppermute | solution.py:479
  31.1 1.6 %collective-permute-start.17 = (s16[528,128]{1,0:T(8,128)(2,1)S(1)}, s16[528,128]{1,0:T(8,128)(2,1)S(1)}, u32[]{:S(2)}, u32[]{:S(2)}) collective-permute-start(s16[528,128]{1,0:T(8,128)(2,1)S(1)} %shard_map.59), channel_id=1, source_target_pairs={{0,24},{1,25},{2,26},{3,27},{4,28},{5,29},{6,30},{7,31},{8,16},{9,... | collective-permute-start | bytes 405512 | tf_op jit(solution)/shard_map/ppermute | solution.py:479
  33.6 1.1 %collective-permute-start.19 = (s16[528,128]{1,0:T(8,128)(2,1)S(1)}, s16[528,128]{1,0:T(8,128)(2,1)S(1)}, u32[]{:S(2)}, u32[]{:S(2)}) collective-permute-start(s16[528,128]{1,0:T(8,128)(2,1)S(1)} %shard_map.59), channel_id=1, source_target_pairs={{0,8},{1,9},{2,10},{3,11},{4,12},{5,13},{6,14},{7,15},{8,0},{9,1},... | collective-permute-start | bytes 405512 | tf_op jit(solution)/shard_map/ppermute | solution.py:479
  34.7 2.9 %collective-permute-done.17 = s16[528,128]{1,0:T(8,128)(2,1)S(1)} collective-permute-done((s16[528,128]{1,0:T(8,128)(2,1)S(1)}, s16[528,128]{1,0:T(8,128)(2,1)S(1)}, u32[]{:S(2)}, u32[]{:S(2)}) %collective-permute-start.17) | collective-permute-done | bytes 135200 | tf_op jit(solution)/shard_map/ppermute | solution.py:479
  37.6 1.2 %collective-permute-done.18 = s16[528,128]{1,0:T(8,128)(2,1)S(1)} collective-permute-done((s16[528,128]{1,0:T(8,128)(2,1)S(1)}, s16[528,128]{1,0:T(8,128)(2,1)S(1)}, u32[]{:S(2)}, u32[]{:S(2)}) %collective-permute-start.18) | collective-permute-done | bytes 135200 | tf_op jit(solution)/shard_map/ppermute | solution.py:479
  39.6 1.2 %collective-permute-done.20.rest = f32[128,128]{1,0:T(8,128)S(1)} collective-permute-done((f32[128,128]{1,0:T(8,128)S(1)}, f32[128,128]{1,0:T(8,128)S(1)}, u32[]{:S(2)}, u32[]{:S(2)}) %collective-permute-start.20) | collective-permute-done | bytes 65568 | tf_op jit(solution)/shard_map/ppermute | solution.py:479
  42.2 1.6 %collective-permute-start.22 = (s16[80,128]{1,0:T(8,128)(2,1)S(1)}, s16[80,128]{1,0:T(8,128)(2,1)S(1)}, u32[]{:S(2)}, u32[]{:S(2)}) collective-permute-start(s16[80,128]{1,0:T(8,128)(2,1)S(1)} %get-tuple-element.91), channel_id=1, source_target_pairs={{0,6},{1,7},{2,4},{3,5},{4,2},{5,3},{6,0},{7,1},{8,14},{9,15},{10,... | collective-permute-start | bytes 61448 | tf_op jit(solution)/shard_map/ppermute | solution.py:479
  43.8 1.9 %collective-permute-start.23 = (s16[80,128]{1,0:T(8,128)(2,1)S(1)}, s16[80,128]{1,0:T(8,128)(2,1)S(1)}, u32[]{:S(2)}, u32[]{:S(2)}) collective-permute-start(s16[80,128]{1,0:T(8,128)(2,1)S(1)} %get-tuple-element.92), channel_id=1, source_target_pairs={{0,7},{1,6},{2,5},{3,4},{4,3},{5,2},{6,1},{7,0},{8,15},{9,14},{10,... | collective-permute-start | bytes 61448 | tf_op jit(solution)/shard_map/ppermute | solution.py:479
  45.7 1.3 %shard_map.64 = (f32[1024,128]{1,0:T(8,128)S(1)}, f32[8,128]{1,0:T(8,128)S(1)}) custom-call(s16[2112,128]{1,0:T(8,128)(2,1)S(1)} %constant_dynamic-update-slice_fusion.4.block.refs_0_), custom_call_target="tpu_custom_call" | custom-call | flops 2000000000 | bytes 1069056 | tf_op jit(solution)/shard_map/pallas_call | solution.py:40
  47.1 1.8 %collective-permute-done.23.refs_3_ = s16[80,128]{1,0:T(8,128)(2,1)S(1)} collective-permute-done((s16[80,128]{1,0:T(8,128)(2,1)S(1)}, s16[80,128]{1,0:T(8,128)(2,1)S(1)}, u32[]{:S(2)}, u32[]{:S(2)}) %collective-permute-start.23) | collective-permute-done | bytes 20512 | tf_op jit(solution)/shard_map/ppermute | solution.py:479
  48.8 1.6 %collective-permute-start.25 = (s16[272,128]{1,0:T(8,128)(2,1)S(1)}, s16[272,128]{1,0:T(8,128)(2,1)S(1)}, u32[]{:S(2)}, u32[]{:S(2)}) collective-permute-start(s16[272,128]{1,0:T(8,128)(2,1)S(1)} %shard_map.63), channel_id=1, source_target_pairs={{0,28},{1,29},{2,30},{3,31},{4,24},{5,25},{6,26},{7,27},{8,20},{9,... | collective-permute-start | bytes 208904 | tf_op jit(solution)/shard_map/ppermute | solution.py:479
  52.1 1.3 %shard_map.65 = (f32[64,2048]{1,0:T(8,128)S(1)}, s32[1]{0:T(128)}) custom-call(f32[64,2048]{1,0:T(8,128)S(1)} %copy-done, f32[1024,128]{1,0:T(8,128)S(1)} %get-tuple-element.97.refs_1_, s16[2112,128]{1,0:T(8,128)(2,1)S(1)} %collective-permute-done.24.refs_2_, f32[8,128]{1,0:T(8,128)S(1)} %get-tuple-element.99.refs_3_), custom_call_target="tpu_custom_call" | custom-call | flops 2000000000 | bytes 2117636 | tf_op jit(solution)/shard_map/pallas_call | solution.py:40
  54.1 1.7 %collective-permute-done.26 = s16[272,128]{1,0:T(8,128)(2,1)S(1)} collective-permute-done((s16[272,128]{1,0:T(8,128)(2,1)S(1)}, s16[272,128]{1,0:T(8,128)(2,1)S(1)}, u32[]{:S(2)}, u32[]{:S(2)}) %collective-permute-start.26) | collective-permute-done | bytes 69664 | tf_op jit(solution)/shard_map/ppermute | solution.py:479
  57.4 1.5 %shard_map.67 = f32[64,2048]{1,0:T(8,128)} custom-call(f32[64,2048]{1,0:T(8,128)S(1)} %get-tuple-element.102.refs_0_, f32[1024,128]{1,0:T(8,128)S(1)} %get-tuple-element.106.refs_1_, s16[1088,128]{1,0:T(8,128)(2,1)S(1)} %get-tuple-element.107.refs_2_), custom_call_target="tpu_custom_call" | custom-call | flops 2000000000 | bytes 1851392 | tf_op jit(solution)/shard_map/pallas_call | solution.py:40
  (47 shorter events, 12.0 us)
Async XLA Ops:
  0.0 19.3 %copy-start = (f32[64,2048]{1,0:T(8,128)S(1)}, f32[64,2048]{1,0:T(8,128)}, u32[]{:S(2)}) copy-start(f32[64,2048]{1,0:T(8,128)} %refs_0_.6) | copy-start | bytes 1572868
  0.0 19.3 %copy-start.1 = (bf16[2,1,256,256]{3,2,1,0:T(8,128)(2,1)S(1)}, bf16[2,1,256,256]{3,2,1,0:T(8,128)(2,1)}, u32[]{:S(2)}) copy-start(bf16[2,1,256,256]{3,2,1,0:T(8,128)(2,1)} %param.11) | copy-start | bytes 786436
  1.3 7.3 %collective-permute-start.7 = (s16[192,128]{1,0:T(8,128)(2,1)S(1)}, s16[192,128]{1,0:T(8,128)(2,1)S(1)}, u32[]{:S(2)}, u32[]{:S(2)}) collective-permute-start(s16[192,128]{1,0:T(8,128)(2,1)S(1)} %get-tuple-element.59), channel_id=1, source_target_pairs={{0,3},{1,2},{2,1},{3,0},{4,7},{5,6},{6,5},{7,4},{8,11},{9,10},{10,... | collective-permute-start | bytes 147464 | tf_op jit(solution)/shard_map/ppermute | solution.py:479
  6.4 5.0 %collective-permute-start.8 = (s16[192,128]{1,0:T(8,128)(2,1)S(1)}, s16[192,128]{1,0:T(8,128)(2,1)S(1)}, u32[]{:S(2)}, u32[]{:S(2)}) collective-permute-start(s16[192,128]{1,0:T(8,128)(2,1)S(1)} %get-tuple-element.60), channel_id=1, source_target_pairs={{0,2},{1,3},{2,0},{3,1},{4,6},{5,7},{6,4},{7,5},{8,10},{9,11},{10,... | collective-permute-start | bytes 147464 | tf_op jit(solution)/shard_map/ppermute | solution.py:479
  6.4 5.0 %collective-permute-start.9 = (s16[192,128]{1,0:T(8,128)(2,1)S(1)}, s16[192,128]{1,0:T(8,128)(2,1)S(1)}, u32[]{:S(2)}, u32[]{:S(2)}) collective-permute-start(s16[192,128]{1,0:T(8,128)(2,1)S(1)} %get-tuple-element.61), channel_id=1, source_target_pairs={{0,1},{1,0},{2,3},{3,2},{4,5},{5,4},{6,7},{7,6},{8,9},{9,8},{10,11... | collective-permute-start | bytes 147464 | tf_op jit(solution)/shard_map/ppermute | solution.py:479
  11.4 6.6 %collective-permute-start.10 = (s16[448,128]{1,0:T(8,128)(2,1)S(1)}, s16[448,128]{1,0:T(8,128)(2,1)S(1)}, u32[]{:S(2)}, u32[]{:S(2)}) collective-permute-start(s16[448,128]{1,0:T(8,128)(2,1)S(1)} %get-tuple-element.64), channel_id=1, source_target_pairs={{0,24},{1,25},{2,26},{3,27},{4,28},{5,29},{6,30},{7,31},{8,16},{9,... | collective-permute-start | bytes 344072 | tf_op jit(solution)/shard_map/ppermute | solution.py:479
  13.9 5.1 %collective-permute-start.11 = (s16[448,128]{1,0:T(8,128)(2,1)S(1)}, s16[448,128]{1,0:T(8,128)(2,1)S(1)}, u32[]{:S(2)}, u32[]{:S(2)}) collective-permute-start(s16[448,128]{1,0:T(8,128)(2,1)S(1)} %get-tuple-element.65), channel_id=1, source_target_pairs={{0,16},{1,17},{2,18},{3,19},{4,20},{5,21},{6,22},{7,23},{8,24},{9,... | collective-permute-start | bytes 344072 | tf_op jit(solution)/shard_map/ppermute | solution.py:479
  14.4 4.8 %collective-permute-start.12 = (s16[448,128]{1,0:T(8,128)(2,1)S(1)}, s16[448,128]{1,0:T(8,128)(2,1)S(1)}, u32[]{:S(2)}, u32[]{:S(2)}) collective-permute-start(s16[448,128]{1,0:T(8,128)(2,1)S(1)} %get-tuple-element.66), channel_id=1, source_target_pairs={{0,8},{1,9},{2,10},{3,11},{4,12},{5,13},{6,14},{7,15},{8,0},{9,1},... | collective-permute-start | bytes 344072 | tf_op jit(solution)/shard_map/ppermute | solution.py:479
  19.3 1.9 %collective-permute-start.13 = (s16[1792,128]{1,0:T(8,128)(2,1)S(1)}, s16[1792,128]{1,0:T(8,128)(2,1)S(1)}, u32[]{:S(2)}, u32[]{:S(2)}) collective-permute-start(s16[1792,128]{1,0:T(8,128)(2,1)S(1)} %constant_dynamic-update-slice_fusion.refs_2_), channel_id=1, source_target_pairs={{0,4},{1,5},{2,6},{3,7},{4,0},{5,1},{6,2},{7,3},{8,12},{9,13},{10,... | collective-permute-start | bytes 1376264 | tf_op jit(solution)/shard_map/ppermute | solution.py:479
  22.6 4.8 %collective-permute-start.14 = (s16[144,128]{1,0:T(8,128)(2,1)S(1)}, s16[144,128]{1,0:T(8,128)(2,1)S(1)}, u32[]{:S(2)}, u32[]{:S(2)}) collective-permute-start(s16[144,128]{1,0:T(8,128)(2,1)S(1)} %get-tuple-element.76.refs_0_), channel_id=1, source_target_pairs={{0,1},{1,0},{2,3},{3,2},{4,5},{5,4},{6,7},{7,6},{8,9},{9,8},{10,11... | collective-permute-start | bytes 110600 | tf_op jit(solution)/shard_map/ppermute | solution.py:479
  23.3 5.0 %collective-permute-start.15 = (s16[144,128]{1,0:T(8,128)(2,1)S(1)}, s16[144,128]{1,0:T(8,128)(2,1)S(1)}, u32[]{:S(2)}, u32[]{:S(2)}) collective-permute-start(s16[144,128]{1,0:T(8,128)(2,1)S(1)} %get-tuple-element.76.refs_0_), channel_id=1, source_target_pairs={{0,2},{1,3},{2,0},{3,1},{4,6},{5,7},{6,4},{7,5},{8,10},{9,11},{10,... | collective-permute-start | bytes 110600 | tf_op jit(solution)/shard_map/ppermute | solution.py:479
  25.3 5.8 %collective-permute-start.16 = (s16[144,128]{1,0:T(8,128)(2,1)S(1)}, s16[144,128]{1,0:T(8,128)(2,1)S(1)}, u32[]{:S(2)}, u32[]{:S(2)}) collective-permute-start(s16[144,128]{1,0:T(8,128)(2,1)S(1)} %get-tuple-element.76.refs_0_), channel_id=1, source_target_pairs={{0,3},{1,2},{2,1},{3,0},{4,7},{5,6},{6,5},{7,4},{8,11},{9,10},{10,... | collective-permute-start | bytes 110600 | tf_op jit(solution)/shard_map/ppermute | solution.py:479
  31.1 6.5 %collective-permute-start.17 = (s16[528,128]{1,0:T(8,128)(2,1)S(1)}, s16[528,128]{1,0:T(8,128)(2,1)S(1)}, u32[]{:S(2)}, u32[]{:S(2)}) collective-permute-start(s16[528,128]{1,0:T(8,128)(2,1)S(1)} %shard_map.59), channel_id=1, source_target_pairs={{0,24},{1,25},{2,26},{3,27},{4,28},{5,29},{6,30},{7,31},{8,16},{9,... | collective-permute-start | bytes 405512 | tf_op jit(solution)/shard_map/ppermute | solution.py:479
  32.6 6.2 %collective-permute-start.18 = (s16[528,128]{1,0:T(8,128)(2,1)S(1)}, s16[528,128]{1,0:T(8,128)(2,1)S(1)}, u32[]{:S(2)}, u32[]{:S(2)}) collective-permute-start(s16[528,128]{1,0:T(8,128)(2,1)S(1)} %shard_map.59), channel_id=1, source_target_pairs={{0,16},{1,17},{2,18},{3,19},{4,20},{5,21},{6,22},{7,23},{8,24},{9,... | collective-permute-start | bytes 405512 | tf_op jit(solution)/shard_map/ppermute | solution.py:479
  33.6 5.4 %collective-permute-start.19 = (s16[528,128]{1,0:T(8,128)(2,1)S(1)}, s16[528,128]{1,0:T(8,128)(2,1)S(1)}, u32[]{:S(2)}, u32[]{:S(2)}) collective-permute-start(s16[528,128]{1,0:T(8,128)(2,1)S(1)} %shard_map.59), channel_id=1, source_target_pairs={{0,8},{1,9},{2,10},{3,11},{4,12},{5,13},{6,14},{7,15},{8,0},{9,1},... | collective-permute-start | bytes 405512 | tf_op jit(solution)/shard_map/ppermute | solution.py:479
  39.5 1.3 %collective-permute-start.20 = (f32[128,128]{1,0:T(8,128)S(1)}, f32[128,128]{1,0:T(8,128)S(1)}, u32[]{:S(2)}, u32[]{:S(2)}) collective-permute-start(f32[128,128]{1,0:T(8,128)S(1)} %get-tuple-element.81), channel_id=1, source_target_pairs={{0,4},{1,5},{2,6},{3,7},{4,0},{5,1},{6,2},{7,3},{8,12},{9,13},{10,... | collective-permute-start | bytes 196616 | tf_op jit(solution)/shard_map/ppermute | solution.py:479
  41.5 7.3 %collective-permute-start.24 = (s16[2112,128]{1,0:T(8,128)(2,1)S(1)}, s16[2112,128]{1,0:T(8,128)(2,1)S(1)}, u32[]{:S(2)}, u32[]{:S(2)}) collective-permute-start(s16[2112,128]{1,0:T(8,128)(2,1)S(1)} %constant_dynamic-update-slice_fusion.4.block.refs_0_), channel_id=1, source_target_pairs={{0,4},{1,5},{2,6},{3,7},{4,0},{5,1},{6,2},{7,3},{8,12},{9,13},{10,... | collective-permute-start | bytes 1622024 | tf_op jit(solution)/shard_map/ppermute | solution.py:479
  41.7 5.4 %collective-permute-start.21 = (s16[80,128]{1,0:T(8,128)(2,1)S(1)}, s16[80,128]{1,0:T(8,128)(2,1)S(1)}, u32[]{:S(2)}, u32[]{:S(2)}) collective-permute-start(s16[80,128]{1,0:T(8,128)(2,1)S(1)} %get-tuple-element.90), channel_id=1, source_target_pairs={{0,5},{1,4},{2,7},{3,6},{4,1},{5,0},{6,3},{7,2},{8,13},{9,12},{10,... | collective-permute-start | bytes 61448 | tf_op jit(solution)/shard_map/ppermute | solution.py:479
  42.2 4.9 %collective-permute-start.22 = (s16[80,128]{1,0:T(8,128)(2,1)S(1)}, s16[80,128]{1,0:T(8,128)(2,1)S(1)}, u32[]{:S(2)}, u32[]{:S(2)}) collective-permute-start(s16[80,128]{1,0:T(8,128)(2,1)S(1)} %get-tuple-element.91), channel_id=1, source_target_pairs={{0,6},{1,7},{2,4},{3,5},{4,2},{5,3},{6,0},{7,1},{8,14},{9,15},{10,... | collective-permute-start | bytes 61448 | tf_op jit(solution)/shard_map/ppermute | solution.py:479
  43.8 5.0 %collective-permute-start.23 = (s16[80,128]{1,0:T(8,128)(2,1)S(1)}, s16[80,128]{1,0:T(8,128)(2,1)S(1)}, u32[]{:S(2)}, u32[]{:S(2)}) collective-permute-start(s16[80,128]{1,0:T(8,128)(2,1)S(1)} %get-tuple-element.92), channel_id=1, source_target_pairs={{0,7},{1,6},{2,5},{3,4},{4,3},{5,2},{6,1},{7,0},{8,15},{9,14},{10,... | collective-permute-start | bytes 61448 | tf_op jit(solution)/shard_map/ppermute | solution.py:479
  48.8 5.2 %collective-permute-start.25 = (s16[272,128]{1,0:T(8,128)(2,1)S(1)}, s16[272,128]{1,0:T(8,128)(2,1)S(1)}, u32[]{:S(2)}, u32[]{:S(2)}) collective-permute-start(s16[272,128]{1,0:T(8,128)(2,1)S(1)} %shard_map.63), channel_id=1, source_target_pairs={{0,28},{1,29},{2,30},{3,31},{4,24},{5,25},{6,26},{7,27},{8,20},{9,... | collective-permute-start | bytes 208904 | tf_op jit(solution)/shard_map/ppermute | solution.py:479
  50.4 5.3 %collective-permute-start.26 = (s16[272,128]{1,0:T(8,128)(2,1)S(1)}, s16[272,128]{1,0:T(8,128)(2,1)S(1)}, u32[]{:S(2)}, u32[]{:S(2)}) collective-permute-start(s16[272,128]{1,0:T(8,128)(2,1)S(1)} %shard_map.63), channel_id=1, source_target_pairs={{0,20},{1,21},{2,22},{3,23},{4,16},{5,17},{6,18},{7,19},{8,28},{9,... | collective-permute-start | bytes 208904 | tf_op jit(solution)/shard_map/ppermute | solution.py:479
  51.1 4.6 %collective-permute-start.27 = (s16[272,128]{1,0:T(8,128)(2,1)S(1)}, s16[272,128]{1,0:T(8,128)(2,1)S(1)}, u32[]{:S(2)}, u32[]{:S(2)}) collective-permute-start(s16[272,128]{1,0:T(8,128)(2,1)S(1)} %shard_map.63), channel_id=1, source_target_pairs={{0,12},{1,13},{2,14},{3,15},{4,8},{5,9},{6,10},{7,11},{8,4},{9,5},... | collective-permute-start | bytes 208904 | tf_op jit(solution)/shard_map/ppermute | solution.py:479
  55.8 1.6 %collective-permute-start.28 = (s16[1088,128]{1,0:T(8,128)(2,1)S(1)}, s16[1088,128]{1,0:T(8,128)(2,1)S(1)}, u32[]{:S(2)}, u32[]{:S(2)}) collective-permute-start(s16[1088,128]{1,0:T(8,128)(2,1)S(1)} %pad_add_fusion.1.refs_0_), channel_id=1, source_target_pairs={{0,4},{1,5},{2,6},{3,7},{4,0},{5,1},{6,2},{7,3},{8,12},{9,13},{10,... | collective-permute-start | bytes 835592 | tf_op jit(solution)/shard_map/ppermute | solution.py:479

commit v9 on v8

--- a/solution.py
+++ b/solution.py
@@ -458,7 +458,7 @@
     else:
         (out,) = refs
     per_band = width // STRIP * TILE
-    chunk = min(256, count)
+    chunk = min(1024, count)
     for at in range(0, count, chunk):
         strips = iota((chunk, STRIP), 0) + (place[1] * count + at)
         gradient = part[at : at + chunk] + summed(decoded, strips)

time: 59.1 us -> 59.1 us (level)
  no operation moved by 1% of the time
where the time goes in v9:
time: 59.1 us; the launch traced here: 58.9 us
  starting transfers between devices  25.2 us (43%)
  waiting for transfers between devices  23 us (39%)
  Pallas kernels  9.82 us (17%)
  between operations  0.83 us (1%)
    ppermute x22, starting transfers between devices, swap(): return lax.ppermute(x, ('chan', 'facet'), pairs)  25.2 us
    ppermute x22, waiting for transfers between devices, swap(): return lax.ppermute(x, ('chan', 'facet'), pairs)  23 us
    pallas_call x13, Pallas kernels, call(): pl.pallas_call(body, out_shape=list(outs), in_specs=spaces, out_specs=[pl...  9.82 us
  transfers between devices with their start and end apart: 22, of which 15 were waited for; matrix products, arithmetic and copies ran while one was open for 0% of the time, Pallas kernels for 7%

profile of v9, /device:TPU:0, one launch (start us, length us, event | category | flops | bytes accessed | tf_op | source)
XLA Modules:
  0.0 58.9 jit_solution(47206904852264321)
XLA Ops:
  0.0 1.2 %shard_map.55 = (s16[64,128]{1,0:T(8,128)(2,1)S(1)}, s16[192,128]{1,0:T(8,128)(2,1)S(1)}, s16[192,128]{1,0:T(8,128)(2,1)S(1)}, s16[192,128]{1,0:T(8,128)(2,1)S(1)}) custom-call(f32[64,2048]{1,0:T(8,128)} %refs_0_.6, bf16[16,4,256]{2,1,0:T(4,128)(2,1)} %bitcast.12, s32[4,2,16]{2,1,0:T(2,128)} %bitcast.13, s32[4,16]{1,0:T(4,128)} %bitcast.14), custom_call_target="tpu_custom_call" | custom-call | flops 100000000 | bytes 721664 | tf_op jit(solution)/shard_map/pallas_call | solution.py:40
  1.3 5.1 %collective-permute-start.7 = (s16[192,128]{1,0:T(8,128)(2,1)S(1)}, s16[192,128]{1,0:T(8,128)(2,1)S(1)}, u32[]{:S(2)}, u32[]{:S(2)}) collective-permute-start(s16[192,128]{1,0:T(8,128)(2,1)S(1)} %get-tuple-element.59), channel_id=1, source_target_pairs={{0,3},{1,2},{2,1},{3,0},{4,7},{5,6},{6,5},{7,4},{8,11},{9,10},{10,... | collective-permute-start | bytes 147464 | tf_op jit(solution)/shard_map/ppermute | solution.py:479
  7.0 1.6 %collective-permute-done.7.refs_0_ = s16[192,128]{1,0:T(8,128)(2,1)S(1)} collective-permute-done((s16[192,128]{1,0:T(8,128)(2,1)S(1)}, s16[192,128]{1,0:T(8,128)(2,1)S(1)}, u32[]{:S(2)}, u32[]{:S(2)}) %collective-permute-start.7) | collective-permute-done | bytes 49184 | tf_op jit(solution)/shard_map/ppermute | solution.py:479
  8.6 2.8 %collective-permute-done.8.refs_1_ = s16[192,128]{1,0:T(8,128)(2,1)S(1)} collective-permute-done((s16[192,128]{1,0:T(8,128)(2,1)S(1)}, s16[192,128]{1,0:T(8,128)(2,1)S(1)}, u32[]{:S(2)}, u32[]{:S(2)}) %collective-permute-start.8) | collective-permute-done | bytes 49184 | tf_op jit(solution)/shard_map/ppermute | solution.py:479
  11.4 2.5 %collective-permute-start.10 = (s16[448,128]{1,0:T(8,128)(2,1)S(1)}, s16[448,128]{1,0:T(8,128)(2,1)S(1)}, u32[]{:S(2)}, u32[]{:S(2)}) collective-permute-start(s16[448,128]{1,0:T(8,128)(2,1)S(1)} %get-tuple-element.64), channel_id=1, source_target_pairs={{0,24},{1,25},{2,26},{3,27},{4,28},{5,29},{6,30},{7,31},{8,16},{9,... | collective-permute-start | bytes 344072 | tf_op jit(solution)/shard_map/ppermute | solution.py:479
  15.0 3.1 %collective-permute-done.10 = s16[448,128]{1,0:T(8,128)(2,1)S(1)} collective-permute-done((s16[448,128]{1,0:T(8,128)(2,1)S(1)}, s16[448,128]{1,0:T(8,128)(2,1)S(1)}, u32[]{:S(2)}, u32[]{:S(2)}) %collective-permute-start.10) | collective-permute-done | bytes 114720 | tf_op jit(solution)/shard_map/ppermute | solution.py:479
  20.0 1.1 %collective-permute-done.13.refs_5_ = s16[1792,128]{1,0:T(8,128)(2,1)S(1)} collective-permute-done((s16[1792,128]{1,0:T(8,128)(2,1)S(1)}, s16[1792,128]{1,0:T(8,128)(2,1)S(1)}, u32[]{:S(2)}, u32[]{:S(2)}) %collective-permute-start.13) | collective-permute-done | bytes 458784 | tf_op jit(solution)/shard_map/ppermute | solution.py:479
  21.1 1.4 %shard_map.58 = (f32[128,128]{1,0:T(8,128)S(1)}, bf16[128,128]{1,0:T(8,128)(2,1)S(1)}, f32[128,128]{1,0:T(8,128)S(1)}, f32[128,128]{1,0:T(8,128)S(1)}, f32[64,12...) custom-call(bf16[2560,256]{1,0:T(8,128)(2,1)S(1)} %get-tuple-element.67.refs_0_, f32[128,128]{1,0:T(8,128)S(1)} %get-tuple-element.68.refs_1_, ...), custom_call_target="tpu_custom_call" | custom-call | flops 500000000 | bytes 2756608 | tf_op jit(solution)/shard_map/pallas_call | solution.py:40
  23.3 2.0 %collective-permute-start.15 = (s16[144,128]{1,0:T(8,128)(2,1)S(1)}, s16[144,128]{1,0:T(8,128)(2,1)S(1)}, u32[]{:S(2)}, u32[]{:S(2)}) collective-permute-start(s16[144,128]{1,0:T(8,128)(2,1)S(1)} %get-tuple-element.76.refs_0_), channel_id=1, source_target_pairs={{0,2},{1,3},{2,0},{3,1},{4,6},{5,7},{6,4},{7,5},{8,10},{9,11},{10,... | collective-permute-start | bytes 110600 | tf_op jit(solution)/shard_map/ppermute | solution.py:479
  25.3 1.7 %collective-permute-start.16 = (s16[144,128]{1,0:T(8,128)(2,1)S(1)}, s16[144,128]{1,0:T(8,128)(2,1)S(1)}, u32[]{:S(2)}, u32[]{:S(2)}) collective-permute-start(s16[144,128]{1,0:T(8,128)(2,1)S(1)} %get-tuple-element.76.refs_0_), channel_id=1, source_target_pairs={{0,3},{1,2},{2,1},{3,0},{4,7},{5,6},{6,5},{7,4},{8,11},{9,10},{10,... | collective-permute-start | bytes 110600 | tf_op jit(solution)/shard_map/ppermute | solution.py:479
  28.3 2.8 %collective-permute-done.16.refs_3_ = s16[144,128]{1,0:T(8,128)(2,1)S(1)} collective-permute-done((s16[144,128]{1,0:T(8,128)(2,1)S(1)}, s16[144,128]{1,0:T(8,128)(2,1)S(1)}, u32[]{:S(2)}, u32[]{:S(2)}) %collective-permute-start.16) | collective-permute-done | bytes 36896 | tf_op jit(solution)/shard_map/ppermute | solution.py:479
  31.1 1.6 %collective-permute-start.17 = (s16[528,128]{1,0:T(8,128)(2,1)S(1)}, s16[528,128]{1,0:T(8,128)(2,1)S(1)}, u32[]{:S(2)}, u32[]{:S(2)}) collective-permute-start(s16[528,128]{1,0:T(8,128)(2,1)S(1)} %shard_map.59), channel_id=1, source_target_pairs={{0,24},{1,25},{2,26},{3,27},{4,28},{5,29},{6,30},{7,31},{8,16},{9,... | collective-permute-start | bytes 405512 | tf_op jit(solution)/shard_map/ppermute | solution.py:479
  33.6 1.1 %collective-permute-start.19 = (s16[528,128]{1,0:T(8,128)(2,1)S(1)}, s16[528,128]{1,0:T(8,128)(2,1)S(1)}, u32[]{:S(2)}, u32[]{:S(2)}) collective-permute-start(s16[528,128]{1,0:T(8,128)(2,1)S(1)} %shard_map.59), channel_id=1, source_target_pairs={{0,8},{1,9},{2,10},{3,11},{4,12},{5,13},{6,14},{7,15},{8,0},{9,1},... | collective-permute-start | bytes 405512 | tf_op jit(solution)/shard_map/ppermute | solution.py:479
  34.7 2.9 %collective-permute-done.17 = s16[528,128]{1,0:T(8,128)(2,1)S(1)} collective-permute-done((s16[528,128]{1,0:T(8,128)(2,1)S(1)}, s16[528,128]{1,0:T(8,128)(2,1)S(1)}, u32[]{:S(2)}, u32[]{:S(2)}) %collective-permute-start.17) | collective-permute-done | bytes 135200 | tf_op jit(solution)/shard_map/ppermute | solution.py:479
  37.6 1.2 %collective-permute-done.18 = s16[528,128]{1,0:T(8,128)(2,1)S(1)} collective-permute-done((s16[528,128]{1,0:T(8,128)(2,1)S(1)}, s16[528,128]{1,0:T(8,128)(2,1)S(1)}, u32[]{:S(2)}, u32[]{:S(2)}) %collective-permute-start.18) | collective-permute-done | bytes 135200 | tf_op jit(solution)/shard_map/ppermute | solution.py:479
  39.6 1.2 %collective-permute-done.20.rest = f32[128,128]{1,0:T(8,128)S(1)} collective-permute-done((f32[128,128]{1,0:T(8,128)S(1)}, f32[128,128]{1,0:T(8,128)S(1)}, u32[]{:S(2)}, u32[]{:S(2)}) %collective-permute-start.20) | collective-permute-done | bytes 65568 | tf_op jit(solution)/shard_map/ppermute | solution.py:479
  42.2 1.6 %collective-permute-start.22 = (s16[80,128]{1,0:T(8,128)(2,1)S(1)}, s16[80,128]{1,0:T(8,128)(2,1)S(1)}, u32[]{:S(2)}, u32[]{:S(2)}) collective-permute-start(s16[80,128]{1,0:T(8,128)(2,1)S(1)} %get-tuple-element.91), channel_id=1, source_target_pairs={{0,6},{1,7},{2,4},{3,5},{4,2},{5,3},{6,0},{7,1},{8,14},{9,15},{10,... | collective-permute-start | bytes 61448 | tf_op jit(solution)/shard_map/ppermute | solution.py:479
  43.8 1.9 %collective-permute-start.23 = (s16[80,128]{1,0:T(8,128)(2,1)S(1)}, s16[80,128]{1,0:T(8,128)(2,1)S(1)}, u32[]{:S(2)}, u32[]{:S(2)}) collective-permute-start(s16[80,128]{1,0:T(8,128)(2,1)S(1)} %get-tuple-element.92), channel_id=1, source_target_pairs={{0,7},{1,6},{2,5},{3,4},{4,3},{5,2},{6,1},{7,0},{8,15},{9,14},{10,... | collective-permute-start | bytes 61448 | tf_op jit(solution)/shard_map/ppermute | solution.py:479
  45.7 1.3 %shard_map.64 = (f32[1024,128]{1,0:T(8,128)S(1)}, f32[8,128]{1,0:T(8,128)S(1)}) custom-call(s16[2112,128]{1,0:T(8,128)(2,1)S(1)} %constant_dynamic-update-slice_fusion.4.block.refs_0_), custom_call_target="tpu_custom_call" | custom-call | flops 2000000000 | bytes 1069056 | tf_op jit(solution)/shard_map/pallas_call | solution.py:40
  47.1 1.8 %collective-permute-done.23.refs_3_ = s16[80,128]{1,0:T(8,128)(2,1)S(1)} collective-permute-done((s16[80,128]{1,0:T(8,128)(2,1)S(1)}, s16[80,128]{1,0:T(8,128)(2,1)S(1)}, u32[]{:S(2)}, u32[]{:S(2)}) %collective-permute-start.23) | collective-permute-done | bytes 20512 | tf_op jit(solution)/shard_map/ppermute | solution.py:479
  48.8 1.6 %collective-permute-start.25 = (s16[272,128]{1,0:T(8,128)(2,1)S(1)}, s16[272,128]{1,0:T(8,128)(2,1)S(1)}, u32[]{:S(2)}, u32[]{:S(2)}) collective-permute-start(s16[272,128]{1,0:T(8,128)(2,1)S(1)} %shard_map.63), channel_id=1, source_target_pairs={{0,28},{1,29},{2,30},{3,31},{4,24},{5,25},{6,26},{7,27},{8,20},{9,... | collective-permute-start | bytes 208904 | tf_op jit(solution)/shard_map/ppermute | solution.py:479
  52.1 1.3 %shard_map.65 = (f32[64,2048]{1,0:T(8,128)S(1)}, s32[1]{0:T(128)}) custom-call(f32[64,2048]{1,0:T(8,128)S(1)} %copy-done, f32[1024,128]{1,0:T(8,128)S(1)} %get-tuple-element.97.refs_1_, s16[2112,128]{1,0:T(8,128)(2,1)S(1)} %collective-permute-done.24.refs_2_, f32[8,128]{1,0:T(8,128)S(1)} %get-tuple-element.99.refs_3_), custom_call_target="tpu_custom_call" | custom-call | flops 2000000000 | bytes 2117636 | tf_op jit(solution)/shard_map/pallas_call | solution.py:40
  54.1 1.7 %collective-permute-done.26 = s16[272,128]{1,0:T(8,128)(2,1)S(1)} collective-permute-done((s16[272,128]{1,0:T(8,128)(2,1)S(1)}, s16[272,128]{1,0:T(8,128)(2,1)S(1)}, u32[]{:S(2)}, u32[]{:S(2)}) %collective-permute-start.26) | collective-permute-done | bytes 69664 | tf_op jit(solution)/shard_map/ppermute | solution.py:479
  57.4 1.5 %shard_map.67 = f32[64,2048]{1,0:T(8,128)} custom-call(f32[64,2048]{1,0:T(8,128)S(1)} %get-tuple-element.102.refs_0_, f32[1024,128]{1,0:T(8,128)S(1)} %get-tuple-element.106.refs_1_, s16[1088,128]{1,0:T(8,128)(2,1)S(1)} %get-tuple-element.107.refs_2_), custom_call_target="tpu_custom_call" | custom-call | flops 2000000000 | bytes 1851392 | tf_op jit(solution)/shard_map/pallas_call | solution.py:40
  (47 shorter events, 12.0 us)
Async XLA Ops:
  0.0 19.3 %copy-start = (f32[64,2048]{1,0:T(8,128)S(1)}, f32[64,2048]{1,0:T(8,128)}, u32[]{:S(2)}) copy-start(f32[64,2048]{1,0:T(8,128)} %refs_0_.6) | copy-start | bytes 1572868
  0.0 19.3 %copy-start.1 = (bf16[2,1,256,256]{3,2,1,0:T(8,128)(2,1)S(1)}, bf16[2,1,256,256]{3,2,1,0:T(8,128)(2,1)}, u32[]{:S(2)}) copy-start(bf16[2,1,256,256]{3,2,1,0:T(8,128)(2,1)} %param.11) | copy-start | bytes 786436
  1.3 7.3 %collective-permute-start.7 = (s16[192,128]{1,0:T(8,128)(2,1)S(1)}, s16[192,128]{1,0:T(8,128)(2,1)S(1)}, u32[]{:S(2)}, u32[]{:S(2)}) collective-permute-start(s16[192,128]{1,0:T(8,128)(2,1)S(1)} %get-tuple-element.59), channel_id=1, source_target_pairs={{0,3},{1,2},{2,1},{3,0},{4,7},{5,6},{6,5},{7,4},{8,11},{9,10},{10,... | collective-permute-start | bytes 147464 | tf_op jit(solution)/shard_map/ppermute | solution.py:479
  6.4 5.0 %collective-permute-start.8 = (s16[192,128]{1,0:T(8,128)(2,1)S(1)}, s16[192,128]{1,0:T(8,128)(2,1)S(1)}, u32[]{:S(2)}, u32[]{:S(2)}) collective-permute-start(s16[192,128]{1,0:T(8,128)(2,1)S(1)} %get-tuple-element.60), channel_id=1, source_target_pairs={{0,2},{1,3},{2,0},{3,1},{4,6},{5,7},{6,4},{7,5},{8,10},{9,11},{10,... | collective-permute-start | bytes 147464 | tf_op jit(solution)/shard_map/ppermute | solution.py:479
  6.4 5.0 %collective-permute-start.9 = (s16[192,128]{1,0:T(8,128)(2,1)S(1)}, s16[192,128]{1,0:T(8,128)(2,1)S(1)}, u32[]{:S(2)}, u32[]{:S(2)}) collective-permute-start(s16[192,128]{1,0:T(8,128)(2,1)S(1)} %get-tuple-element.61), channel_id=1, source_target_pairs={{0,1},{1,0},{2,3},{3,2},{4,5},{5,4},{6,7},{7,6},{8,9},{9,8},{10,11... | collective-permute-start | bytes 147464 | tf_op jit(solution)/shard_map/ppermute | solution.py:479
  11.4 6.6 %collective-permute-start.10 = (s16[448,128]{1,0:T(8,128)(2,1)S(1)}, s16[448,128]{1,0:T(8,128)(2,1)S(1)}, u32[]{:S(2)}, u32[]{:S(2)}) collective-permute-start(s16[448,128]{1,0:T(8,128)(2,1)S(1)} %get-tuple-element.64), channel_id=1, source_target_pairs={{0,24},{1,25},{2,26},{3,27},{4,28},{5,29},{6,30},{7,31},{8,16},{9,... | collective-permute-start | bytes 344072 | tf_op jit(solution)/shard_map/ppermute | solution.py:479
  13.9 5.1 %collective-permute-start.11 = (s16[448,128]{1,0:T(8,128)(2,1)S(1)}, s16[448,128]{1,0:T(8,128)(2,1)S(1)}, u32[]{:S(2)}, u32[]{:S(2)}) collective-permute-start(s16[448,128]{1,0:T(8,128)(2,1)S(1)} %get-tuple-element.65), channel_id=1, source_target_pairs={{0,16},{1,17},{2,18},{3,19},{4,20},{5,21},{6,22},{7,23},{8,24},{9,... | collective-permute-start | bytes 344072 | tf_op jit(solution)/shard_map/ppermute | solution.py:479
  14.4 4.8 %collective-permute-start.12 = (s16[448,128]{1,0:T(8,128)(2,1)S(1)}, s16[448,128]{1,0:T(8,128)(2,1)S(1)}, u32[]{:S(2)}, u32[]{:S(2)}) collective-permute-start(s16[448,128]{1,0:T(8,128)(2,1)S(1)} %get-tuple-element.66), channel_id=1, source_target_pairs={{0,8},{1,9},{2,10},{3,11},{4,12},{5,13},{6,14},{7,15},{8,0},{9,1},... | collective-permute-start | bytes 344072 | tf_op jit(solution)/shard_map/ppermute | solution.py:479
  19.3 1.9 %collective-permute-start.13 = (s16[1792,128]{1,0:T(8,128)(2,1)S(1)}, s16[1792,128]{1,0:T(8,128)(2,1)S(1)}, u32[]{:S(2)}, u32[]{:S(2)}) collective-permute-start(s16[1792,128]{1,0:T(8,128)(2,1)S(1)} %constant_dynamic-update-slice_fusion.refs_2_), channel_id=1, source_target_pairs={{0,4},{1,5},{2,6},{3,7},{4,0},{5,1},{6,2},{7,3},{8,12},{9,13},{10,... | collective-permute-start | bytes 1376264 | tf_op jit(solution)/shard_map/ppermute | solution.py:479
  22.6 4.8 %collective-permute-start.14 = (s16[144,128]{1,0:T(8,128)(2,1)S(1)}, s16[144,128]{1,0:T(8,128)(2,1)S(1)}, u32[]{:S(2)}, u32[]{:S(2)}) collective-permute-start(s16[144,128]{1,0:T(8,128)(2,1)S(1)} %get-tuple-element.76.refs_0_), channel_id=1, source_target_pairs={{0,1},{1,0},{2,3},{3,2},{4,5},{5,4},{6,7},{7,6},{8,9},{9,8},{10,11... | collective-permute-start | bytes 110600 | tf_op jit(solution)/shard_map/ppermute | solution.py:479
  23.3 5.0 %collective-permute-start.15 = (s16[144,128]{1,0:T(8,128)(2,1)S(1)}, s16[144,128]{1,0:T(8,128)(2,1)S(1)}, u32[]{:S(2)}, u32[]{:S(2)}) collective-permute-start(s16[144,128]{1,0:T(8,128)(2,1)S(1)} %get-tuple-element.76.refs_0_), channel_id=1, source_target_pairs={{0,2},{1,3},{2,0},{3,1},{4,6},{5,7},{6,4},{7,5},{8,10},{9,11},{10,... | collective-permute-start | bytes 110600 | tf_op jit(solution)/shard_map/ppermute | solution.py:479
  25.3 5.8 %collective-permute-start.16 = (s16[144,128]{1,0:T(8,128)(2,1)S(1)}, s16[144,128]{1,0:T(8,128)(2,1)S(1)}, u32[]{:S(2)}, u32[]{:S(2)}) collective-permute-start(s16[144,128]{1,0:T(8,128)(2,1)S(1)} %get-tuple-element.76.refs_0_), channel_id=1, source_target_pairs={{0,3},{1,2},{2,1},{3,0},{4,7},{5,6},{6,5},{7,4},{8,11},{9,10},{10,... | collective-permute-start | bytes 110600 | tf_op jit(solution)/shard_map/ppermute | solution.py:479
  31.1 6.5 %collective-permute-start.17 = (s16[528,128]{1,0:T(8,128)(2,1)S(1)}, s16[528,128]{1,0:T(8,128)(2,1)S(1)}, u32[]{:S(2)}, u32[]{:S(2)}) collective-permute-start(s16[528,128]{1,0:T(8,128)(2,1)S(1)} %shard_map.59), channel_id=1, source_target_pairs={{0,24},{1,25},{2,26},{3,27},{4,28},{5,29},{6,30},{7,31},{8,16},{9,... | collective-permute-start | bytes 405512 | tf_op jit(solution)/shard_map/ppermute | solution.py:479
  32.6 6.2 %collective-permute-start.18 = (s16[528,128]{1,0:T(8,128)(2,1)S(1)}, s16[528,128]{1,0:T(8,128)(2,1)S(1)}, u32[]{:S(2)}, u32[]{:S(2)}) collective-permute-start(s16[528,128]{1,0:T(8,128)(2,1)S(1)} %shard_map.59), channel_id=1, source_target_pairs={{0,16},{1,17},{2,18},{3,19},{4,20},{5,21},{6,22},{7,23},{8,24},{9,... | collective-permute-start | bytes 405512 | tf_op jit(solution)/shard_map/ppermute | solution.py:479
  33.6 5.4 %collective-permute-start.19 = (s16[528,128]{1,0:T(8,128)(2,1)S(1)}, s16[528,128]{1,0:T(8,128)(2,1)S(1)}, u32[]{:S(2)}, u32[]{:S(2)}) collective-permute-start(s16[528,128]{1,0:T(8,128)(2,1)S(1)} %shard_map.59), channel_id=1, source_target_pairs={{0,8},{1,9},{2,10},{3,11},{4,12},{5,13},{6,14},{7,15},{8,0},{9,1},... | collective-permute-start | bytes 405512 | tf_op jit(solution)/shard_map/ppermute | solution.py:479
  39.5 1.3 %collective-permute-start.20 = (f32[128,128]{1,0:T(8,128)S(1)}, f32[128,128]{1,0:T(8,128)S(1)}, u32[]{:S(2)}, u32[]{:S(2)}) collective-permute-start(f32[128,128]{1,0:T(8,128)S(1)} %get-tuple-element.81), channel_id=1, source_target_pairs={{0,4},{1,5},{2,6},{3,7},{4,0},{5,1},{6,2},{7,3},{8,12},{9,13},{10,... | collective-permute-start | bytes 196616 | tf_op jit(solution)/shard_map/ppermute | solution.py:479
  41.5 7.3 %collective-permute-start.24 = (s16[2112,128]{1,0:T(8,128)(2,1)S(1)}, s16[2112,128]{1,0:T(8,128)(2,1)S(1)}, u32[]{:S(2)}, u32[]{:S(2)}) collective-permute-start(s16[2112,128]{1,0:T(8,128)(2,1)S(1)} %constant_dynamic-update-slice_fusion.4.block.refs_0_), channel_id=1, source_target_pairs={{0,4},{1,5},{2,6},{3,7},{4,0},{5,1},{6,2},{7,3},{8,12},{9,13},{10,... | collective-permute-start | bytes 1622024 | tf_op jit(solution)/shard_map/ppermute | solution.py:479
  41.7 5.4 %collective-permute-start.21 = (s16[80,128]{1,0:T(8,128)(2,1)S(1)}, s16[80,128]{1,0:T(8,128)(2,1)S(1)}, u32[]{:S(2)}, u32[]{:S(2)}) collective-permute-start(s16[80,128]{1,0:T(8,128)(2,1)S(1)} %get-tuple-element.90), channel_id=1, source_target_pairs={{0,5},{1,4},{2,7},{3,6},{4,1},{5,0},{6,3},{7,2},{8,13},{9,12},{10,... | collective-permute-start | bytes 61448 | tf_op jit(solution)/shard_map/ppermute | solution.py:479
  42.2 4.9 %collective-permute-start.22 = (s16[80,128]{1,0:T(8,128)(2,1)S(1)}, s16[80,128]{1,0:T(8,128)(2,1)S(1)}, u32[]{:S(2)}, u32[]{:S(2)}) collective-permute-start(s16[80,128]{1,0:T(8,128)(2,1)S(1)} %get-tuple-element.91), channel_id=1, source_target_pairs={{0,6},{1,7},{2,4},{3,5},{4,2},{5,3},{6,0},{7,1},{8,14},{9,15},{10,... | collective-permute-start | bytes 61448 | tf_op jit(solution)/shard_map/ppermute | solution.py:479
  43.8 5.0 %collective-permute-start.23 = (s16[80,128]{1,0:T(8,128)(2,1)S(1)}, s16[80,128]{1,0:T(8,128)(2,1)S(1)}, u32[]{:S(2)}, u32[]{:S(2)}) collective-permute-start(s16[80,128]{1,0:T(8,128)(2,1)S(1)} %get-tuple-element.92), channel_id=1, source_target_pairs={{0,7},{1,6},{2,5},{3,4},{4,3},{5,2},{6,1},{7,0},{8,15},{9,14},{10,... | collective-permute-start | bytes 61448 | tf_op jit(solution)/shard_map/ppermute | solution.py:479
  48.8 5.2 %collective-permute-start.25 = (s16[272,128]{1,0:T(8,128)(2,1)S(1)}, s16[272,128]{1,0:T(8,128)(2,1)S(1)}, u32[]{:S(2)}, u32[]{:S(2)}) collective-permute-start(s16[272,128]{1,0:T(8,128)(2,1)S(1)} %shard_map.63), channel_id=1, source_target_pairs={{0,28},{1,29},{2,30},{3,31},{4,24},{5,25},{6,26},{7,27},{8,20},{9,... | collective-permute-start | bytes 208904 | tf_op jit(solution)/shard_map/ppermute | solution.py:479
  50.4 5.3 %collective-permute-start.26 = (s16[272,128]{1,0:T(8,128)(2,1)S(1)}, s16[272,128]{1,0:T(8,128)(2,1)S(1)}, u32[]{:S(2)}, u32[]{:S(2)}) collective-permute-start(s16[272,128]{1,0:T(8,128)(2,1)S(1)} %shard_map.63), channel_id=1, source_target_pairs={{0,20},{1,21},{2,22},{3,23},{4,16},{5,17},{6,18},{7,19},{8,28},{9,... | collective-permute-start | bytes 208904 | tf_op jit(solution)/shard_map/ppermute | solution.py:479
  51.1 4.6 %collective-permute-start.27 = (s16[272,128]{1,0:T(8,128)(2,1)S(1)}, s16[272,128]{1,0:T(8,128)(2,1)S(1)}, u32[]{:S(2)}, u32[]{:S(2)}) collective-permute-start(s16[272,128]{1,0:T(8,128)(2,1)S(1)} %shard_map.63), channel_id=1, source_target_pairs={{0,12},{1,13},{2,14},{3,15},{4,8},{5,9},{6,10},{7,11},{8,4},{9,5},... | collective-permute-start | bytes 208904 | tf_op jit(solution)/shard_map/ppermute | solution.py:479
  55.8 1.6 %collective-permute-start.28 = (s16[1088,128]{1,0:T(8,128)(2,1)S(1)}, s16[1088,128]{1,0:T(8,128)(2,1)S(1)}, u32[]{:S(2)}, u32[]{:S(2)}) collective-permute-start(s16[1088,128]{1,0:T(8,128)(2,1)S(1)} %pad_add_fusion.1.refs_0_), channel_id=1, source_target_pairs={{0,4},{1,5},{2,6},{3,7},{4,0},{5,1},{6,2},{7,3},{8,12},{9,13},{10,... | collective-permute-start | bytes 835592 | tf_op jit(solution)/shard_map/ppermute | solution.py:479
